TPU v7x, 128 devices: a whole 4x4x4 slice. The times are simulated.
128 devices in a mesh: dp: 8 (over x_hi, z), row: 4 (over y), col: 4 (over x_lo, core).
Axes of the slice: x: 4 (x_hi: 2, x_lo: 2; x = x_hi * 2 + x_lo), y: 4, z: 4, core: 2. Of those that a mesh axis runs over, the one named last changes fastest.
Arguments:
- inputs: bfloat16 [8192, 2048], P(('dp', 'row'), 'col'), may hold values from -6 to 6
- attention_gain: bfloat16 [2048], P('col'), may hold values from 0.5 to 1.5
- query_weight: bfloat16 [2048, 3072], P('col', 'row'), may hold values from -0.125 to 0.125
- latent_weight: bfloat16 [2048, 576], P('col'), may hold values from -0.125 to 0.125
- latent_gain: bfloat16 [512], replicated, may hold values from 0.5 to 1.5
- expand_weight: bfloat16 [512, 4096], P(None, ('row', 'col')), may hold values from -0.25 to 0.25
- output_weight: bfloat16 [2048, 2048], P('row', 'col'), may hold values from -0.5 to 0.5
- feedforward_gain: bfloat16 [2048], P('col'), may hold values from 0.5 to 1.5
- router_weight: bfloat16 [2048, 8], P('col'), may hold values from -0.25 to 0.25
- shared_gate: bfloat16 [2048, 2816], P('col', 'row'), may hold values from -0.125 to 0.125
- shared_up: bfloat16 [2048, 2816], P('col', 'row'), may hold values from -0.125 to 0.125
- shared_down: bfloat16 [2816, 2048], P('row', 'col'), may hold values from -0.109375 to 0.109375
- expert_gate: bfloat16 [8, 2048, 1408], P(None, 'col', 'row'), may hold values from -0.125 to 0.125
- expert_up: bfloat16 [8, 2048, 1408], P(None, 'col', 'row'), may hold values from -0.125 to 0.125
- expert_down: bfloat16 [8, 1408, 2048], P(None, 'row', 'col'), may hold values from -0.625 to 0.625
- routes: int32 [8192, 6], P('dp'), may hold values from 0 to 7, all different within a row; in each aligned block of 1024 rows (0 to 1023, 1024 to 2047, ...) at most 832 rows name the same one
- prefix: int32 [8], P('dp'), may hold values from 102 to 512
- cotangent: bfloat16 [8192, 2048], P(('dp', 'row'), 'col'), may hold values from -6 to 6
Outputs:
- output: bfloat16 [8192, 2048], P(('dp', 'row'), 'col')
- inputs_grad: bfloat16 [8192, 2048], P(('dp', 'row'), 'col')
- attention_gain_grad: float32 [2048], P('col')
- query_weight_grad: float32 [2048, 3072], P('col', 'row')
- latent_weight_grad: float32 [2048, 576], P('col')
- latent_gain_grad: float32 [512], replicated
- expand_weight_grad: float32 [512, 4096], P(None, ('row', 'col'))
- output_weight_grad: float32 [2048, 2048], P('row', 'col')
- feedforward_gain_grad: float32 [2048], P('col')
- router_weight_grad: float32 [2048, 8], P('col')
- shared_gate_grad: float32 [2048, 2816], P('col', 'row')
- shared_up_grad: float32 [2048, 2816], P('col', 'row')
- shared_down_grad: float32 [2816, 2048], P('row', 'col')
- expert_gate_grad: float32 [8, 2048, 1408], P('dp', 'col', 'row')
- expert_up_grad: float32 [8, 2048, 1408], P('dp', 'col', 'row')
- expert_down_grad: float32 [8, 1408, 2048], P('dp', 'row', 'col')
Inputs may be any that keep to these rules, and one draw needn't show every extreme that they name: `routes`: within the 1024 rows of one sequence no expert is named by more than 832 rows, a bound that some block reaches; a row names 6 different experts.
All inputs are finite; a program needn't handle non-finite values.
Results may differ from a plain program's by a relative error of at most 0.019.
Values may be sent and summed in bfloat16 or wider, within the bound.
A program may use at most 256 MiB of HBM per device.

v0:
```python
import math

import jax
import jax.numpy as jnp
from jax import lax
from jax.sharding import PartitionSpec as P

D = 2048
NOPE = 128
ROPE = 64
VDIM = 128
RANK = 512
TOPK = 6
EXPERTS = 8
SEQ = 1024
CAP = 832


norm_eps = 1e-06
highest = lax.Precision.HIGHEST
masked_score = -1e30


def rotary_tables(length, half_width):
    position = jnp.arange(length, dtype=jnp.float32)[:, None]
    frequency = jnp.exp(
        jnp.arange(half_width, dtype=jnp.float32) * (-math.log(10000.0) / half_width)
    )
    angles = position * frequency[None, :]
    return (jnp.cos(angles), jnp.sin(angles))


def rotate(values, cos_table, sin_table):
    half_width = cos_table.shape[-1]
    first_half = values[..., :half_width]
    second_half = values[..., half_width:]
    return jnp.concatenate(
        [
            first_half * cos_table - second_half * sin_table,
            second_half * cos_table + first_half * sin_table,
        ],
        axis=-1,
    )


def dispatch(route_rows):
    pair_count = route_rows.shape[0] * TOPK
    flat_routes = route_rows.reshape(-1)
    one_hot = (flat_routes[:, None] == jnp.arange(EXPERTS, dtype=jnp.int32)[None, :]).astype(
        jnp.int32
    )
    before = jnp.cumsum(one_hot, axis=0) - one_hot
    position = jnp.sum(before * one_hot, axis=1)
    token_ids = jnp.arange(pair_count, dtype=jnp.int32) // TOPK
    slot_token = jnp.zeros((EXPERTS, CAP), jnp.int32).at[flat_routes, position].set(token_ids)
    filled = (
        jnp.zeros((EXPERTS, CAP), jnp.int32).at[flat_routes, position].set(jnp.ones_like(token_ids))
    )
    return (slot_token, filled)


def gather_rows(values):
    return lax.all_gather(values, "row", axis=0, tiled=True)


def sum_rows(values):
    return lax.psum_scatter(values, "row", scatter_dimension=0, tiled=True)


def col_total(values):
    return lax.psum(values, "col")


def head_total(values):
    return lax.psum_scatter(values, "col", scatter_dimension=1, tiled=True)


def head_collect(values):
    return lax.all_gather(values, "col", axis=1, tiled=True)


def grid_total(values):
    return lax.psum(values, ("row", "col"))


def norm_scale(values):
    total_sq = col_total(jnp.sum(values * values, axis=1))
    return lax.rsqrt(total_sq / D + norm_eps)


def norm_back(values, gain_row, scale_row, upstream):
    weighted = upstream * gain_row[None, :]
    inner_sum = col_total(jnp.sum(weighted * values, axis=1))
    value_grad = (
        scale_row[:, None] * weighted
        - values * (scale_row * scale_row * scale_row * inner_sum / D)[:, None]
    )
    gain_grad = jnp.sum(upstream * values * scale_row[:, None], axis=0)
    return (value_grad, gain_grad)


def silu_slope(pre_value):
    sigmoid_value = jax.nn.sigmoid(pre_value)
    return sigmoid_value * (1.0 + pre_value * (1.0 - sigmoid_value))


def visible_mask(offset, block_rows, prefix_len):
    query_pos = offset + jnp.arange(block_rows, dtype=jnp.int32)
    key_pos = jnp.arange(SEQ, dtype=jnp.int32)
    return (key_pos[None, :] <= query_pos[:, None]) | (key_pos[None, :] < prefix_len)


def attend_forward(queries, key_rows, value_rows, prefix_len):
    block_rows = min(512, SEQ)
    score_scale = (NOPE + ROPE) ** (-0.5)

    def one_block(offset):
        query_block = lax.dynamic_slice_in_dim(queries, offset, block_rows, 0)
        scores = (
            jnp.einsum("qd,kd->qk", query_block, key_rows, preferred_element_type=jnp.float32)
            * score_scale
        )
        scores = jnp.where(visible_mask(offset, block_rows, prefix_len), scores, masked_score)
        top_score = jnp.max(scores, axis=1, keepdims=True)
        exp_scores = jnp.exp(scores - top_score)
        row_total = jnp.sum(exp_scores, axis=1, keepdims=True)
        weights = (exp_scores / row_total).astype(jnp.bfloat16)
        result = jnp.dot(weights, value_rows, preferred_element_type=jnp.float32)
        return (result, (top_score + jnp.log(row_total))[:, 0])

    starts = jnp.arange(SEQ // block_rows, dtype=jnp.int32) * block_rows
    result, log_total = lax.map(one_block, starts)
    return (result.reshape(SEQ, VDIM), log_total.reshape(SEQ))


def attend_backward(queries, key_rows, value_rows, log_total, out_grad, prefix_len):
    block_rows = min(512, SEQ)
    score_scale = (NOPE + ROPE) ** (-0.5)

    def one_block(running, offset):
        key_grad, value_grad = running
        query_block = lax.dynamic_slice_in_dim(queries, offset, block_rows, 0)
        grad_block = lax.dynamic_slice_in_dim(out_grad, offset, block_rows, 0)
        total_block = lax.dynamic_slice_in_dim(log_total, offset, block_rows, 0)
        scores = (
            jnp.einsum("qd,kd->qk", query_block, key_rows, preferred_element_type=jnp.float32)
            * score_scale
        )
        scores = jnp.where(visible_mask(offset, block_rows, prefix_len), scores, masked_score)
        weights = jnp.exp(scores - total_block[:, None])
        value_grad = value_grad + jnp.einsum(
            "qk,qd->kd",
            weights.astype(jnp.bfloat16),
            grad_block,
            preferred_element_type=jnp.float32,
        )
        weight_grad = jnp.einsum(
            "qd,kd->qk", grad_block, value_rows, preferred_element_type=jnp.float32
        )
        centre = jnp.sum(weights * weight_grad, axis=1, keepdims=True)
        score_grad = (weights * (weight_grad - centre)).astype(jnp.bfloat16)
        query_grad = (
            jnp.einsum("qk,kd->qd", score_grad, key_rows, preferred_element_type=jnp.float32)
            * score_scale
        )
        key_grad = (
            key_grad
            + jnp.einsum("qk,qd->kd", score_grad, query_block, preferred_element_type=jnp.float32)
            * score_scale
        )
        return ((key_grad, value_grad), query_grad)

    starts = jnp.arange(SEQ // block_rows, dtype=jnp.int32) * block_rows
    start_state = (jnp.zeros((SEQ, NOPE + ROPE), jnp.float32), jnp.zeros((SEQ, VDIM), jnp.float32))
    (key_grad, value_grad), query_grad = lax.scan(one_block, start_state, starts)
    return (query_grad.reshape(SEQ, NOPE + ROPE), key_grad, value_grad)


def on_device(
    inputs,
    attention_gain,
    query_weight,
    latent_weight,
    latent_gain,
    expand_weight,
    output_weight,
    feedforward_gain,
    router_weight,
    shared_gate,
    shared_up,
    shared_down,
    expert_gate,
    expert_up,
    expert_down,
    routes,
    prefix,
    cotangent,
):
    row_index = lax.axis_index("row")
    col_index = lax.axis_index("col")
    col_count = lax.axis_size("col")
    quarter = CAP // col_count
    prefix_len = prefix[0]
    cos_table, sin_table = rotary_tables(SEQ, ROPE // 2)
    first_gain = attention_gain.astype(jnp.float32)
    second_gain = feedforward_gain.astype(jnp.float32)
    compact_gain = latent_gain.astype(jnp.float32)
    residual_in = inputs.astype(jnp.float32)
    scale_one = norm_scale(residual_in)
    normed = (residual_in * scale_one[:, None] * first_gain[None, :]).astype(jnp.bfloat16)
    normed_rows = gather_rows(normed)
    queries_all = head_total(jnp.dot(normed_rows, query_weight, preferred_element_type=jnp.float32))
    latent = col_total(jnp.dot(normed_rows, latent_weight, preferred_element_type=jnp.float32))
    content = latent[:, :RANK]
    latent_scale = lax.rsqrt(jnp.mean(content * content, axis=1) + norm_eps)
    compact = (content * latent_scale[:, None] * compact_gain[None, :]).astype(jnp.bfloat16)
    shared_key = rotate(latent[:, RANK:], cos_table, sin_table).astype(jnp.bfloat16)
    key_value = jnp.dot(compact, expand_weight, preferred_element_type=jnp.float32).astype(
        jnp.bfloat16
    )
    head_slot = 0
    query_rot = jnp.concatenate(
        [queries_all[:, :NOPE], rotate(queries_all[:, NOPE:], cos_table, sin_table)], axis=1
    ).astype(jnp.bfloat16)
    column_base = head_slot * (NOPE + VDIM)
    key_rows = jnp.concatenate([key_value[:, column_base : column_base + NOPE], shared_key], axis=1)
    value_rows = key_value[:, column_base + NOPE : column_base + NOPE + VDIM]
    head_result, log_total = attend_forward(query_rot, key_rows, value_rows, prefix_len)
    kept_queries = [query_rot]
    kept_keys = [key_rows]
    kept_values = [value_rows]
    kept_totals = [log_total]
    attended = head_result.astype(jnp.bfloat16)
    attended_rows = head_collect(attended)
    residual_mid = residual_in + sum_rows(
        jnp.dot(attended_rows, output_weight, preferred_element_type=jnp.float32)
    )
    scale_two = norm_scale(residual_mid)
    hidden = (residual_mid * scale_two[:, None] * second_gain[None, :]).astype(jnp.bfloat16)
    hidden_rows = gather_rows(hidden)
    router_probs = jax.nn.softmax(
        col_total(jnp.dot(hidden_rows, router_weight, preferred_element_type=jnp.float32)), axis=1
    )
    slot_token, filled = dispatch(routes)
    slot_fill = filled.astype(jnp.float32)
    slot_weight = (
        router_probs[slot_token, jnp.arange(EXPERTS, dtype=jnp.int32)[:, None]] * slot_fill
    )
    slot_rows = hidden_rows[slot_token] * filled[:, :, None].astype(jnp.bfloat16)
    my_weight = lax.dynamic_slice_in_dim(slot_weight, col_index * quarter, quarter, 1)
    my_token = lax.dynamic_slice_in_dim(slot_token, col_index * quarter, quarter, 1)
    my_fill = lax.dynamic_slice_in_dim(slot_fill, col_index * quarter, quarter, 1)
    shared_gate_part = jnp.dot(hidden_rows, shared_gate, preferred_element_type=jnp.float32)
    shared_up_part = jnp.dot(hidden_rows, shared_up, preferred_element_type=jnp.float32)
    expert_gate_part = jnp.einsum(
        "ecd,edf->ecf", slot_rows, expert_gate, preferred_element_type=jnp.float32
    )
    expert_up_part = jnp.einsum(
        "ecd,edf->ecf", slot_rows, expert_up, preferred_element_type=jnp.float32
    )
    shared_gate_pre, shared_up_pre, expert_gate_pre, expert_up_pre = (
        lax.psum_scatter(shared_gate_part, "col", scatter_dimension=0, tiled=True),
        lax.psum_scatter(shared_up_part, "col", scatter_dimension=0, tiled=True),
        lax.psum_scatter(expert_gate_part, "col", scatter_dimension=1, tiled=True),
        lax.psum_scatter(expert_up_part, "col", scatter_dimension=1, tiled=True),
    )
    shared_act = (jax.nn.silu(shared_gate_pre) * shared_up_pre).astype(jnp.bfloat16)
    expert_act = (my_weight[:, :, None] * (jax.nn.silu(expert_gate_pre) * expert_up_pre)).astype(
        jnp.bfloat16
    )
    shared_act_rows, expert_act_rows = (
        lax.all_gather(shared_act, "col", axis=0, tiled=True),
        lax.all_gather(expert_act, "col", axis=1, tiled=True),
    )
    combined = jnp.dot(shared_act_rows, shared_down, preferred_element_type=jnp.float32)
    expert_out = jnp.einsum(
        "ecf,efd->ecd", expert_act_rows, expert_down, preferred_element_type=jnp.float32
    )
    combined = combined.at[slot_token.reshape(-1)].add(expert_out.reshape(-1, expert_out.shape[2]))
    output = (residual_mid + sum_rows(combined)).astype(jnp.bfloat16)
    out_grad_rows = gather_rows(cotangent)
    shared_act_part = jnp.einsum(
        "td,fd->tf", out_grad_rows, shared_down, preferred_element_type=jnp.float32
    )
    slot_grad_rows = out_grad_rows[slot_token] * filled[:, :, None].astype(jnp.bfloat16)
    expert_act_part = jnp.einsum(
        "ecd,efd->ecf", slot_grad_rows, expert_down, preferred_element_type=jnp.float32
    )
    shared_act_grad, expert_act_grad = (
        lax.psum_scatter(shared_act_part, "col", scatter_dimension=0, tiled=True),
        lax.psum_scatter(expert_act_part, "col", scatter_dimension=1, tiled=True),
    )
    shared_down_grad = jnp.einsum(
        "tf,td->fd", shared_act_rows, out_grad_rows, preferred_element_type=jnp.float32
    )
    expert_down_grad = jnp.einsum(
        "ecf,ecd->efd", expert_act_rows, slot_grad_rows, preferred_element_type=jnp.float32
    )
    shared_gate_delta = (shared_act_grad * shared_up_pre * silu_slope(shared_gate_pre)).astype(
        jnp.bfloat16
    )
    shared_up_delta = (shared_act_grad * jax.nn.silu(shared_gate_pre)).astype(jnp.bfloat16)
    expert_silu = jax.nn.silu(expert_gate_pre)
    weighted_grad = my_weight[:, :, None] * expert_act_grad
    expert_gate_delta = (weighted_grad * expert_up_pre * silu_slope(expert_gate_pre)).astype(
        jnp.bfloat16
    )
    expert_up_delta = (weighted_grad * expert_silu).astype(jnp.bfloat16)
    weight_term = jnp.sum(expert_act_grad * expert_silu * expert_up_pre, axis=2) * my_fill
    flat_slot = (my_token * EXPERTS + jnp.arange(EXPERTS, dtype=jnp.int32)[:, None]).reshape(-1)
    probs_local = (
        jnp.zeros((SEQ * EXPERTS,), jnp.float32).at[flat_slot].add(weight_term.reshape(-1))
    )
    probs_grad = grid_total(probs_local.reshape(SEQ, EXPERTS))
    logits_grad = router_probs * (
        probs_grad - jnp.sum(router_probs * probs_grad, axis=1, keepdims=True)
    )
    shared_gate_rows, shared_up_rows, expert_gate_rows, expert_up_rows = (
        lax.all_gather(shared_gate_delta, "col", axis=0, tiled=True),
        lax.all_gather(shared_up_delta, "col", axis=0, tiled=True),
        lax.all_gather(expert_gate_delta, "col", axis=1, tiled=True),
        lax.all_gather(expert_up_delta, "col", axis=1, tiled=True),
    )
    hidden_grad = jnp.einsum(
        "tf,df->td", shared_gate_rows, shared_gate, preferred_element_type=jnp.float32
    )
    hidden_grad = hidden_grad + jnp.einsum(
        "tf,df->td", shared_up_rows, shared_up, preferred_element_type=jnp.float32
    )
    slot_grad = jnp.einsum(
        "ecf,edf->ecd", expert_gate_rows, expert_gate, preferred_element_type=jnp.float32
    )
    slot_grad = slot_grad + jnp.einsum(
        "ecf,edf->ecd", expert_up_rows, expert_up, preferred_element_type=jnp.float32
    )
    hidden_grad = hidden_grad.at[slot_token.reshape(-1)].add(
        slot_grad.reshape(-1, slot_grad.shape[2])
    )
    router_term = jnp.einsum(
        "te,de->td", logits_grad, router_weight.astype(jnp.float32), precision=highest
    )
    hidden_grad = hidden_grad + jnp.where(row_index == 0, router_term, jnp.zeros_like(router_term))
    router_grad = jnp.einsum(
        "td,te->de", hidden_rows.astype(jnp.float32), logits_grad, precision=highest
    )
    shared_gate_grad = jnp.einsum(
        "td,tf->df", hidden_rows, shared_gate_rows, preferred_element_type=jnp.float32
    )
    shared_up_grad = jnp.einsum(
        "td,tf->df", hidden_rows, shared_up_rows, preferred_element_type=jnp.float32
    )
    expert_gate_grad = jnp.einsum(
        "ecd,ecf->edf", slot_rows, expert_gate_rows, preferred_element_type=jnp.float32
    )
    expert_up_grad = jnp.einsum(
        "ecd,ecf->edf", slot_rows, expert_up_rows, preferred_element_type=jnp.float32
    )
    mid_norm_grad, second_gain_part = norm_back(
        residual_mid, second_gain, scale_two, sum_rows(hidden_grad)
    )
    residual_grad = cotangent.astype(jnp.float32) + mid_norm_grad
    residual_rows = gather_rows(residual_grad.astype(jnp.bfloat16))
    output_weight_grad = jnp.einsum(
        "th,td->hd", attended_rows, residual_rows, preferred_element_type=jnp.float32
    )
    attended_grad = head_total(
        jnp.einsum("td,hd->th", residual_rows, output_weight, preferred_element_type=jnp.float32)
    ).astype(jnp.bfloat16)
    head_slot = 0
    query_rot_grad, key_grad, value_grad = attend_backward(
        kept_queries[head_slot],
        kept_keys[head_slot],
        kept_values[head_slot],
        kept_totals[head_slot],
        attended_grad,
        prefix_len,
    )
    query_grads = jnp.concatenate(
        [query_rot_grad[:, :NOPE], rotate(query_rot_grad[:, NOPE:], cos_table, -sin_table)], axis=1
    )
    pair_grads = jnp.concatenate([key_grad[:, :NOPE], value_grad], axis=1)
    shared_key_part = key_grad[:, NOPE:]
    query_grad_all = query_grads.astype(jnp.bfloat16)
    pair_grad_all = pair_grads.astype(jnp.bfloat16)
    expand_grad = jnp.einsum(
        "tr,tk->rk", compact, pair_grad_all, preferred_element_type=jnp.float32
    )
    compact_part = jnp.einsum(
        "tk,rk->tr", pair_grad_all, expand_weight, preferred_element_type=jnp.float32
    )
    latent_pre_grad = grid_total(jnp.concatenate([compact_part, shared_key_part], axis=1))
    compact_grad = latent_pre_grad[:, :RANK]
    rotary_grad = rotate(latent_pre_grad[:, RANK:], cos_table, -sin_table)
    weighted_compact = compact_grad * compact_gain[None, :]
    inner_sum = jnp.sum(weighted_compact * content, axis=1)
    content_grad = (
        latent_scale[:, None] * weighted_compact
        - content * (latent_scale * latent_scale * latent_scale * inner_sum / RANK)[:, None]
    )
    latent_gain_grad = jnp.sum(compact_grad * content * latent_scale[:, None], axis=0)
    latent_grad = jnp.concatenate([content_grad, rotary_grad], axis=1).astype(jnp.bfloat16)
    latent_weight_grad = jnp.einsum(
        "td,tl->dl", normed_rows, latent_grad, preferred_element_type=jnp.float32
    )
    latent_term = jnp.einsum(
        "tl,dl->td", latent_grad, latent_weight, preferred_element_type=jnp.float32
    )
    query_rows = head_collect(query_grad_all)
    query_weight_grad = jnp.einsum(
        "td,tq->dq", normed_rows, query_rows, preferred_element_type=jnp.float32
    )
    normed_grad = jnp.einsum(
        "tq,dq->td", query_rows, query_weight, preferred_element_type=jnp.float32
    )
    normed_grad = normed_grad + jnp.where(row_index == 0, latent_term, jnp.zeros_like(latent_term))
    input_norm_grad, first_gain_part = norm_back(
        residual_in, first_gain, scale_one, sum_rows(normed_grad)
    )
    inputs_grad = (residual_grad + input_norm_grad).astype(jnp.bfloat16)
    expert_gate_grad, expert_up_grad, expert_down_grad = (
        lax.psum_scatter(expert_gate_grad, "dp", scatter_dimension=0, tiled=True),
        lax.psum_scatter(expert_up_grad, "dp", scatter_dimension=0, tiled=True),
        lax.psum_scatter(expert_down_grad, "dp", scatter_dimension=0, tiled=True),
    )
    (
        query_weight_grad,
        latent_weight_grad,
        latent_gain_grad,
        expand_grad,
        output_weight_grad,
        router_grad,
        shared_gate_grad,
        shared_up_grad,
        shared_down_grad,
    ) = lax.psum(
        (
            query_weight_grad,
            latent_weight_grad,
            latent_gain_grad,
            expand_grad,
            output_weight_grad,
            router_grad,
            shared_gate_grad,
            shared_up_grad,
            shared_down_grad,
        ),
        "dp",
    )
    first_gain_grad, second_gain_grad = lax.psum((first_gain_part, second_gain_part), ("dp", "row"))
    return (
        output,
        inputs_grad,
        first_gain_grad,
        query_weight_grad,
        latent_weight_grad,
        latent_gain_grad,
        expand_grad,
        output_weight_grad,
        second_gain_grad,
        router_grad,
        shared_gate_grad,
        shared_up_grad,
        shared_down_grad,
        expert_gate_grad,
        expert_up_grad,
        expert_down_grad,
    )


def solution(mesh):
    placed = (
        P(("dp", "row"), "col"),
        P("col"),
        P("col", "row"),
        P("col", None),
        P(),
        P(None, ("row", "col")),
        P("row", "col"),
        P("col"),
        P("col", None),
        P("col", "row"),
        P("col", "row"),
        P("row", "col"),
        P(None, "col", "row"),
        P(None, "col", "row"),
        P(None, "row", "col"),
        P("dp", None),
        P("dp"),
        P(("dp", "row"), "col"),
    )
    return jax.shard_map(
        on_device,
        mesh=mesh,
        in_specs=placed,
        out_specs=(
            P(("dp", "row"), "col"),
            P(("dp", "row"), "col"),
            P("col"),
            P("col", "row"),
            P("col", None),
            P(),
            P(None, ("row", "col")),
            P("row", "col"),
            P("col"),
            P("col", None),
            P("col", "row"),
            P("col", "row"),
            P("row", "col"),
            P("dp", "col", "row"),
            P("dp", "col", "row"),
            P("dp", "row", "col"),
        ),
        check_vma=False,
    )
```

profile of v0, /device:TPU:5, one launch (start us, length us, event | category | flops | bytes accessed | tf_op | source)
XLA Modules:
  0.0 1942.1 jit_solution(10393854372003021542)
XLA Ops:
  17.3 26.4 %all-gather.13.cloned.1.call-done = bf16[1024,512]{1,0:T(8,128)(2,1)} async-done(((bf16[256,512]{1,0:T(8,128)(2,1)}), bf16[1024,512]{1,0:T(8,128)(2,1)}) %all-gather.13.cloned.1.call-update) | async-done | bytes 1048592 | tf_op jit(solution)/shard_map/all_gather | solution.py:63
  52.2 58.2 %all-reduce.7.cloned.1.call-done = f32[1024,576]{0,1:T(8,128)} async-done(((f32[1024,576]{0,1:T(8,128)}), f32[1024,576]{0,1:T(8,128)}) %all-reduce.7.cloned.1.call-update) | async-done | bytes 2359312 | tf_op jit(solution)/shard_map/psum | solution.py:71
  115.8 34.7 %reduce-scatter.16.cloned.1.call-done = f32[1024,192]{0,1:T(8,128)} async-done(((f32[1024,768]{0,1:T(8,128)}), f32[1024,192]{0,1:T(8,128)}) %reduce-scatter.16.cloned.1.call-update) | async-done | bytes 786448 | tf_op jit(solution)/shard_map/reduce_scatter | solution.py:75
  173.4 22.4 %all-gather.15.cloned.1.call-done = bf16[1024,512]{1,0:T(8,128)(2,1)} async-done(((bf16[1024,128]{1,0:T(8,128)(2,1)}), bf16[1024,512]{1,0:T(8,128)(2,1)}) %all-gather.15.cloned.1.call-update) | async-done | bytes 1048592 | tf_op jit(solution)/shard_map/all_gather | solution.py:79
  200.0 30.0 %reduce-scatter.18.cloned.1.call-done = f32[256,512]{1,0:T(8,128)} async-done(((f32[1024,512]{1,0:T(8,128)}), f32[256,512]{1,0:T(8,128)}) %reduce-scatter.18.cloned.1.call-update) | async-done | bytes 524304 | tf_op jit(solution)/shard_map/reduce_scatter | solution.py:67
  258.5 22.5 %all-gather.17.cloned.1.call-done = bf16[1024,512]{1,0:T(8,128)(2,1)} async-done(((bf16[256,512]{1,0:T(8,128)(2,1)}), bf16[1024,512]{1,0:T(8,128)(2,1)}) %all-gather.17.cloned.1.call-update) | async-done | bytes 1048592 | tf_op jit(solution)/shard_map/all_gather | solution.py:63
  294.6 23.0 %scatter_custom_fusion.3 = s32[6656]{0:T(1024)S(1)} fusion(s32[6144]{0:T(1024)S(1)} %broadcast_select_fusion, s32[6144]{0:T(1024)S(1)} %add_select_fusion, s32[]{:T(128)} %constant.34.clone.1), kind=kCustom, calls=%fused_computation.163 | custom fusion | bytes 26628
  317.6 23.0 %scatter_custom_fusion.4 = s32[6656]{0:T(1024)S(1)} fusion(s32[6144]{0:T(1024)S(1)} %broadcast_select_fusion, s32[6144]{0:T(1024)S(1)} %ne.14, s32[]{:T(128)} %constant.34.clone.1), kind=kCustom, calls=%fused_computation.161 | custom fusion | bytes 26628
  340.9 21.0 %gather_fusion.2 = bf16[6656,512]{1,0:T(8,128)(2,1)} fusion(bf16[1024,512]{1,0:T(8,128)(2,1)} %all-gather.23.cloned.1.call-done, s32[7168]{0:T(1024)S(1)} %pad_clamp_fusion), kind=kCustom, calls=%fused_computation.2 | custom fusion | bytes 13658112 | tf_op jit(solution)/shard_map/gather | solution.py:285
  371.3 21.0 %gather_fusion.1 = bf16[6656,512]{1,0:T(8,128)(2,1)} fusion(bf16[1024,512]{1,0:T(8,128)(2,1)} %all-gather.17.cloned.1.call-done, s32[7168]{0:T(1024)S(1)} %pad_clamp_fusion), kind=kCustom, calls=%fused_computation.1 | custom fusion | bytes 13658112 | tf_op jit(solution)/shard_map/gather | solution.py:249
  439.6 54.2 %reduce-scatter.32.cloned.1.call-done = f32[8,208,352]{2,1,0:T(8,128)} async-done(((f32[8,832,352]{2,1,0:T(8,128)}), f32[8,208,352]{2,1,0:T(8,128)}) %reduce-scatter.32.cloned.1.call-update) | async-done | bytes 2342928 | tf_op jit(solution)/shard_map/reduce_scatter | solution.py:291
  493.8 97.3 %reduce-scatter.26.cloned.1.call-done = f32[8,208,352]{2,1,0:T(8,128)} async-done(((f32[8,832,352]{2,1,0:T(8,128)}), f32[8,208,352]{2,1,0:T(8,128)}) %reduce-scatter.26.cloned.1.call-update) | async-done | bytes 2342928 | tf_op jit(solution)/shard_map/reduce_scatter | solution.py:265
  591.1 97.5 %reduce-scatter.24.cloned.1.call-done = f32[8,208,352]{2,1,0:T(8,128)} async-done(((f32[8,832,352]{2,1,0:T(8,128)}), f32[8,208,352]{2,1,0:T(8,128)}) %reduce-scatter.24.cloned.1.call-update) | async-done | bytes 2342928 | tf_op jit(solution)/shard_map/reduce_scatter | solution.py:264
  706.1 51.7 %psum.137 = f32[1024,8]{0,1:T(8,128)S(1)} all-reduce(f32[1024,8]{0,1:T(8,128)S(1)} %copy.60), channel_id=1, replica_groups=mesh['dp'=8,'row'=4,'col'=4] {'row','col'}, use_global_device_ids=true, to_apply=%region_30.31 | all-reduce | flops 8192 | bytes 65536 | tf_op jit(solution)/shard_map/psum | solution.py:83
  757.8 39.5 %gather_fusion = f32[6656]{0:T(1024)S(1)} fusion(f32[1024,8]{0,1:T(8,128)S(1)} %get-tuple-element.272, s32[6656]{0:T(1024)S(1)} %reshape.273), kind=kCustom, calls=%fused_computation | custom fusion | bytes 106496 | tf_op jit(solution)/shard_map/gather | solution.py:247
  813.7 46.7 %all-gather.29.cloned.1.call-done = bf16[8,832,352]{2,1,0:T(8,128)(2,1)} async-done(((bf16[8,208,352]{2,1,0:T(8,128)(2,1)}), bf16[8,832,352]{2,1,0:T(8,128)(2,1)}) %all-gather.29.cloned.1.call-update) | async-done | bytes 4685840 | tf_op jit(solution)/shard_map/all_gather | solution.py:321
  869.8 47.9 %all-gather.31.cloned.1.call-done = bf16[8,832,352]{2,1,0:T(8,128)(2,1)} async-done(((bf16[8,208,352]{2,1,0:T(8,128)(2,1)}), bf16[8,832,352]{2,1,0:T(8,128)(2,1)}) %all-gather.31.cloned.1.call-update) | async-done | bytes 4685840 | tf_op jit(solution)/shard_map/all_gather | solution.py:322
  933.6 41.4 %scatter_fusion.1 = f32[1024,512]{1,0:T(8,128)S(1)} fusion(f32[1024,512]{1,0:T(8,128)S(1)} %copy-done.4, s32[6656]{0:T(1024)S(1)} %fusion.59, f32[6656,512]{1,0:T(8,128)} %bitcast.131), kind=kCustom, calls=%fused_computation.5 | custom fusion | flops 3407872 | bytes 40921088 | tf_op jit(solution)/shard_map/scatter-add | solution.py:336
  976.5 30.6 %reduce-scatter.34.cloned.1.call-done = f32[256,512]{1,0:T(8,128)} async-done(((f32[1024,512]{1,0:T(8,128)}), f32[256,512]{1,0:T(8,128)}) %reduce-scatter.34.cloned.1.call-update) | async-done | bytes 524304 | tf_op jit(solution)/shard_map/reduce_scatter | solution.py:67
  1016.6 23.7 %all-gather.33.cloned.1.call-done = bf16[1024,512]{1,0:T(8,128)(2,1)} async-done(((bf16[256,512]{1,0:T(8,128)(2,1)}), bf16[1024,512]{1,0:T(8,128)(2,1)}) %all-gather.33.cloned.1.call-update) | async-done | bytes 1048592 | tf_op jit(solution)/shard_map/all_gather | solution.py:63
  1044.2 29.0 %reduce-scatter.36.cloned.1.call-done = f32[1024,128]{1,0:T(8,128)} async-done(((f32[1024,512]{1,0:T(8,128)}), f32[1024,128]{1,0:T(8,128)}) %reduce-scatter.36.cloned.1.call-update) | async-done | bytes 524304 | tf_op jit(solution)/shard_map/reduce_scatter | solution.py:75
  1075.0 30.3 %while.28 = (s32[]{:T(128)}, f32[1024,192]{0,1:T(8,128)S(1)}, f32[1024,128]{1,0:T(8,128)}, f32[2,512,192]{1,0,2:T(2,128)}, s32[2]{0:T(128)S(1)}, /*index=5*/s32[...) while((s32[]{:T(128)}, f32[1024,192]{0,1:T(8,128)S(1)}, ...), condition=%wide.region_39.40_spmd.clone, body=%wide.region_37.39_spmd.clone.sunk | while | flops 879133696 | bytes 34357616 | solution.py:175
  1111.9 124.0 %all-reduce.9.cloned.1.call-done = f32[1024,576]{0,1:T(8,128)} async-done(((f32[1024,576]{0,1:T(8,128)}), f32[1024,576]{0,1:T(8,128)}) %all-reduce.9.cloned.1.call-update) | async-done | bytes 2359312 | tf_op jit(solution)/shard_map/psum | solution.py:83
  1243.5 21.3 %all-gather.35.cloned.1.call-done = bf16[1024,768]{0,1:T(8,128)(2,1)} async-done(((bf16[1024,192]{0,1:T(8,128)(2,1)}), bf16[1024,768]{0,1:T(8,128)(2,1)}) %all-gather.35.cloned.1.call-update) | async-done | bytes 1572880 | tf_op jit(solution)/shard_map/all_gather | solution.py:79
  1270.0 22.0 %all-gather.19.cloned.1.call-done = bf16[1024,704]{0,1:T(8,128)(2,1)} async-done(((bf16[256,704]{0,1:T(8,128)(2,1)}), bf16[1024,704]{0,1:T(8,128)(2,1)}) %all-gather.19.cloned.1.call-update) | async-done | bytes 1441808 | tf_op jit(solution)/shard_map/all_gather | solution.py:272
  1294.5 54.7 %all-gather.21.cloned.1.call-done = bf16[8,832,352]{2,1,0:T(8,128)(2,1)} async-done(((bf16[8,208,352]{2,1,0:T(8,128)(2,1)}), bf16[8,832,352]{2,1,0:T(8,128)(2,1)}) %all-gather.21.cloned.1.call-update) | async-done | bytes 4685840 | tf_op jit(solution)/shard_map/all_gather | solution.py:273
  1361.2 41.6 %scatter_fusion = f32[1024,512]{1,0:T(8,128)S(1)} fusion(f32[1024,512]{1,0:T(8,128)S(1)} %fusion.91, s32[6656]{0:T(1024)S(1)} %fusion.59, f32[6656,512]{1,0:T(8,128)} %bitcast.130), kind=kCustom, calls=%fused_computation.3 | custom fusion | flops 3407872 | bytes 40921088 | tf_op jit(solution)/shard_map/scatter-add | solution.py:279
  1454.4 33.7 %all-reduce.1 = (f32[512]{0:T(512)}, f32[512,8]{0,1:T(8,128)}) all-reduce(f32[512]{0:T(512)S(1)} %get-tuple-element.216, f32[512,8]{0,1:T(8,128)S(1)} %fusion.69), channel_id=1, replica_groups=mesh['dp'=8,'row'=4,'col'=4] {'dp'}, use_global_device_ids=true, to_apply=%region_50.51 | all-reduce | flops 4608 | bytes 36864 | tf_op jit(solution)/shard_map/psum | solution.py:435
  1501.0 77.7 %all-reduce = (f32[512]{0:T(512)}, f32[512]{0:T(512)}) all-reduce(f32[512]{0:T(512)S(1)} %get-tuple-element.220, f32[512]{0:T(512)S(1)} %copy-done.76), channel_id=1, replica_groups=mesh['dp'=8,'row'=4,'col'=4] {'dp','row'}, use_global_device_ids=true, to_apply=%region_46.47 | all-reduce | flops 1024 | bytes 8192 | tf_op jit(solution)/shard_map/psum | solution.py:449
  1581.1 49.4 %reduce-scatter.42.cloned.1.call-done = f32[1,512,352]{1,2,0:T(8,128)} async-done(((f32[8,512,352]{1,2,0:T(8,128)}), f32[1,512,352]{1,2,0:T(8,128)}) %reduce-scatter.42.cloned.1.call-update) | async-done | bytes 720912 | tf_op jit(solution)/shard_map/reduce_scatter | solution.py:422
  1630.4 98.7 %reduce-scatter.40.cloned.1.call-done = f32[1,512,352]{1,2,0:T(8,128)} async-done(((f32[8,512,352]{1,2,0:T(8,128)}), f32[1,512,352]{1,2,0:T(8,128)}) %reduce-scatter.40.cloned.1.call-update) | async-done | bytes 720912 | tf_op jit(solution)/shard_map/reduce_scatter | solution.py:421
  1729.2 196.7 %all-reduce.11.cloned.1.call-done = (f32[512,768]{1,0:T(8,128)}, f32[512,576]{0,1:T(8,128)}, f32[512,256]{1,0:T(8,128)}, f32[512,512]{1,0:T(8,128)}, f32[512,704...) async-done(((f32[512,768]{1,0:T(8,128)}, f32[512,576]{0,1:T(8,128)}, f32[512,256]{1,0:T(8,128)}, f32[512,512]{1,0:T(8,128)}, f32[512,704]{0,1:T(8,128)}, ...) | async-done | bytes 8650768 | tf_op jit(solution)/shard_map/psum | solution.py:435
  (435 shorter events, 373.5 us)
Async XLA Ops:
  7.2 394.6 %copy-start = (bf16[8,512,352]{1,2,0:T(8,128)(2,1)S(1)}, bf16[8,512,352]{1,2,0:T(8,128)(2,1)}, u32[]{:S(2)}) copy-start(bf16[8,512,352]{1,2,0:T(8,128)(2,1)} %param.34) | copy-start | bytes 8650756
  7.2 36.5 %all-gather.13.cloned.1.call-start = ((), (), s32[]{:S(2)}) async-start(), calls=%async_computation.15 | async-start | bytes 1310720 | tf_op jit(solution)/shard_map/all_gather | solution.py:63
  17.3 93.1 %all-reduce.7.cloned.1.call-start = ((), (), s32[]{:S(2)}) async-start(), calls=%async_computation.17 | async-start | bytes 4718592 | tf_op jit(solution)/shard_map/psum | solution.py:71
  47.4 103.1 %reduce-scatter.16.cloned.1.call-start = ((), (), s32[]{:S(2)}) async-start(), calls=%async_computation.16 | async-start | bytes 3932160 | tf_op jit(solution)/shard_map/reduce_scatter | solution.py:75
  51.6 144.3 %all-gather.15.cloned.1.call-start = ((), (), s32[]{:S(2)}) async-start(), calls=%async_computation.18 | async-start | bytes 1310720 | tf_op jit(solution)/shard_map/all_gather | solution.py:79
  173.4 56.6 %reduce-scatter.18.cloned.1.call-start = ((), (), s32[]{:S(2)}) async-start(), calls=%async_computation.19 | async-start | bytes 2621440 | tf_op jit(solution)/shard_map/reduce_scatter | solution.py:67
  199.3 55.1 %all-gather.23.cloned.1.call-start = ((), (), s32[]{:S(2)}) async-start(), calls=%async_computation.28 | async-start | bytes 1310720 | tf_op jit(solution)/shard_map/all_gather | solution.py:63
  199.9 81.1 %all-gather.17.cloned.1.call-start = ((), (), s32[]{:S(2)}) async-start(), calls=%async_computation.20 | async-start | bytes 1310720 | tf_op jit(solution)/shard_map/all_gather | solution.py:63
  238.3 183.0 %reduce-scatter.30.cloned.1.call-start = ((), (), s32[]{:S(2)}) async-start(), calls=%async_computation.29 | async-start | bytes 3604480 | tf_op jit(solution)/shard_map/reduce_scatter | solution.py:290
  258.5 162.9 %reduce-scatter.22.cloned.1.call-start = ((), (), s32[]{:S(2)}) async-start(), calls=%async_computation.22 | async-start | bytes 3604480 | tf_op jit(solution)/shard_map/reduce_scatter | solution.py:263
  285.0 136.4 %reduce-scatter.20.cloned.1.call-start = ((), (), s32[]{:S(2)}) async-start(), calls=%async_computation.21 | async-start | bytes 3604480 | tf_op jit(solution)/shard_map/reduce_scatter | solution.py:262
  289.0 204.7 %reduce-scatter.32.cloned.1.call-start = ((), (), s32[]{:S(2)}) async-start(), calls=%async_computation.32 | async-start | bytes 12779520 | tf_op jit(solution)/shard_map/reduce_scatter | solution.py:291
  371.3 219.8 %reduce-scatter.26.cloned.1.call-start = ((), (), s32[]{:S(2)}) async-start(), calls=%async_computation.25 | async-start | bytes 12779520 | tf_op jit(solution)/shard_map/reduce_scatter | solution.py:265
  401.7 286.9 %reduce-scatter.24.cloned.1.call-start = ((), (), s32[]{:S(2)}) async-start(), calls=%async_computation.24 | async-start | bytes 12779520 | tf_op jit(solution)/shard_map/reduce_scatter | solution.py:264
  410.2 394.1 %all-gather.25.cloned.1.call-start = ((), (), s32[]{:S(2)}) async-start(), calls=%async_computation.30 | async-start | bytes 1802240 | tf_op jit(solution)/shard_map/all_gather | solution.py:319
  424.4 383.8 %all-gather.27.cloned.1.call-start = ((), (), s32[]{:S(2)}) async-start(), calls=%async_computation.31 | async-start | bytes 1802240 | tf_op jit(solution)/shard_map/all_gather | solution.py:320
  424.6 268.2 %copy-start.47 = (f32[8,832]{1,0:T(8,128)}, f32[8,832]{1,0:T(8,128)S(1)}, u32[]{:S(2)}) copy-start(f32[8,832]{1,0:T(8,128)S(1)} %reshape.271) | copy-start | bytes 79876
  425.0 435.4 %all-gather.29.cloned.1.call-start = ((), (), s32[]{:S(2)}) async-start(), calls=%async_computation.33 | async-start | bytes 6389760 | tf_op jit(solution)/shard_map/all_gather | solution.py:321
  803.5 114.2 %all-gather.31.cloned.1.call-start = ((), (), s32[]{:S(2)}) async-start(), calls=%async_computation.34 | async-start | bytes 6389760 | tf_op jit(solution)/shard_map/all_gather | solution.py:322
  804.1 203.0 %reduce-scatter.34.cloned.1.call-start = ((), (), s32[]{:S(2)}) async-start(), calls=%async_computation.35 | async-start | bytes 2621440 | tf_op jit(solution)/shard_map/reduce_scatter | solution.py:67
  976.5 63.9 %all-gather.33.cloned.1.call-start = ((), (), s32[]{:S(2)}) async-start(), calls=%async_computation.36 | async-start | bytes 1310720 | tf_op jit(solution)/shard_map/all_gather | solution.py:63
  1016.5 56.7 %reduce-scatter.36.cloned.1.call-start = ((), (), s32[]{:S(2)}) async-start(), calls=%async_computation.37 | async-start | bytes 2621440 | tf_op jit(solution)/shard_map/reduce_scatter | solution.py:75
  1043.7 192.2 %all-reduce.9.cloned.1.call-start = ((), (), s32[]{:S(2)}) async-start(), calls=%async_computation.39 | async-start | bytes 4718592 | tf_op jit(solution)/shard_map/psum | solution.py:83
  1109.8 155.0 %all-gather.35.cloned.1.call-start = ((), (), s32[]{:S(2)}) async-start(), calls=%async_computation.38 | async-start | bytes 1966080 | tf_op jit(solution)/shard_map/all_gather | solution.py:79
  1238.4 53.6 %all-gather.19.cloned.1.call-start = ((), (), s32[]{:S(2)}) async-start(), calls=%async_computation.23 | async-start | bytes 1802240 | tf_op jit(solution)/shard_map/all_gather | solution.py:272
  1239.2 110.1 %all-gather.21.cloned.1.call-start = ((), (), s32[]{:S(2)}) async-start(), calls=%async_computation.26 | async-start | bytes 6389760 | tf_op jit(solution)/shard_map/all_gather | solution.py:273
  1239.7 248.3 %reduce-scatter.38.cloned.1.call-start = ((), (), s32[]{:S(2)}) async-start(), calls=%async_computation.40 | async-start | bytes 2621440 | tf_op jit(solution)/shard_map/reduce_scatter | solution.py:67
  1269.9 308.8 %reduce-scatter.28.cloned.1.call-start = ((), (), s32[]{:S(2)}) async-start(), calls=%async_computation.27 | async-start | bytes 2621440 | tf_op jit(solution)/shard_map/reduce_scatter | solution.py:67
  1404.0 177.0 %reduce-scatter.44.cloned.1.call-start = ((), (), s32[]{:S(2)}) async-start(), calls=%async_computation.43 | async-start | bytes 6488064 | tf_op jit(solution)/shard_map/reduce_scatter | solution.py:423
  1414.9 215.5 %reduce-scatter.42.cloned.1.call-start = ((), (), s32[]{:S(2)}) async-start(), calls=%async_computation.42 | async-start | bytes 6488064 | tf_op jit(solution)/shard_map/reduce_scatter | solution.py:422
  1425.8 303.4 %reduce-scatter.40.cloned.1.call-start = ((), (), s32[]{:S(2)}) async-start(), calls=%async_computation.41 | async-start | bytes 6488064 | tf_op jit(solution)/shard_map/reduce_scatter | solution.py:421
  1436.9 489.0 %all-reduce.11.cloned.1.call-start = ((), (), s32[]{:S(2)}) async-start(), calls=%async_computation.44 | async-start | bytes 17301504 | tf_op jit(solution)/shard_map/psum | solution.py:435
  (95 other events, 2917.7 us)
Sparse Core Ops, SparseCore 0:
  17.4 26.2 all-gather.12
  47.5 62.8 all-reduce.6
  112.8 37.6 reduce-scatter.15
  173.5 22.3 all-gather.14
  199.4 30.5 reduce-scatter.17
  231.6 22.7 all-gather.22
  256.7 24.2 all-gather.16
  283.6 35.8 reduce-scatter.29
  322.0 35.6 reduce-scatter.21
  360.1 35.5 reduce-scatter.19
  398.3 95.3 reduce-scatter.31
  496.2 94.8 reduce-scatter.25
  593.7 94.8 reduce-scatter.23
  690.8 25.3 all-gather.24
  718.4 25.0 all-gather.26
  803.6 56.7 all-gather.28
  862.6 55.0 all-gather.30
  976.6 30.4 reduce-scatter.33
  1016.6 23.6 all-gather.32
  1043.9 29.3 reduce-scatter.35
  1109.9 125.9 all-reduce.8
  1238.5 26.2 all-gather.34
  1267.2 24.7 all-gather.18
  1294.2 55.0 all-gather.20
  1351.8 30.4 reduce-scatter.37
  1404.2 30.4 reduce-scatter.27
  1439.5 92.1 reduce-scatter.43
  1536.7 93.6 reduce-scatter.41
  1635.4 93.7 reduce-scatter.39
  1733.5 192.2 all-reduce.10
where the time goes:
time: 1950 us; the launch traced here: 1940 us
  waiting for transfers between devices  1210 us (62%)
  blocking collectives  205 us (11%)
  matrix products  177 us (9%)
  local copies, waits for them, and re-layouts  170 us (9%)
  other arithmetic  146 us (7%)
    psum x1, waiting for transfers between devices, on_device(): lax.psum((query_weight_grad, latent_weight_grad, latent_gain_grad, expand...  197 us
    psum x1, waiting for transfers between devices, grid_total(): return lax.psum(values, ('row', 'col'))  124 us
    reduce_scatter x1, waiting for transfers between devices, on_device(): lax.psum_scatter(expert_gate_grad, 'dp', scatter_dimension=0, tiled=True)  98.7 us
    reduce_scatter x1, waiting for transfers between devices, on_device(): lax.psum_scatter(expert_gate_part, 'col', scatter_dimension=1, tiled=True)  97.5 us
    reduce_scatter x1, waiting for transfers between devices, on_device(): lax.psum_scatter(expert_up_part, 'col', scatter_dimension=1, tiled=True)  97.3 us
    all_gather x4, waiting for transfers between devices, gather_rows(): return lax.all_gather(values, 'row', axis=0, tiled=True)  88.7 us
    psum x1, blocking collectives, on_device(): lax.psum((first_gain_part, second_gain_part), ('dp', 'row'))  77.7 us
    unnamed x178, local copies, waits for them, and re-layouts  65.4 us
  transfers between devices with their start and end apart: 30, of which 22 were waited for; matrix products, arithmetic and copies ran while one was open for 18% of the time, Pallas kernels for 0%

commit v1 on v0

v1 whole, which is shorter than its diff:
```python
import math

import jax
import jax.numpy as jnp
from jax import lax
from jax.experimental import pallas as pl
from jax.experimental.pallas import tpu as pltpu
from jax.sharding import PartitionSpec as P

D = 2048
NOPE = 128
ROPE = 64
VDIM = 128
RANK = 512
TOPK = 6
EXPERTS = 8
SEQ = 1024

norm_eps = 1e-06
masked_score = -1e30
bf16 = jnp.bfloat16
f32 = jnp.float32
MESH = pl.DeviceIdType.MESH
DMA = pltpu.SemaphoreType.DMA
VMEM = pl.BlockSpec(memory_space=pltpu.VMEM)


def place():
    row = lax.axis_index("row")
    col = lax.axis_index("col")
    sibling = col + 1 - 2 * lax.rem(col, 2)
    across = lax.rem(col + 2, 4)
    return (row, sibling, across)


def greet(row, sibling, across):
    barrier = pltpu.get_barrier_semaphore()
    pl.semaphore_signal(barrier, inc=1, device_id={"col": sibling}, device_id_type=MESH)
    pl.semaphore_signal(barrier, inc=1, device_id={"col": across}, device_id_type=MESH)
    for step in (1, 2, 3):
        pl.semaphore_signal(
            barrier, inc=1, device_id={"row": lax.rem(row + step, 4)}, device_id_type=MESH
        )
    pl.semaphore_wait(barrier, 5)


def starter(pending):
    def go(source, target, send_sem, recv_sem, **device):
        copy = pltpu.make_async_remote_copy(
            src_ref=source,
            dst_ref=target,
            send_sem=send_sem,
            recv_sem=recv_sem,
            device_id=device,
            device_id_type=MESH,
        )
        copy.start()
        pending.append(copy)
        return copy

    return go


def gather_kernel(own, full, xs, xr, ys, yr, cs, cr):
    row, sibling, across = place()
    rows, columns = own.shape
    greet(row, sibling, across)
    pending = []
    go = starter(pending)

    def block(at_row, at_col):
        start = pl.multiple_of(at_row * rows, rows)
        return full.at[pl.ds(start, rows), pl.ds(at_col * columns, columns)]

    side = go(own, block(row, 2), xs, xr, col=across)
    first = [
        go(own, block(row, 0), ys.at[k - 1], yr.at[k - 1], row=lax.rem(row + k, 4))
        for k in (1, 2, 3)
    ]
    arrivals = [go(own, block(row, 1), cs.at[0], cr.at[0], col=sibling)]
    full[pl.ds(pl.multiple_of(row * rows, rows), rows), pl.ds(0, columns)] = own[...]
    side.wait_recv()
    second = [
        go(block(row, 2), block(row, 2), ys.at[2 + k], yr.at[2 + k], row=lax.rem(row + k, 4))
        for k in (1, 2, 3)
    ]
    arrivals.append(go(block(row, 2), block(row, 3), cs.at[1], cr.at[1], col=sibling))
    count = 2
    for group, at_col in ((first, 0), (second, 2)):
        for k in (1, 3, 2):
            group[k - 1].wait_recv()
            source = lax.rem(row + 4 - k, 4)
            arrivals.append(
                go(
                    block(source, at_col),
                    block(source, at_col + 1),
                    cs.at[count],
                    cr.at[count],
                    col=sibling,
                )
            )
            count += 1
    for copy in arrivals:
        copy.wait_recv()
    for copy in pending:
        copy.wait_send()


def gather_grid(own, collective):
    rows, columns = own.shape
    return pl.pallas_call(
        gather_kernel,
        out_shape=jax.ShapeDtypeStruct((4 * rows, 4 * columns), own.dtype),
        in_specs=[VMEM],
        out_specs=VMEM,
        scratch_shapes=[DMA, DMA, DMA((6,)), DMA((6,)), DMA((8,)), DMA((8,))],
        compiler_params=pltpu.CompilerParams(
            collective_id=collective, has_side_effects=True, vmem_limit_bytes=40 << 20
        ),
        cost_estimate=pl.CostEstimate(flops=0, bytes_accessed=80 << 20, transcendentals=0),
        name="gather_grid",
    )(own)


def reduce_kernel(part, total, held, out_buf, in_buf, acc, sx, rx, xs, xr, ys, yr, cs, cr):
    row, sibling, across = place()
    rows, columns = total.shape
    greet(row, sibling, across)
    pending = []
    go = starter(pending)

    def rows_of(k):
        return pl.ds(pl.multiple_of(lax.rem(row + k, 4) * rows, rows), rows)

    order = (2, 1, 3, 0)
    paired = {}
    for k in order:
        for x in (0, 1):
            paired[k, x] = go(
                part.at[rows_of(k), pl.ds((2 * x + 1) * columns, columns)],
                held.at[k, x],
                cs.at[k, x],
                cr.at[k, x],
                col=sibling,
            )
    along = {}
    for k in order:
        for x in (0, 1):
            paired[k, x].wait_recv()
            mine = part[rows_of(k), pl.ds(2 * x * columns, columns)]
            value = mine.astype(f32) + held[k, x].astype(f32)
            if k:
                out_buf[k - 1, x] = value.astype(bf16)
                along[k, x] = go(
                    out_buf.at[k - 1, x],
                    in_buf.at[k - 1, x],
                    ys.at[k - 1, x],
                    yr.at[k - 1, x],
                    row=lax.rem(row + k, 4),
                )
            else:
                acc[x] = value
    for x in (1, 0):
        for k in (1, 3, 2):
            along[k, x].wait_recv()
            acc[x] += in_buf[k - 1, x].astype(f32)
        if x:
            sx[...] = acc[1].astype(bf16)
            side = go(sx, rx, xs, xr, col=across)
    side.wait_recv()
    total[...] = acc[0] + rx[...].astype(f32)
    for copy in pending:
        copy.wait_send()


def reduce_grid(part, collective):
    rows, columns = part.shape[0] // 4, part.shape[1] // 4
    return pl.pallas_call(
        reduce_kernel,
        out_shape=jax.ShapeDtypeStruct((rows, columns), f32),
        in_specs=[VMEM],
        out_specs=VMEM,
        scratch_shapes=[
            pltpu.VMEM((4, 2, rows, columns), bf16),
            pltpu.VMEM((3, 2, rows, columns), bf16),
            pltpu.VMEM((3, 2, rows, columns), bf16),
            pltpu.VMEM((2, rows, columns), f32),
            pltpu.VMEM((rows, columns), bf16),
            pltpu.VMEM((rows, columns), bf16),
            DMA,
            DMA,
            DMA((3, 2)),
            DMA((3, 2)),
            DMA((4, 2)),
            DMA((4, 2)),
        ],
        compiler_params=pltpu.CompilerParams(
            collective_id=collective, has_side_effects=True, vmem_limit_bytes=40 << 20
        ),
        cost_estimate=pl.CostEstimate(flops=0, bytes_accessed=100 << 20, transcendentals=0),
        name="reduce_grid",
    )(part)


def dot(spec, left, right, kind=f32):
    return jnp.einsum(spec, left, right, preferred_element_type=f32).astype(kind)


def rotary_tables(length, half_width):
    position = jnp.arange(length, dtype=f32)[:, None]
    frequency = jnp.exp(jnp.arange(half_width, dtype=f32) * (-math.log(10000.0) / half_width))
    angles = position * frequency[None, :]
    return (jnp.cos(angles), jnp.sin(angles))


def rotate(values, cos_table, sin_table):
    half_width = cos_table.shape[-1]
    first_half = values[..., :half_width]
    second_half = values[..., half_width:]
    return jnp.concatenate(
        [
            first_half * cos_table - second_half * sin_table,
            second_half * cos_table + first_half * sin_table,
        ],
        axis=-1,
    )


def swap_chips(values, distance, other_replica):
    flip = 4 if other_replica else 0
    pairs = [
        (dp * 4 + col, (dp ^ flip) * 4 + (col ^ distance)) for dp in range(8) for col in range(4)
    ]
    return lax.ppermute(values, ("dp", "col"), pairs)


def deal(pieces):
    got = [pieces(0)]
    for k in (1, 2, 3):
        piece = pieces(k)
        if k == 1:
            got.append(swap_chips(piece, k, False))
        else:
            half = piece.shape[0] // 2
            got.append(
                jnp.concatenate(
                    [swap_chips(piece[:half], k, False), swap_chips(piece[half:], k, True)], axis=0
                )
            )
    return got


def pad_to(values, axis, size):
    widths = [(0, 0)] * values.ndim
    widths[axis] = (0, size - values.shape[axis])
    return jnp.pad(values, widths)


def visible_mask(offset, block_rows, prefix_len):
    query_pos = offset + jnp.arange(block_rows, dtype=jnp.int32)
    key_pos = jnp.arange(SEQ, dtype=jnp.int32)
    return (key_pos[None, :] <= query_pos[:, None]) | (key_pos[None, :] < prefix_len)


def attend_forward(queries, key_rows, value_rows, prefix_len):
    score_scale = (NOPE + ROPE) ** (-0.5)
    scores = dot("qd,kd->qk", queries, key_rows) * score_scale
    scores = jnp.where(visible_mask(0, SEQ, prefix_len), scores, masked_score)
    top_score = jnp.max(scores, axis=1, keepdims=True)
    exp_scores = jnp.exp(scores - top_score)
    row_total = jnp.sum(exp_scores, axis=1, keepdims=True)
    weights = (exp_scores / row_total).astype(bf16)
    result = dot("qk,kd->qd", weights, value_rows)
    return (result, (top_score + jnp.log(row_total))[:, 0])


def attend_backward(queries, key_rows, value_rows, log_total, out_grad, prefix_len):
    score_scale = (NOPE + ROPE) ** (-0.5)
    scores = dot("qd,kd->qk", queries, key_rows) * score_scale
    scores = jnp.where(visible_mask(0, SEQ, prefix_len), scores, masked_score)
    weights = jnp.exp(scores - log_total[:, None])
    value_grad = dot("qk,qd->kd", weights.astype(bf16), out_grad)
    weight_grad = dot("qd,kd->qk", out_grad, value_rows)
    centre = jnp.sum(weights * weight_grad, axis=1, keepdims=True)
    score_grad = (weights * (weight_grad - centre)).astype(bf16)
    query_grad = dot("qk,kd->qd", score_grad, key_rows) * score_scale
    key_grad = dot("qk,qd->kd", score_grad, queries) * score_scale
    return (query_grad, key_grad, value_grad)


def norm_back(values, gain_row, scale_row, upstream):
    weighted = upstream * gain_row[None, :]
    inner_sum = lax.psum(jnp.sum(weighted * values, axis=1), "col")
    value_grad = (
        scale_row[:, None] * weighted
        - values * (scale_row * scale_row * scale_row * inner_sum / D)[:, None]
    )
    gain_grad = jnp.sum(upstream * values * scale_row[:, None], axis=0)
    return (value_grad, gain_grad)


def sigmoid(value):
    return jax.nn.sigmoid(value)


def on_device(
    inputs,
    attention_gain,
    query_weight,
    latent_weight,
    latent_gain,
    expand_weight,
    output_weight,
    feedforward_gain,
    router_weight,
    shared_gate,
    shared_up,
    shared_down,
    expert_gate,
    expert_up,
    expert_down,
    routes,
    prefix,
    cotangent,
):
    row = lax.axis_index("row")
    col = lax.axis_index("col")
    prefix_len = prefix[0]
    cos_table, sin_table = rotary_tables(SEQ, ROPE // 2)
    first_gain = attention_gain.astype(f32)
    second_gain = feedforward_gain.astype(f32)
    compact_gain = latent_gain.astype(f32)
    residual_in = inputs.astype(f32)
    rows = inputs.shape[0]
    ff = expert_gate.shape[2]
    ff_pad = -(-ff // 128) * 128
    sff = shared_gate.shape[1] // 4
    sff_pad = 256

    gains = jnp.stack([attention_gain, feedforward_gain], axis=1)
    common = pad_to(jnp.concatenate([latent_weight[:, RANK:], router_weight, gains], axis=1), 1, 192)
    heads = query_weight.reshape(512, 4, NOPE + ROPE)

    def attention_piece(k):
        head = lax.dynamic_index_in_dim(heads, col ^ k, 1, False)
        return jnp.concatenate([latent_weight[:, :RANK], head, common], axis=1)

    attention_weights = jnp.concatenate(deal(attention_piece), axis=0)
    first_all = attention_weights[:, RANK + 256 + 8]
    second_all = attention_weights[:, RANK + 256 + 9]
    project_weight = attention_weights[:, : RANK + 256]

    gate_parts = expert_gate.reshape(4, 2, 512, ff)
    up_parts = expert_up.reshape(4, 2, 512, ff)
    down_parts = expert_down.reshape(4, 2, ff, 512)
    shared_gate_parts = shared_gate.reshape(512, 4, sff)
    shared_up_parts = shared_up.reshape(512, 4, sff)
    shared_down_parts = shared_down.reshape(4, sff, 512)

    def up_piece(k):
        gate = lax.dynamic_index_in_dim(gate_parts, col ^ k, 0, False)
        up = lax.dynamic_index_in_dim(up_parts, col ^ k, 0, False)
        return jnp.concatenate([pad_to(gate, 2, ff_pad), pad_to(up, 2, ff_pad)], axis=2)

    def down_piece(k):
        down = pad_to(lax.dynamic_index_in_dim(down_parts, col ^ k, 0, False), 1, ff_pad)
        low = pad_to(lax.dynamic_index_in_dim(shared_down_parts, col ^ k, 0, False), 0, sff_pad)
        gate = lax.dynamic_index_in_dim(shared_gate_parts, col ^ k, 1, False)
        up = lax.dynamic_index_in_dim(shared_up_parts, col ^ k, 1, False)
        both = jnp.concatenate(
            [pad_to(jnp.concatenate([gate, router_weight], axis=1), 1, sff_pad), pad_to(up, 1, sff_pad)],
            axis=1,
        )
        return jnp.concatenate([down.reshape(2 * ff_pad, 512), low, both], axis=0)

    up_weight = jnp.concatenate(deal(up_piece), axis=1)
    down_got = deal(down_piece)
    down_weight = jnp.concatenate(
        [piece[: 2 * ff_pad].reshape(2, ff_pad, 512) for piece in down_got], axis=2
    )
    shared_down_weight = jnp.concatenate(
        [piece[2 * ff_pad : 2 * ff_pad + sff_pad] for piece in down_got], axis=1
    )
    shared_up_weight = jnp.concatenate([piece[2 * ff_pad + sff_pad :] for piece in down_got], axis=0)

    input_rows = gather_grid(inputs, 0).astype(f32)
    scale_one = lax.rsqrt(jnp.mean(input_rows * input_rows, axis=1) + norm_eps)
    normed = (input_rows * scale_one[:, None] * first_all.astype(f32)[None, :]).astype(bf16)
    projected = dot("td,dq->tq", normed, project_weight)
    content = projected[:, :RANK]
    latent_scale = lax.rsqrt(jnp.mean(content * content, axis=1) + norm_eps)
    compact = (content * latent_scale[:, None] * compact_gain[None, :]).astype(bf16)
    shared_key = rotate(projected[:, RANK + 192 :], cos_table, sin_table).astype(bf16)
    key_value = dot("tr,rk->tk", compact, expand_weight, bf16)
    query_rot = jnp.concatenate(
        [
            projected[:, RANK : RANK + NOPE],
            rotate(projected[:, RANK + NOPE : RANK + 192], cos_table, sin_table),
        ],
        axis=1,
    ).astype(bf16)
    key_rows = jnp.concatenate([key_value[:, :NOPE], shared_key], axis=1)
    value_rows = key_value[:, NOPE:]
    head_result, log_total = attend_forward(query_rot, key_rows, value_rows, prefix_len)
    attended_rows = lax.all_gather(head_result.astype(bf16), "col", axis=1, tiled=True)
    residual_mid = residual_in + lax.psum_scatter(
        dot("th,hd->td", attended_rows, output_weight, bf16), "row", scatter_dimension=0, tiled=True
    ).astype(f32)

    middle_rows = gather_grid(residual_mid.astype(bf16), 0).astype(f32)
    scale_two = lax.rsqrt(jnp.mean(middle_rows * middle_rows, axis=1) + norm_eps)
    hidden = (middle_rows * scale_two[:, None] * second_all.astype(f32)[None, :]).astype(bf16)
    out_grad = gather_grid(cotangent, 0)
    named = jnp.any(
        routes[:, :, None] == jnp.arange(EXPERTS, dtype=jnp.int32)[None, None, :], axis=1
    ).astype(f32)
    shared_pre = dot("td,df->tf", hidden, shared_up_weight)
    router_probs = jax.nn.softmax(shared_pre[:, sff : sff + EXPERTS], axis=1)
    weight_all = router_probs * named
    mine = (
        2 * col + jnp.arange(2, dtype=jnp.int32)[:, None]
        == jnp.arange(EXPERTS, dtype=jnp.int32)[None, :]
    ).astype(f32)
    slot_weight = jnp.sum(weight_all[None] * mine[:, None, :], axis=2)[:, :, None]
    pre = dot("td,edf->etf", hidden, up_weight)
    gate_pre, up_pre = pre[:, :, :ff_pad], pre[:, :, ff_pad:]
    gate_sig = sigmoid(gate_pre)
    gate_silu = gate_pre * gate_sig
    act = (slot_weight * gate_silu * up_pre).astype(bf16)
    shared_gate_pre, shared_up_pre = shared_pre[:, :sff_pad], shared_pre[:, sff_pad:]
    shared_sig = sigmoid(shared_gate_pre)
    shared_silu = shared_gate_pre * shared_sig
    shared_act = (shared_silu * shared_up_pre).astype(bf16)
    combined = dot("etf,efd->td", act, down_weight) + dot(
        "tf,fd->td", shared_act, shared_down_weight
    )
    output = (residual_mid + reduce_grid(combined.astype(bf16), 1)).astype(bf16)
    act_grad = dot("td,efd->etf", out_grad, down_weight)
    shared_act_grad = dot("td,fd->tf", out_grad, shared_down_weight)
    weighted = slot_weight * act_grad
    gate_delta = weighted * up_pre * (gate_sig * (1.0 + gate_pre * (1.0 - gate_sig)))
    up_delta = weighted * gate_silu
    delta = jnp.concatenate([gate_delta, up_delta], axis=2).astype(bf16)
    probs_part = jnp.sum(act_grad * gate_silu * up_pre, axis=2)
    probs_part = jnp.sum(probs_part[:, :, None] * mine[:, None, :], axis=0) * named
    logits_part = router_probs * (
        probs_part - jnp.sum(router_probs * probs_part, axis=1, keepdims=True)
    )
    shared_gate_delta = (
        shared_act_grad
        * shared_up_pre
        * (shared_sig * (1.0 + shared_gate_pre * (1.0 - shared_sig)))
    )
    shared_delta = jnp.concatenate(
        [
            shared_gate_delta[:, :sff],
            logits_part,
            shared_gate_delta[:, sff + EXPERTS :],
            shared_act_grad * shared_silu,
        ],
        axis=1,
    ).astype(bf16)
    hidden_grad = dot("etf,edf->td", delta, up_weight) + dot(
        "tf,df->td", shared_delta, shared_up_weight
    )
    hidden_sum = reduce_grid(hidden_grad.astype(bf16), 1)
    up_grad = dot("td,etf->edf", hidden, delta, bf16)
    down_grad = dot("td,etf->edf", out_grad, act, bf16)
    expert_grad = jnp.concatenate([up_grad, down_grad], axis=2).reshape(8, 512, 3 * ff_pad)
    shared_grad = jnp.concatenate(
        [
            dot("td,tf->df", hidden, shared_delta),
            dot("td,tf->df", out_grad, shared_act),
        ],
        axis=1,
    )

    my_scale_one = lax.dynamic_slice_in_dim(scale_one, row * rows, rows, 0)
    my_scale_two = lax.dynamic_slice_in_dim(scale_two, row * rows, rows, 0)
    mid_norm_grad, second_gain_part = norm_back(residual_mid, second_gain, my_scale_two, hidden_sum)
    residual_grad = cotangent.astype(f32) + mid_norm_grad
    residual_rows = lax.all_gather(residual_grad.astype(bf16), "row", axis=0, tiled=True)
    output_weight_grad = dot("th,td->hd", attended_rows, residual_rows, bf16)
    attended_grad = lax.psum_scatter(
        dot("td,hd->th", residual_rows, output_weight, bf16),
        "col",
        scatter_dimension=1,
        tiled=True,
    )
    query_rot_grad, key_grad, value_grad = attend_backward(
        query_rot, key_rows, value_rows, log_total, attended_grad, prefix_len
    )
    pair_grad = jnp.concatenate([key_grad[:, :NOPE], value_grad], axis=1).astype(bf16)
    expand_grad = dot("tr,tk->rk", compact, pair_grad, bf16)
    compact_grad = dot("tk,rk->tr", pair_grad, expand_weight)
    weighted_compact = compact_grad * compact_gain[None, :]
    inner_sum = jnp.sum(weighted_compact * content, axis=1)
    content_grad = (
        latent_scale[:, None] * weighted_compact
        - content * (latent_scale * latent_scale * latent_scale * inner_sum / RANK)[:, None]
    )
    latent_gain_part = jnp.sum(compact_grad * content * latent_scale[:, None], axis=0)
    project_grad = jnp.concatenate(
        [
            content_grad,
            query_rot_grad[:, :NOPE],
            rotate(query_rot_grad[:, NOPE:], cos_table, -sin_table),
            rotate(key_grad[:, NOPE:], cos_table, -sin_table),
        ],
        axis=1,
    ).astype(bf16)
    latent_part = jnp.concatenate([project_grad[:, :RANK], project_grad[:, RANK + 192 :]], axis=1)
    normed_grad = dot("tq,dq->td", project_grad, project_weight, bf16)
    latent_weight_part = dot("tl,td->ld", latent_part, normed, bf16)
    tail = jnp.concatenate(
        [normed_grad.reshape(4, rows, D), latent_weight_part.reshape(4, -1, D)], axis=1
    )
    tail_rows = tail.shape[1]
    tail_sum = reduce_grid(tail.reshape(4 * tail_rows, D), 2)
    input_norm_grad, first_gain_part = norm_back(
        residual_in, first_gain, my_scale_one, tail_sum[:rows]
    )
    inputs_grad = (residual_grad + input_norm_grad).astype(bf16)
    query_rows = lax.all_gather(project_grad[:, RANK : RANK + 192], "col", axis=1, tiled=True)
    query_weight_grad = dot("td,tq->dq", normed[:, :512], query_rows, bf16)

    expert_sum = lax.psum_scatter(expert_grad, "dp", scatter_dimension=0, tiled=True)[0]
    pairs = [
        (dp * 4 + c, (2 * c + dp // 4) * 4 + (c ^ (dp % 4))) for dp in range(8) for c in range(4)
    ]
    expert_sum = lax.ppermute(expert_sum, ("dp", "col"), pairs).astype(f32)
    expert_gate_grad = expert_sum[None, :, :ff]
    expert_up_grad = expert_sum[None, :, ff_pad : ff_pad + ff]
    expert_down_grad = expert_sum[None, :, 2 * ff_pad : 2 * ff_pad + ff].transpose(0, 2, 1)

    order = col ^ jnp.arange(4, dtype=jnp.int32)
    router_part = shared_grad[:, sff : sff + EXPERTS].reshape(4, 512, EXPERTS)[order]
    small = lax.psum(
        jnp.concatenate([router_part.reshape(-1), latent_gain_part]), ("dp", "row", "col")
    )
    router_grad = lax.dynamic_index_in_dim(
        small[: D * EXPERTS].reshape(4, 512, EXPERTS), col, 0, False
    )
    latent_gain_grad = small[D * EXPERTS :]
    shared_sum = lax.psum(shared_grad.astype(bf16), "dp").reshape(4, 512, 3 * sff_pad)
    shared_got = jnp.stack(
        [shared_sum[0]] + [swap_chips(shared_sum[k], k, False) for k in (1, 2, 3)]
    )[order].astype(f32)
    shared_gate_grad = shared_got[:, :, :sff].transpose(1, 0, 2).reshape(512, 4 * sff)
    shared_up_grad = (
        shared_got[:, :, sff_pad : sff_pad + sff].transpose(1, 0, 2).reshape(512, 4 * sff)
    )
    shared_down_grad = (
        shared_got[:, :, 2 * sff_pad : 2 * sff_pad + sff].transpose(0, 2, 1).reshape(4 * sff, 512)
    )
    summed = lax.psum(
        jnp.concatenate(
            [
                query_weight_grad.reshape(-1, 512),
                expand_grad.reshape(-1, 512),
                output_weight_grad,
                tail_sum[rows:].astype(bf16),
            ],
            axis=0,
        ),
        "dp",
    )
    query_weight_grad = summed[:768].reshape(512, 768).astype(f32)
    expand_grad = summed[768:1024].reshape(512, 256).astype(f32)
    output_weight_grad = summed[1024:1536].astype(f32)
    latent_weight_grad = (
        lax.all_gather(summed[1536:], "row", axis=0, tiled=True).transpose(1, 0).astype(f32)
    )
    first_gain_grad, second_gain_grad = lax.psum((first_gain_part, second_gain_part), ("dp", "row"))
    return (
        output,
        inputs_grad,
        first_gain_grad,
        query_weight_grad,
        latent_weight_grad,
        latent_gain_grad,
        expand_grad,
        output_weight_grad,
        second_gain_grad,
        router_grad,
        shared_gate_grad,
        shared_up_grad,
        shared_down_grad,
        expert_gate_grad,
        expert_up_grad,
        expert_down_grad,
    )


def solution(mesh):
    placed = (
        P(("dp", "row"), "col"),
        P("col"),
        P("col", "row"),
        P("col", None),
        P(),
        P(None, ("row", "col")),
        P("row", "col"),
        P("col"),
        P("col", None),
        P("col", "row"),
        P("col", "row"),
        P("row", "col"),
        P(None, "col", "row"),
        P(None, "col", "row"),
        P(None, "row", "col"),
        P("dp", None),
        P("dp"),
        P(("dp", "row"), "col"),
    )
    return jax.shard_map(
        on_device,
        mesh=mesh,
        in_specs=placed,
        out_specs=(
            P(("dp", "row"), "col"),
            P(("dp", "row"), "col"),
            P("col"),
            P("col", "row"),
            P("col", None),
            P(),
            P(None, ("row", "col")),
            P("row", "col"),
            P("col"),
            P("col", None),
            P("col", "row"),
            P("col", "row"),
            P("row", "col"),
            P("dp", "col", "row"),
            P("dp", "col", "row"),
            P("dp", "row", "col"),
        ),
        check_vma=False,
    )
```

time: 1950 us -> 954 us (0.49)
  waiting for transfers between devices: 1210 us -> 283 us
  Pallas kernels: 0 us -> 244 us
  blocking collectives: 205 us -> 105 us
  other arithmetic: 146 us -> 65.9 us
  matrix products: 177 us -> 101 us
  local copies, waits for them, and re-layouts: 170 us -> 96 us
    reduce_scatter x15 -> x2, waiting for transfers between devices: 522 us -> 143 us  [the longest x1 137 us: on_device(): lax.psum_scatter(expert_grad, 'dp', scatter_dimension=0, tiled=True)[0]]
    psum x3 -> x2, waiting for transfers between devices: 379 us -> 85 us  [the longest x1 85 us: on_device(): lax.psum(shared_grad.astype(bf16), 'dp').reshape(4, 512, 3 * sff_pad)]
    all_gather x12 -> x3, waiting for transfers between devices: 304 us -> 24 us  [the longest x1 24 us: on_device(): lax.all_gather(residual_grad.astype(bf16), 'row', axis=0, tiled=True)]
    pallas_call x0 -> x6, Pallas kernels: none -> 244 us  [the longest x3 126 us: reduce_grid(): pl.pallas_call(reduce_kernel, out_shape=jax.ShapeDtypeStruct((rows, colum...]
    psum x7 -> x2, blocking collectives: 127 us -> 11.9 us  [norm_back(): inner_sum = lax.psum(jnp.sum(weighted * values, axis=1), 'col')]
    scatter-add x3 -> x0, other arithmetic: 95.6 us -> none  [the longest x1 41.6 us: on_device(): combined.at[slot_token.reshape(-1)]]
    gather x4 -> x3, local copies, waits for them, and re-layouts: 81.6 us -> 5.29 us  [the longest x1 4.4 us: on_device(): jnp.stack([shared_sum[0]] + [swap_chips(shared_sum[k], k, False) for k in...]
    dot_general x47 -> x28, matrix products: 177 us -> 101 us  [dot(): jnp.einsum(spec, left, right, preferred_element_type=f32).astype(kind)]
  transfers between devices with their start and end apart: 30 -> 27, of which waited for: 22 -> 7; matrix products, arithmetic and copies ran while one was open for 18% -> 21% of each run, Pallas kernels for 0% -> 22%
where the time goes in v1:
time: 954 us; the launch traced here: 935 us
  waiting for transfers between devices  283 us (30%)
  Pallas kernels  244 us (26%)
  blocking collectives  105 us (11%)
  matrix products  101 us (11%)
  local copies, waits for them, and re-layouts  96 us (10%)
  other arithmetic  65.9 us (7%)
  starting transfers between devices  22.3 us (2%)
  between operations  18.4 us (2%)
    reduce_scatter x1, waiting for transfers between devices, on_device(): lax.psum_scatter(expert_grad, 'dp', scatter_dimension=0, tiled=True)[0]  137 us
    pallas_call x3, Pallas kernels, reduce_grid(): pl.pallas_call(reduce_kernel, out_shape=jax.ShapeDtypeStruct((rows, colum...  126 us
    pallas_call x3, Pallas kernels, gather_grid(): pl.pallas_call(gather_kernel, out_shape=jax.ShapeDtypeStruct((4 * rows, 4...  118 us
    dot_general x28, matrix products, dot(): jnp.einsum(spec, left, right, preferred_element_type=f32).astype(kind)  101 us
    psum x1, waiting for transfers between devices, on_device(): lax.psum(shared_grad.astype(bf16), 'dp').reshape(4, 512, 3 * sff_pad)  85 us
    psum x1, blocking collectives, on_device(): lax.psum((first_gain_part, second_gain_part), ('dp', 'row'))  80.7 us
    ppermute x18, waiting for transfers between devices, swap_chips(): return lax.ppermute(values, ('dp', 'col'), pairs)  25.6 us
    all_gather x1, waiting for transfers between devices, on_device(): lax.all_gather(residual_grad.astype(bf16), 'row', axis=0, tiled=True)  24 us
  transfers between devices with their start and end apart: 27, of which 7 were waited for; matrix products, arithmetic and copies ran while one was open for 21% of the time, Pallas kernels for 22%

profile of v1, /device:TPU:5, one launch (start us, length us, event | category | flops | bytes accessed | tf_op | source)
XLA Modules:
  0.0 935.3 jit_solution(8289701453383252097)
XLA Ops:
  20.7 39.3 %gather_grid.3 = bf16[1024,2048]{1,0:T(8,128)(2,1)S(1)} custom-call(bf16[256,512]{1,0:T(8,128)(2,1)S(1)} %copy-done.6), custom_call_target="tpu_custom_call" | custom-call | bytes 83886080 | tf_op jit(solution)/shard_map/gather_grid/pallas_call | solution.py:111
  82.3 4.9 fusion.79
  118.6 11.0 %collective-permute-done.7 = bf16[768,512]{1,0:T(8,128)(2,1)} collective-permute-done((bf16[768,512]{1,0:T(8,128)(2,1)}, bf16[768,512]{1,0:T(8,128)(2,1)}, u32[]{:S(2)}, u32[]{:S(2)}) %collective-permute-start.7) | collective-permute-done | bytes 786464 | tf_op jit(solution)/shard_map/ppermute | solution.py:234
  131.0 14.5 %collective-permute-done.6 = bf16[768,512]{1,0:T(8,128)(2,1)S(1)} collective-permute-done((bf16[768,512]{1,0:T(8,128)(2,1)S(1)}, bf16[768,512]{1,0:T(8,128)(2,1)S(1)}, u32[]{:S(2)}, u32[]{:S(2)}) %collective-permute-start.6) | collective-permute-done | bytes 786464 | tf_op jit(solution)/shard_map/ppermute | solution.py:234
  149.2 36.9 %gather_grid.5 = bf16[1024,2048]{1,0:T(8,128)(2,1)S(1)} custom-call(bf16[256,512]{1,0:T(8,128)(2,1)S(1)} %copy-done.11), custom_call_target="tpu_custom_call" | custom-call | bytes 83886080 | tf_op jit(solution)/shard_map/gather_grid/pallas_call | solution.py:111
  204.9 7.1 fusion.17
  211.9 5.3 reduce-scatter.6.cloned.1.call-done
  218.3 42.1 %gather_grid.4 = bf16[1024,2048]{1,0:T(8,128)(2,1)S(1)} custom-call(bf16[256,512]{1,0:T(8,128)(2,1)S(1)} %fusion.121.own), custom_call_target="tpu_custom_call" | custom-call | bytes 83886080 | tf_op jit(solution)/shard_map/gather_grid/pallas_call | solution.py:111
  261.4 6.8 fusion.64
  274.2 5.2 fusion.52
  284.3 9.1 fusion.77
  293.4 8.3 fusion.12.part
  301.7 36.3 %reduce_grid.4 = f32[256,512]{1,0:T(8,128)S(1)} custom-call(bf16[1024,2048]{1,0:T(8,128)(2,1)S(1)} %fusion.12.part), custom_call_target="tpu_custom_call" | custom-call | bytes 104857600 | tf_op jit(solution)/shard_map/reduce_grid/pallas_call | solution.py:178
  338.9 5.9 psum.49
  345.9 24.0 %all-gather.6.cloned.1.call-done = bf16[1024,512]{1,0:T(8,128)(2,1)} async-done(((bf16[256,512]{1,0:T(8,128)(2,1)}), bf16[1024,512]{1,0:T(8,128)(2,1)}) %all-gather.6.cloned.1.call-update) | async-done | bytes 1048592 | tf_op jit(solution)/shard_map/all_gather | solution.py:482
  373.5 6.3 fusion.182
  389.5 5.3 reduce-scatter.10.cloned.1.call-done
  409.6 6.9 convolution_convert_fusion.1
  416.6 5.1 convolution_convert_fusion
  425.3 53.0 %reduce_grid.5 = f32[400,512]{1,0:T(8,128)S(1)} custom-call(bf16[1600,2048]{1,0:T(8,128)(2,1)S(1)} %bitcast.175), custom_call_target="tpu_custom_call" | custom-call | bytes 104857600 | tf_op jit(solution)/shard_map/reduce_grid/pallas_call | solution.py:178
  487.8 6.0 fusion.58
  493.8 8.7 convert_bitcast_fusion
  502.5 8.5 pad_maximum_fusion
  510.9 12.7 %copy.143 = bf16[2,2048,1152]{2,1,0:T(8,128)(2,1)} copy(bf16[2,2048,1152]{1,2,0:T(8,128)(2,1)} %pad_maximum_fusion) | data formatting | bytes 18874368 | tf_op jit(solution)/shard_map/concatenate | solution.py:469
  524.5 5.6 fusion.166
  531.5 36.4 %reduce_grid.3 = f32[256,512]{1,0:T(8,128)S(1)} custom-call(bf16[1024,2048]{1,0:T(8,128)(2,1)S(1)} %fusion.13.part), custom_call_target="tpu_custom_call" | custom-call | bytes 104857600 | tf_op jit(solution)/shard_map/reduce_grid/pallas_call | solution.py:178
  568.1 5.9 psum.50
  574.0 80.7 %all-reduce.25 = (f32[512]{0:T(512)}, f32[512]{0:T(512)}) all-reduce(f32[512]{0:T(512)S(1)} %get-tuple-element.82, f32[512]{0:T(512)S(1)} %copy-done.117), channel_id=1, replica_groups=mesh['dp'=8,'row'=4,'col'=4] {'dp','row'}, use_global_device_ids=true, to_apply=%region_21.22 | all-reduce | flops 1024 | bytes 8192 | tf_op jit(solution)/shard_map/psum | solution.py:574
  659.4 85.0 %all-reduce.32.cloned.1.call-done = (bf16[2048,768]{0,1:T(8,128)(2,1)}, bf16[1680,512]{1,0:T(8,128)(2,1)}) async-done(((bf16[2048,768]{0,1:T(8,128)(2,1)}, bf16[1680,512]{1,0:T(8,128)(2,1)}), (bf16[2048,768]{0,1:T(8,128)(2,1)}, bf16[1680,512]{1,0:T(8,128)(2,1)})) %all-reduce.32.cloned.1.call-update) | async-done | bytes 4866064 | tf_op jit(solution)/shard_map/psum | solution.py:545
  751.8 137.3 %reduce-scatter.8.cloned.1.call-done = bf16[1,512,1152]{2,1,0:T(8,128)(2,1)} async-done(((bf16[8,512,1152]{2,1,0:T(8,128)(2,1)}), bf16[1,512,1152]{2,1,0:T(8,128)(2,1)}) %reduce-scatter.8.cloned.1.call-update) | async-done | bytes 1179664 | tf_op jit(solution)/shard_map/reduce_scatter | solution.py:527
  889.1 4.8 collective-permute-start.18
  893.9 12.3 %all_gather.15 = bf16[576,512]{1,0:T(8,128)(2,1)S(1)} all-gather(bf16[144,512]{1,0:T(8,128)(2,1)} %slice.326), channel_id=1, replica_groups=mesh['dp'=8,'row'=4,'col'=4] {'row'}, dimensions={0}, use_global_device_ids=true | all-gather | bytes 737280 | tf_op jit(solution)/shard_map/all_gather | solution.py:572
  (461 shorter events, 179.7 us)
Async XLA Ops:
  7.2 184.3 %copy-start = (bf16[512,512]{1,0:T(8,128)(2,1)S(1)}, bf16[512,512]{1,0:T(8,128)(2,1)}, u32[]{:S(2)}) copy-start(bf16[512,512]{1,0:T(8,128)(2,1)} %param.24) | copy-start | bytes 1572868
  7.2 184.3 %all-gather.4.cloned.1.call-start = ((), (), s32[]{:S(2)}) async-start(), calls=%async_computation.3 | async-start | bytes 1310720 | tf_op jit(solution)/shard_map/all_gather | solution.py:405
  13.4 75.1 %collective-permute-start = (bf16[512,896]{0,1:T(8,128)(2,1)}, bf16[512,896]{0,1:T(8,128)(2,1)}, u32[]{:S(2)}, u32[]{:S(2)}) collective-permute-start(bf16[512,896]{0,1:T(8,128)(2,1)} %get-tuple-element.163), channel_id=1, source_target_pairs={{0,1},{1,0},{2,3},{3,2},{16,17},{17,16},{18,19},{19,18},{32,33},{3... | collective-permute-start | bytes 2752520 | tf_op jit(solution)/shard_map/ppermute | solution.py:234
  15.1 75.1 %collective-permute-start.1 = (bf16[256,896]{0,1:T(8,128)(2,1)}, bf16[256,896]{0,1:T(8,128)(2,1)}, u32[]{:S(2)}, u32[]{:S(2)}) collective-permute-start(bf16[256,896]{0,1:T(8,128)(2,1)} %get-tuple-element.145), channel_id=1, source_target_pairs={{0,2},{1,3},{2,0},{3,1},{16,18},{17,19},{18,16},{19,17},{32,34},{3... | collective-permute-start | bytes 1376264 | tf_op jit(solution)/shard_map/ppermute | solution.py:234
  16.0 76.0 %collective-permute-start.2 = (bf16[256,896]{0,1:T(8,128)(2,1)}, bf16[256,896]{0,1:T(8,128)(2,1)}, u32[]{:S(2)}, u32[]{:S(2)}) collective-permute-start(bf16[256,896]{0,1:T(8,128)(2,1)} %get-tuple-element.144), channel_id=1, source_target_pairs={{0,66},{1,67},{2,64},{3,65},{16,82},{17,83},{18,80},{19,81},{32,98... | collective-permute-start | bytes 1376264 | tf_op jit(solution)/shard_map/ppermute | solution.py:234
  17.0 76.1 %collective-permute-start.3 = (bf16[256,896]{0,1:T(8,128)(2,1)}, bf16[256,896]{0,1:T(8,128)(2,1)}, u32[]{:S(2)}, u32[]{:S(2)}) collective-permute-start(bf16[256,896]{0,1:T(8,128)(2,1)} %get-tuple-element.143), channel_id=1, source_target_pairs={{0,3},{1,2},{2,1},{3,0},{16,19},{17,18},{18,17},{19,16},{32,35},{3... | collective-permute-start | bytes 1376264 | tf_op jit(solution)/shard_map/ppermute | solution.py:234
  18.8 75.4 %collective-permute-start.4 = (bf16[256,896]{0,1:T(8,128)(2,1)}, bf16[256,896]{0,1:T(8,128)(2,1)}, u32[]{:S(2)}, u32[]{:S(2)}) collective-permute-start(bf16[256,896]{0,1:T(8,128)(2,1)} %get-tuple-element.142), channel_id=1, source_target_pairs={{0,67},{1,66},{2,65},{3,64},{16,83},{17,82},{18,81},{19,80},{32,99... | collective-permute-start | bytes 1376264 | tf_op jit(solution)/shard_map/ppermute | solution.py:234
  88.5 116.3 %collective-permute-start.8 = (bf16[2,512,768]{1,2,0:T(8,128)(2,1)}, bf16[2,512,768]{1,2,0:T(8,128)(2,1)}, u32[]{:S(2)}, u32[]{:S(2)}) collective-permute-start(bf16[2,512,768]{1,2,0:T(8,128)(2,1)} %fusion.81), channel_id=1, source_target_pairs={{0,1},{1,0},{2,3},{3,2},{16,17},{17,16},{18,19},{19,18},{32,33},{3... | collective-permute-start | bytes 4718600 | tf_op jit(solution)/shard_map/ppermute | solution.py:234
  90.2 56.5 %collective-permute-start.5 = (bf16[1536,512]{1,0:T(8,128)(2,1)}, bf16[1536,512]{1,0:T(8,128)(2,1)}, u32[]{:S(2)}, u32[]{:S(2)}) collective-permute-start(bf16[1536,512]{1,0:T(8,128)(2,1)} %fusion.79), channel_id=1, source_target_pairs={{0,1},{1,0},{2,3},{3,2},{16,17},{17,16},{18,19},{19,18},{32,33},{3... | collective-permute-start | bytes 4718600 | tf_op jit(solution)/shard_map/ppermute | solution.py:234
  107.4 109.9 %reduce-scatter.6.cloned.1.call-start = ((), (), s32[]{:S(2)}) async-start(), calls=%async_computation.4 | async-start | bytes 1310720 | tf_op jit(solution)/shard_map/reduce_scatter | solution.py:406
  109.5 20.1 %collective-permute-start.7 = (bf16[768,512]{1,0:T(8,128)(2,1)}, bf16[768,512]{1,0:T(8,128)(2,1)}, u32[]{:S(2)}, u32[]{:S(2)}) collective-permute-start(bf16[768,512]{1,0:T(8,128)(2,1)} %fusion.114), channel_id=1, source_target_pairs={{0,67},{1,66},{2,65},{3,64},{16,83},{17,82},{18,81},{19,80},{32,99... | collective-permute-start | bytes 2359304 | tf_op jit(solution)/shard_map/ppermute | solution.py:234
  112.6 33.0 %collective-permute-start.6 = (bf16[768,512]{1,0:T(8,128)(2,1)S(1)}, bf16[768,512]{1,0:T(8,128)(2,1)S(1)}, u32[]{:S(2)}, u32[]{:S(2)}) collective-permute-start(bf16[768,512]{1,0:T(8,128)(2,1)S(1)} %fusion.112), channel_id=1, source_target_pairs={{0,66},{1,67},{2,64},{3,65},{16,82},{17,83},{18,80},{19,81},{32,98... | collective-permute-start | bytes 2359304 | tf_op jit(solution)/shard_map/ppermute | solution.py:234
  116.3 86.6 %collective-permute-start.12 = (bf16[1,512,768]{1,2,0:T(8,128)(2,1)}, bf16[1,512,768]{1,2,0:T(8,128)(2,1)}, u32[]{:S(2)}, u32[]{:S(2)}) collective-permute-start(bf16[1,512,768]{1,2,0:T(8,128)(2,1)} %get-tuple-element.141), channel_id=1, source_target_pairs={{0,67},{1,66},{2,65},{3,64},{16,83},{17,82},{18,81},{19,80},{32,99... | collective-permute-start | bytes 2359304 | tf_op jit(solution)/shard_map/ppermute | solution.py:234
  129.6 74.5 %collective-permute-start.11 = (bf16[1,512,768]{1,2,0:T(8,128)(2,1)}, bf16[1,512,768]{1,2,0:T(8,128)(2,1)}, u32[]{:S(2)}, u32[]{:S(2)}) collective-permute-start(bf16[1,512,768]{1,2,0:T(8,128)(2,1)} %get-tuple-element.140), channel_id=1, source_target_pairs={{0,3},{1,2},{2,1},{3,0},{16,19},{17,18},{18,17},{19,16},{32,35},{3... | collective-permute-start | bytes 2359304 | tf_op jit(solution)/shard_map/ppermute | solution.py:234
  146.4 58.4 %collective-permute-start.10 = (bf16[1,512,768]{1,2,0:T(8,128)(2,1)}, bf16[1,512,768]{1,2,0:T(8,128)(2,1)}, u32[]{:S(2)}, u32[]{:S(2)}) collective-permute-start(bf16[1,512,768]{1,2,0:T(8,128)(2,1)} %get-tuple-element.139), channel_id=1, source_target_pairs={{0,66},{1,67},{2,64},{3,65},{16,82},{17,83},{18,80},{19,81},{32,98... | collective-permute-start | bytes 2359304 | tf_op jit(solution)/shard_map/ppermute | solution.py:234
  146.7 58.1 %collective-permute-start.9 = (bf16[1,512,768]{1,2,0:T(8,128)(2,1)}, bf16[1,512,768]{1,2,0:T(8,128)(2,1)}, u32[]{:S(2)}, u32[]{:S(2)}) collective-permute-start(bf16[1,512,768]{1,2,0:T(8,128)(2,1)} %get-tuple-element.138), channel_id=1, source_target_pairs={{0,2},{1,3},{2,0},{3,1},{16,18},{17,19},{18,16},{19,17},{32,34},{3... | collective-permute-start | bytes 2359304 | tf_op jit(solution)/shard_map/ppermute | solution.py:234
  194.4 175.4 %all-gather.6.cloned.1.call-start = ((), (), s32[]{:S(2)}) async-start(), calls=%async_computation.5 | async-start | bytes 1310720 | tf_op jit(solution)/shard_map/all_gather | solution.py:482
  202.9 71.3 %collective-permute-start.14 = (bf16[768,512]{1,0:T(8,128)(2,1)}, bf16[768,512]{1,0:T(8,128)(2,1)}, u32[]{:S(2)}, u32[]{:S(2)}) collective-permute-start(bf16[768,512]{1,0:T(8,128)(2,1)} %bitcast.43), channel_id=1, source_target_pairs={{0,3},{1,2},{2,1},{3,0},{16,19},{17,18},{18,17},{19,16},{32,35},{3... | collective-permute-start | bytes 2359304 | tf_op jit(solution)/shard_map/ppermute | solution.py:234
  204.2 70.0 %collective-permute-start.13 = (bf16[768,512]{1,0:T(8,128)(2,1)}, bf16[768,512]{1,0:T(8,128)(2,1)}, u32[]{:S(2)}, u32[]{:S(2)}) collective-permute-start(bf16[768,512]{1,0:T(8,128)(2,1)} %bitcast.40), channel_id=1, source_target_pairs={{0,2},{1,3},{2,0},{3,1},{16,18},{17,19},{18,16},{19,17},{32,34},{3... | collective-permute-start | bytes 2359304 | tf_op jit(solution)/shard_map/ppermute | solution.py:234
  345.8 49.0 %reduce-scatter.10.cloned.1.call-start = ((), (), s32[]{:S(2)}) async-start(), calls=%async_computation.9 | async-start | bytes 1310720
  373.1 107.6 %all-gather.8.cloned.1.call-start = ((), (), s32[]{:S(2)}) async-start(), calls=%async_computation.6 | async-start | bytes 1966080 | tf_op jit(solution)/shard_map/all_gather | solution.py:524
  409.2 246.8 %all-reduce.30.cloned.1.call-start = ((), (), s32[]{:S(2)}) async-start(), calls=%async_computation.7 | async-start | bytes 139264 | tf_op jit(solution)/shard_map/psum | solution.py:538
  480.6 263.7 %all-reduce.32.cloned.1.call-start = ((), (), s32[]{:S(2)}) async-start(), calls=%async_computation.10 | async-start | bytes 9732096 | tf_op jit(solution)/shard_map/psum | solution.py:545
  486.3 402.7 %reduce-scatter.8.cloned.1.call-start = ((), (), s32[]{:S(2)}) async-start(), calls=%async_computation.8 | async-start | bytes 10616832 | tf_op jit(solution)/shard_map/reduce_scatter | solution.py:527
  531.4 123.3 %copy-start.20 = (bf16[256,512]{1,0:T(8,128)(2,1)S(1)}, bf16[256,512]{1,0:T(8,128)(2,1)}, u32[]{:S(2)}) copy-start(bf16[256,512]{1,0:T(8,128)(2,1)} %reduce-scatter.6.cloned.1.call-done) | copy-start | bytes 786436
  531.4 123.3 %copy-start.99 = (f32[512]{0:T(512)S(1)}, f32[512]{0:T(512)}, u32[]{:S(2)}) copy-start(f32[512]{0:T(512)} %convert_element_type.223) | copy-start | bytes 6148
  531.5 123.3 %copy-start.103 = (f32[256]{0:T(256)S(1)}, f32[256]{0:T(256)}, u32[]{:S(2)}) copy-start(f32[256]{0:T(256)} %copy-done.102) | copy-start | bytes 3076
  531.5 123.3 %copy-start.112 = (f32[256]{0:T(256)S(1)}, f32[256]{0:T(256)}, u32[]{:S(2)}) copy-start(f32[256]{0:T(256)} %copy-done.111) | copy-start | bytes 3076
  747.8 164.1 %collective-permute-start.17 = (bf16[512,768]{0,1:T(8,128)(2,1)}, bf16[512,768]{0,1:T(8,128)(2,1)}, u32[]{:S(2)}, u32[]{:S(2)}) collective-permute-start(bf16[512,768]{0,1:T(8,128)(2,1)} %get-tuple-element.117), channel_id=1, source_target_pairs={{0,3},{1,2},{2,1},{3,0},{16,19},{17,18},{18,17},{19,16},{32,35},{3... | collective-permute-start | bytes 2359304 | tf_op jit(solution)/shard_map/ppermute | solution.py:234
  750.4 161.5 %collective-permute-start.16 = (bf16[512,768]{0,1:T(8,128)(2,1)}, bf16[512,768]{0,1:T(8,128)(2,1)}, u32[]{:S(2)}, u32[]{:S(2)}) collective-permute-start(bf16[512,768]{0,1:T(8,128)(2,1)} %get-tuple-element.118), channel_id=1, source_target_pairs={{0,2},{1,3},{2,0},{3,1},{16,18},{17,19},{18,16},{19,17},{32,34},{3... | collective-permute-start | bytes 2359304 | tf_op jit(solution)/shard_map/ppermute | solution.py:234
  750.4 161.5 %collective-permute-start.15 = (bf16[512,768]{0,1:T(8,128)(2,1)}, bf16[512,768]{0,1:T(8,128)(2,1)}, u32[]{:S(2)}, u32[]{:S(2)}) collective-permute-start(bf16[512,768]{0,1:T(8,128)(2,1)} %get-tuple-element.119), channel_id=1, source_target_pairs={{0,1},{1,0},{2,3},{3,2},{16,17},{17,16},{18,19},{19,18},{32,33},{3... | collective-permute-start | bytes 2359304 | tf_op jit(solution)/shard_map/ppermute | solution.py:234
  889.1 34.2 %collective-permute-start.18 = (bf16[512,1152]{1,0:T(8,128)(2,1)}, bf16[512,1152]{1,0:T(8,128)(2,1)}, u32[]{:S(2)}, u32[]{:S(2)}) collective-permute-start(bf16[512,1152]{1,0:T(8,128)(2,1)} %bitcast.209), channel_id=1, source_target_pairs={{0,0},{1,33},{2,66},{3,99},{16,1},{17,32},{18,67},{19,98},{32,2},{... | collective-permute-start | bytes 3538952 | tf_op jit(solution)/shard_map/ppermute | solution.py:531
  (125 other events, 1532.0 us)
Sparse Core Ops, SparseCore 0:
  107.5 21.6 all-gather.3
  194.6 22.6 reduce-scatter.5
  345.9 23.8 all-gather.5
  373.3 21.4 reduce-scatter.9
  409.3 26.0 all-gather.7
  480.8 144.3 all-reduce.29
  628.0 116.3 all-reduce.31
  748.7 140.3 reduce-scatter.7

commit v2 on v1

v2 whole, which is shorter than its diff:
```python
import functools
import math

import jax
import jax.numpy as jnp
from jax import lax
from jax.experimental import pallas as pl
from jax.experimental.pallas import tpu as pltpu
from jax.sharding import PartitionSpec as P

D = 2048
NOPE = 128
ROPE = 64
VDIM = 128
RANK = 512
TOPK = 6
EXPERTS = 8
SEQ = 1024

norm_eps = 1e-06
masked_score = -1e30
bf16 = jnp.bfloat16
f32 = jnp.float32
MESH = pl.DeviceIdType.MESH
DMA = pltpu.SemaphoreType.DMA
VMEM = pl.BlockSpec(memory_space=pltpu.VMEM)


def place():
    row = lax.axis_index("row")
    col = lax.axis_index("col")
    sibling = col + 1 - 2 * lax.rem(col, 2)
    across = lax.rem(col + 2, 4)
    return (row, sibling, across, lax.rem(sibling + 2, 4))


def greet(columns, row, over_dp=False):
    barrier = pltpu.get_barrier_semaphore()
    count = 3 + len(columns)
    for column in columns:
        pl.semaphore_signal(barrier, inc=1, device_id={"col": column}, device_id_type=MESH)
    for step in (1, 2, 3):
        pl.semaphore_signal(
            barrier, inc=1, device_id={"row": lax.rem(row + step, 4)}, device_id_type=MESH
        )
    if over_dp:
        dp = lax.axis_index("dp")
        count += 7
        for step in range(1, 8):
            pl.semaphore_signal(
                barrier, inc=1, device_id={"dp": lax.rem(dp + step, 8)}, device_id_type=MESH
            )
    pl.semaphore_wait(barrier, count)


def starter(pending):
    def go(source, target, sems, at, **device):
        copy = pltpu.make_async_remote_copy(
            src_ref=source,
            dst_ref=target,
            send_sem=sems[0].at[at],
            recv_sem=sems[1].at[at],
            device_id=device,
            device_id_type=MESH,
        )
        copy.start()
        pending.append(copy)
        return copy

    return go


def pair(*shape):
    return [DMA(shape), DMA(shape)]


def params(collective):
    return pltpu.CompilerParams(
        collective_id=collective, has_side_effects=True, vmem_limit_bytes=52 << 20
    )


def cost(flops, mebibytes):
    return pl.CostEstimate(flops=flops, bytes_accessed=mebibytes << 20, transcendentals=0)


def gather_steps(own, full, go, xs, ys, cs, row, sibling, across):
    rows, columns = own.shape

    def block(at_row, at_col):
        start = pl.multiple_of(at_row * rows, rows)
        return full.at[pl.ds(start, rows), pl.ds(at_col * columns, columns)]

    side = go(own, block(row, 2), xs, 0, col=across)
    first = [go(own, block(row, 0), ys, k - 1, row=lax.rem(row + k, 4)) for k in (1, 2, 3)]
    arrivals = [go(own, block(row, 1), cs, 0, col=sibling)]
    full[pl.ds(pl.multiple_of(row * rows, rows), rows), pl.ds(0, columns)] = own[...]
    side.wait_recv()
    second = [
        go(block(row, 2), block(row, 2), ys, 2 + k, row=lax.rem(row + k, 4)) for k in (1, 2, 3)
    ]
    arrivals.append(go(block(row, 2), block(row, 3), cs, 1, col=sibling))
    count = 2
    for group, at_col in ((first, 0), (second, 2)):
        for k in (1, 3, 2):
            group[k - 1].wait_recv()
            source = lax.rem(row + 4 - k, 4)
            arrivals.append(
                go(block(source, at_col), block(source, at_col + 1), cs, count, col=sibling)
            )
            count += 1
    for copy in arrivals:
        copy.wait_recv()


gather_scratch = pair(1) + pair(6) + pair(8)


def gather_kernel(own, full, *sems):
    row, sibling, across, corner = place()
    greet((sibling, across), row)
    pending = []
    gather_steps(
        own, full, starter(pending), sems[0:2], sems[2:4], sems[4:6], row, sibling, across
    )
    for copy in pending:
        copy.wait_send()


def gather_grid(own, collective):
    rows, columns = own.shape
    return pl.pallas_call(
        gather_kernel,
        out_shape=jax.ShapeDtypeStruct((4 * rows, 4 * columns), own.dtype),
        in_specs=[VMEM],
        out_specs=VMEM,
        scratch_shapes=gather_scratch,
        compiler_params=params(collective),
        cost_estimate=cost(0, 80),
        name="gather_grid",
    )(own)


def reduce_scratch(rows, columns):
    return [
        pltpu.VMEM((4, 2, rows, columns), bf16),
        pltpu.VMEM((3, 2, rows, columns), bf16),
        pltpu.VMEM((3, 2, rows, columns), bf16),
        pltpu.VMEM((2, rows, columns), f32),
        pltpu.VMEM((2, rows, columns), bf16),
        *pair(1),
        *pair(3, 2),
        *pair(4, 2),
    ]


class Reduction:
    order = (2, 1, 3, 0)

    def __init__(self, part, scratch, go, row, sibling, across):
        self.part, self.go = part, go
        self.held, self.out_buf, self.in_buf, self.acc, self.side_buf = scratch[:5]
        self.xs, self.ys, self.cs = scratch[5:7], scratch[7:9], scratch[9:11]
        self.row, self.sibling, self.across = row, sibling, across
        self.rows, self.columns = self.acc.shape[1:]

    def rows_of(self, k):
        start = lax.rem(self.row + k, 4) * self.rows
        return pl.ds(pl.multiple_of(start, self.rows), self.rows)

    def start(self):
        self.paired = {}
        for k in self.order:
            for x in (0, 1):
                self.paired[k, x] = self.go(
                    self.part.at[self.rows_of(k), pl.ds((2 * x + 1) * self.columns, self.columns)],
                    self.held.at[k, x],
                    self.cs,
                    (k, x),
                    col=self.sibling,
                )

    def along(self):
        self.sent = {}
        for k in self.order:
            for x in (0, 1):
                self.paired[k, x].wait_recv()
                mine = self.part[self.rows_of(k), pl.ds(2 * x * self.columns, self.columns)]
                value = mine.astype(f32) + self.held[k, x].astype(f32)
                if k:
                    self.out_buf[k - 1, x] = value.astype(bf16)
                    self.sent[k, x] = self.go(
                        self.out_buf.at[k - 1, x],
                        self.in_buf.at[k - 1, x],
                        self.ys,
                        (k - 1, x),
                        row=lax.rem(self.row + k, 4),
                    )
                else:
                    self.acc[x] = value

    def side(self):
        for x in (1, 0):
            for k in (1, 3, 2):
                self.sent[k, x].wait_recv()
                self.acc[x] += self.in_buf[k - 1, x].astype(f32)
            if x:
                self.side_buf[0] = self.acc[1].astype(bf16)
                self.last = self.go(
                    self.side_buf.at[0], self.side_buf.at[1], self.xs, 0, col=self.across
                )

    def total(self):
        self.last.wait_recv()
        return self.acc[0] + self.side_buf[1].astype(f32)


def reduce_kernel(part, total, *scratch):
    row, sibling, across, corner = place()
    greet((sibling, across), row)
    pending = []
    steps = Reduction(part, scratch, starter(pending), row, sibling, across)
    steps.start()
    steps.along()
    steps.side()
    total[...] = steps.total()
    for copy in pending:
        copy.wait_send()


def reduce_grid(part, collective):
    rows, columns = part.shape[0] // 4, part.shape[1] // 4
    return pl.pallas_call(
        reduce_kernel,
        out_shape=jax.ShapeDtypeStruct((rows, columns), f32),
        in_specs=[VMEM],
        out_specs=VMEM,
        scratch_shapes=reduce_scratch(rows, columns),
        compiler_params=params(collective),
        cost_estimate=cost(0, 100),
        name="reduce_grid",
    )(part)


class ColumnSum:
    def __init__(self, value, buf, sems, go, peers):
        self.buf, self.own = buf, value
        buf[0] = jnp.broadcast_to(value, buf.shape[1:])
        self.sent = [
            go(buf.at[0], buf.at[k + 1], sems, k, col=peer) for k, peer in enumerate(peers)
        ]

    def total(self):
        for copy in self.sent:
            copy.wait_recv()
        buf = self.buf
        return ((buf[0] + buf[1]) + (buf[2] + buf[3]))[:, :1]


def middle_kernel(
    part, middle, cotangent, scale, gain, weight,
    residual_grad, residual_rows, attended_grad, gain_part,
    sum_buf, out_buf, in_buf, acc, ss, sr, rs, rr, hs, hr, *scratch,
):
    row, sibling, across, corner = place()
    peers = (sibling, across, corner)
    greet(peers, row)
    pending = []
    go = starter(pending)
    steps = Reduction(part, scratch, go, row, sibling, across)
    rows, columns = middle.shape
    head = attended_grad.shape[1]
    steps.start()
    steps.along()
    steps.side()
    upstream = steps.total()
    weighted = upstream * gain[...]
    values = middle[...]
    scales = scale[...]
    inner = ColumnSum(
        jnp.sum(weighted * values, axis=1, keepdims=True), sum_buf, (ss, sr), go, peers
    )
    gain_part[...] = jnp.sum(upstream * values * scales, axis=0, keepdims=True)
    base = cotangent[...].astype(f32) + scales * weighted
    grad = base - values * (scales * scales * scales * inner.total() / D)
    residual_grad[...] = grad

    def block(at_row):
        return pl.ds(pl.multiple_of(at_row * rows, rows), rows)

    residual_rows[block(row), :] = grad.astype(bf16)
    sent = [
        go(
            residual_rows.at[block(row)],
            residual_rows.at[block(row)],
            (rs, rr),
            k - 1,
            row=lax.rem(row + k, 4),
        )
        for k in (1, 2, 3)
    ]
    got = []
    for k in (0, 1, 3, 2):
        source = lax.rem(row + 4 - k, 4)
        if k:
            sent[k - 1].wait_recv()
        product = lax.dot_general(
            residual_rows[block(source), :],
            weight[...],
            (((1,), (1,)), ((), ())),
            preferred_element_type=f32,
        )
        acc[block(source), :] = product[:, :head]
        for j, peer in enumerate(peers):
            out_buf[j, block(source), :] = product[:, (j + 1) * head : (j + 2) * head].astype(bf16)
            got.append(
                (
                    source,
                    j,
                    go(
                        out_buf.at[j, block(source)],
                        in_buf.at[j, block(source)],
                        (hs, hr),
                        (j, k),
                        col=peer,
                    ),
                )
            )
    for source, j, copy in got:
        copy.wait_recv()
    attended_grad[...] = (
        acc[...] + in_buf[0].astype(f32) + in_buf[1].astype(f32) + in_buf[2].astype(f32)
    ).astype(bf16)
    for copy in pending:
        copy.wait_send()


def middle_step(part, middle, cotangent, scale, gain, weight):
    rows, columns = middle.shape
    return pl.pallas_call(
        middle_kernel,
        out_shape=(
            jax.ShapeDtypeStruct((rows, columns), f32),
            jax.ShapeDtypeStruct((4 * rows, columns), bf16),
            jax.ShapeDtypeStruct((4 * rows, VDIM), bf16),
            jax.ShapeDtypeStruct((1, columns), f32),
        ),
        in_specs=[VMEM] * 6,
        out_specs=(VMEM,) * 4,
        scratch_shapes=[
            pltpu.VMEM((4, rows, 128), f32),
            pltpu.VMEM((3, 4 * rows, VDIM), bf16),
            pltpu.VMEM((3, 4 * rows, VDIM), bf16),
            pltpu.VMEM((4 * rows, VDIM), f32),
            *pair(3),
            *pair(3),
            *pair(3, 4),
            *reduce_scratch(rows, columns),
        ],
        compiler_params=params(3),
        cost_estimate=cost(1 << 29, 150),
        name="middle_step",
    )(part, middle, cotangent, scale, gain, weight)


def tail_kernel(
    part, query, ready, residual_grad, inputs, scale, gain, gain_part,
    inputs_grad, sums, narrow, gains, latent_gain,
    chunk_in, all_parts, narrow_all, lat_buf, sum_buf,
    qs, qr, ps, pr, as_, ar, ls, lr, ns, nr, ss, sr, gs, gr, *scratch,
):
    row, sibling, across, corner = place()
    col = lax.axis_index("col")
    dp = lax.axis_index("dp")
    peers = (sibling, across, corner)
    greet(peers, row, over_dp=True)
    pending = []
    go = starter(pending)
    steps = Reduction(part, scratch, go, row, sibling, across)
    rows, columns = inputs.shape
    piece = query.shape[0]
    lat = narrow_all.shape[1]

    def chunk(at):
        return pl.ds(pl.multiple_of(at * piece, piece), piece)

    steps.start()
    dealt = [
        go(
            query.at[:, pl.ds((j + 1) * columns, columns)],
            all_parts.at[chunk(4 + col)],
            (qs, qr),
            j,
            col=peer,
        )
        for j, peer in enumerate(peers)
    ]
    all_parts[pl.ds(0, 4 * piece), :] = ready[...]
    all_parts[chunk(4 + col), :] = query[:, pl.ds(0, columns)]
    steps.along()
    for copy in dealt:
        copy.wait_recv()
    scattered = [
        go(
            all_parts.at[chunk(lax.rem(dp + k, 8))],
            chunk_in.at[k - 1],
            (ps, pr),
            k - 1,
            dp=lax.rem(dp + k, 8),
        )
        for k in range(1, 8)
    ]
    steps.side()
    total = all_parts[chunk(dp), :].astype(f32)
    for k in range(1, 8):
        scattered[k - 1].wait_recv()
        total += chunk_in[k - 1].astype(f32)
    sums[chunk(dp), :] = total.astype(bf16)
    shared = [
        go(sums.at[chunk(dp)], sums.at[chunk(dp)], (as_, ar), k - 1, dp=lax.rem(dp + k, 8))
        for k in range(1, 8)
    ]
    whole = steps.total()
    upstream = whole[:rows]
    weighted = upstream * gain[...]
    values = inputs[...].astype(f32)
    scales = scale[...]
    inner = ColumnSum(
        jnp.sum(weighted * values, axis=1, keepdims=True), sum_buf, (ss, sr), go, peers
    )
    first_part = jnp.sum(upstream * values * scales, axis=0, keepdims=True)
    extra = jnp.concatenate(
        [first_part, gain_part[...], jnp.zeros((14, columns), f32)], axis=0
    )
    lat_buf[dp] = jnp.concatenate([whole[rows:], extra], axis=0).astype(bf16)
    along = [
        go(lat_buf.at[dp], lat_buf.at[dp], (ls, lr), k - 1, dp=lax.rem(dp + k, 8))
        for k in range(1, 8)
    ]
    inputs_grad[...] = (
        residual_grad[...]
        + scales * weighted
        - values * (scales * scales * scales * inner.total() / D)
    ).astype(bf16)
    for copy in along:
        copy.wait_recv()
    summed = lat_buf[0].astype(f32)
    for k in range(1, 8):
        summed += lat_buf[k].astype(f32)
    narrow_all[row] = summed.astype(bf16)
    spread = [
        go(narrow_all.at[row], narrow_all.at[row], (ns, nr), k - 1, row=lax.rem(row + k, 4))
        for k in (1, 2, 3)
    ]
    for copy in spread:
        copy.wait_recv()
    keep = lat - 32
    narrow[...] = narrow_all[:, :keep, :]
    small = narrow_all[0, pl.ds(keep, 16), :]
    latent_gain[col] = small
    last = [
        go(latent_gain.at[col], latent_gain.at[col], (gs, gr), j, col=peer)
        for j, peer in enumerate(peers)
    ]
    edge = pl.ds(keep + 16, 16)
    gains[...] = (
        narrow_all[0, edge, :].astype(f32)
        + narrow_all[1, edge, :].astype(f32)
        + narrow_all[2, edge, :].astype(f32)
        + narrow_all[3, edge, :].astype(f32)
    )
    for copy in last + shared:
        copy.wait_recv()
    for copy in pending:
        copy.wait_send()


def tail_step(part, query, ready, residual_grad, inputs, scale, gain, gain_part):
    rows, columns = inputs.shape
    piece = query.shape[0]
    all_rows = part.shape[0] // 4
    lat = all_rows - rows + 16
    return pl.pallas_call(
        tail_kernel,
        out_shape=(
            jax.ShapeDtypeStruct((rows, columns), bf16),
            jax.ShapeDtypeStruct((8 * piece, columns), bf16),
            jax.ShapeDtypeStruct((4, lat - 32, columns), bf16),
            jax.ShapeDtypeStruct((16, columns), f32),
            jax.ShapeDtypeStruct((4, 16, columns), bf16),
        ),
        in_specs=[VMEM] * 8,
        out_specs=(VMEM,) * 5,
        scratch_shapes=[
            pltpu.VMEM((7, piece, columns), bf16),
            pltpu.VMEM((8 * piece, columns), bf16),
            pltpu.VMEM((4, lat, columns), bf16),
            pltpu.VMEM((8, lat, columns), bf16),
            pltpu.VMEM((4, rows, 128), f32),
            *pair(3),
            *pair(7),
            *pair(7),
            *pair(7),
            *pair(3),
            *pair(3),
            *pair(3),
            *reduce_scratch(all_rows, columns),
        ],
        compiler_params=params(4),
        cost_estimate=cost(1 << 20, 200),
        name="tail_step",
    )(part, query, ready, residual_grad, inputs, scale, gain, gain_part)


def front_kernel(
    attended, weight, inputs, middle, full, attended_rows,
    own, out_buf, in_buf, acc, as_, ar, ps, pr, *sems,
):
    row, sibling, across, corner = place()
    greet((sibling, across), row)
    pending = []
    go = starter(pending)
    rows, columns = inputs.shape
    head = attended.shape[1]
    order = (2, 1, 3, 0)

    def block(k):
        return pl.ds(pl.multiple_of(lax.rem(row + k, 4) * rows, rows), rows)

    def slot(k):
        return pl.ds(k * head, head)

    got = {}
    for k in order:
        got[2, k] = go(
            attended.at[block(k)], attended_rows.at[block(k), slot(2)], (as_, ar), (1, k), col=across
        )
    for k in order:
        got[1, k] = go(
            attended.at[block(k)], attended_rows.at[block(k), slot(1)], (as_, ar), (0, k), col=sibling
        )
    attended_rows[:, slot(0)] = attended[...]
    for k in order:
        got[2, k].wait_recv()
        view = attended_rows.at[block(k), slot(2)]
        got[3, k] = go(
            view, attended_rows.at[block(k), slot(3)], (as_, ar), (2, k), col=sibling
        )
    sent = {}
    for k in order:
        got[1, k].wait_recv()
        got[3, k].wait_recv()
        product = jnp.dot(attended_rows[block(k), :], weight[...], preferred_element_type=f32)
        if k:
            out_buf[k - 1] = product.astype(bf16)
            sent[k] = go(
                out_buf.at[k - 1], in_buf.at[k - 1], (ps, pr), k - 1, row=lax.rem(row + k, 4)
            )
        else:
            acc[...] = product + inputs[...].astype(f32)
    total = acc[...]
    for k in (1, 3, 2):
        sent[k].wait_recv()
        total += in_buf[k - 1].astype(f32)
    middle[...] = total
    own[...] = total.astype(bf16)
    gather_steps(own, full, go, sems[0:2], sems[2:4], sems[4:6], row, sibling, across)
    for copy in pending:
        copy.wait_send()


def front_step(attended, weight, inputs):
    rows, columns = inputs.shape
    return pl.pallas_call(
        front_kernel,
        out_shape=(
            jax.ShapeDtypeStruct((rows, columns), f32),
            jax.ShapeDtypeStruct((4 * rows, 4 * columns), bf16),
            jax.ShapeDtypeStruct((4 * rows, columns), bf16),
        ),
        in_specs=[VMEM] * 3,
        out_specs=(VMEM,) * 3,
        scratch_shapes=[
            pltpu.VMEM((rows, columns), bf16),
            pltpu.VMEM((3, rows, columns), bf16),
            pltpu.VMEM((3, rows, columns), bf16),
            pltpu.VMEM((rows, columns), f32),
            *pair(3, 4),
            *pair(3),
            *gather_scratch,
        ],
        compiler_params=params(5),
        cost_estimate=cost(1 << 29, 150),
        name="front_step",
    )(attended, weight, inputs)


def dot(spec, left, right, kind=f32):
    return jnp.einsum(spec, left, right, preferred_element_type=f32).astype(kind)


def rotary_tables(length, half_width):
    position = jnp.arange(length, dtype=f32)[:, None]
    frequency = jnp.exp(jnp.arange(half_width, dtype=f32) * (-math.log(10000.0) / half_width))
    angles = position * frequency[None, :]
    return (jnp.cos(angles), jnp.sin(angles))


def rotate(values, cos_table, sin_table):
    half_width = cos_table.shape[-1]
    first_half = values[..., :half_width]
    second_half = values[..., half_width:]
    return jnp.concatenate(
        [
            first_half * cos_table - second_half * sin_table,
            second_half * cos_table + first_half * sin_table,
        ],
        axis=-1,
    )


def swap_chips(values, distance, other_replica):
    flip = 4 if other_replica else 0
    pairs = [
        (dp * 4 + col, (dp ^ flip) * 4 + (col ^ distance)) for dp in range(8) for col in range(4)
    ]
    return lax.ppermute(values, ("dp", "col"), pairs)


def deal(pieces):
    got = [pieces(0)]
    for k in (1, 2, 3):
        piece = pieces(k)
        if k == 1:
            got.append(swap_chips(piece, k, False))
        else:
            half = piece.shape[0] // 2
            got.append(
                jnp.concatenate(
                    [swap_chips(piece[:half], k, False), swap_chips(piece[half:], k, True)], axis=0
                )
            )
    return got


def pad_to(values, axis, size):
    widths = [(0, 0)] * values.ndim
    widths[axis] = (0, size - values.shape[axis])
    return jnp.pad(values, widths)


def visible_mask(offset, block_rows, prefix_len):
    query_pos = offset + jnp.arange(block_rows, dtype=jnp.int32)
    key_pos = jnp.arange(SEQ, dtype=jnp.int32)
    return (key_pos[None, :] <= query_pos[:, None]) | (key_pos[None, :] < prefix_len)


def attend_forward(queries, key_rows, value_rows, prefix_len):
    score_scale = (NOPE + ROPE) ** (-0.5)
    scores = dot("qd,kd->qk", queries, key_rows) * score_scale
    scores = jnp.where(visible_mask(0, SEQ, prefix_len), scores, masked_score)
    top_score = jnp.max(scores, axis=1, keepdims=True)
    exp_scores = jnp.exp(scores - top_score)
    row_total = jnp.sum(exp_scores, axis=1, keepdims=True)
    weights = (exp_scores / row_total).astype(bf16)
    result = dot("qk,kd->qd", weights, value_rows)
    return (result, (top_score + jnp.log(row_total))[:, 0])


def attend_backward(queries, key_rows, value_rows, log_total, out_grad, prefix_len):
    score_scale = (NOPE + ROPE) ** (-0.5)
    scores = dot("qd,kd->qk", queries, key_rows) * score_scale
    scores = jnp.where(visible_mask(0, SEQ, prefix_len), scores, masked_score)
    weights = jnp.exp(scores - log_total[:, None])
    value_grad = dot("qk,qd->kd", weights.astype(bf16), out_grad)
    weight_grad = dot("qd,kd->qk", out_grad, value_rows)
    centre = jnp.sum(weights * weight_grad, axis=1, keepdims=True)
    score_grad = (weights * (weight_grad - centre)).astype(bf16)
    query_grad = dot("qk,kd->qd", score_grad, key_rows) * score_scale
    key_grad = dot("qk,qd->kd", score_grad, queries) * score_scale
    return (query_grad, key_grad, value_grad)


def across_dp(values, step, flip):
    pairs = [(dp, ((dp // 4) ^ flip) * 4 + (dp + step) % 4) for dp in range(8)]
    return lax.ppermute(values, "dp", pairs)


def sum_sequences(values):
    z = lax.rem(lax.axis_index("dp"), 4)
    total = lax.dynamic_index_in_dim(values, z, 0, False).astype(f32)
    for step in (1, 2, 3):
        chunk = lax.dynamic_index_in_dim(values, lax.rem(z + step, 4), 0, False)
        total = total + across_dp(chunk, step, 0).astype(f32)
    total = total.astype(bf16)
    total = (total.astype(f32) + across_dp(total, 0, 1).astype(f32)).astype(bf16)
    return jnp.stack([total] + [across_dp(total, step, 0) for step in (1, 2, 3)])


def product(left, right):
    return jnp.dot(left, right, preferred_element_type=f32).astype(bf16)


def expert_grad_kernel(hidden, out_grad, delta, act, grads, *, ff, ff_pad):
    grads[0, pl.ds(0, ff), :] = product(delta[pl.ds(0, ff), :], hidden[...])
    grads[0, pl.ds(ff, ff), :] = product(delta[pl.ds(ff_pad, ff), :], hidden[...])
    grads[0, pl.ds(2 * ff, ff), :] = product(act[pl.ds(0, ff), :], out_grad[...])


def expert_grads(hidden, out_grad, delta, act, ff, ff_pad):
    tokens = hidden.shape[0]
    wide = pl.BlockSpec((tokens, 512), lambda e, k: (0, k))
    return pl.pallas_call(
        functools.partial(expert_grad_kernel, ff=ff, ff_pad=ff_pad),
        grid=(2, 4),
        out_shape=jax.ShapeDtypeStruct((8, 3 * ff, 512), bf16),
        in_specs=[
            wide,
            wide,
            pl.BlockSpec((2 * ff_pad, tokens), lambda e, k: (e, 0)),
            pl.BlockSpec((ff_pad, tokens), lambda e, k: (e, 0)),
        ],
        out_specs=pl.BlockSpec((1, 3 * ff, 512), lambda e, k: (e * 4 + k, 0, 0)),
        compiler_params=pltpu.CompilerParams(vmem_limit_bytes=52 << 20),
        cost_estimate=cost(2 * 8 * 3 * ff * 512 * tokens, 20),
        name="expert_grads",
    )(hidden, out_grad, delta, act)


def shared_grad_kernel(hidden, out_grad, delta, act, grads, router, *, sff, sff_pad):
    gate = product(delta[pl.ds(0, sff_pad), :], hidden[...])
    grads[0, pl.ds(0, sff), :] = gate[:sff]
    router[...] = gate[sff : sff + 16]
    grads[0, pl.ds(sff, sff), :] = product(delta[pl.ds(sff_pad, sff), :], hidden[...])
    grads[0, pl.ds(2 * sff, sff), :] = product(act[pl.ds(0, sff), :], out_grad[...])


def shared_grads(hidden, out_grad, delta, act, sff, sff_pad):
    tokens = hidden.shape[0]
    wide = pl.BlockSpec((tokens, 512), lambda k: (0, k))
    return pl.pallas_call(
        functools.partial(shared_grad_kernel, sff=sff, sff_pad=sff_pad),
        grid=(4,),
        out_shape=(
            jax.ShapeDtypeStruct((4, 3 * sff, 512), bf16),
            jax.ShapeDtypeStruct((16, D), bf16),
        ),
        in_specs=[
            wide,
            wide,
            pl.BlockSpec((2 * sff_pad, tokens), lambda k: (3, 0)),
            pl.BlockSpec((sff_pad, tokens), lambda k: (3, 0)),
        ],
        out_specs=(
            pl.BlockSpec((1, 3 * sff, 512), lambda k: (k, 0, 0)),
            pl.BlockSpec((16, 512), lambda k: (0, k)),
        ),
        compiler_params=pltpu.CompilerParams(vmem_limit_bytes=52 << 20),
        cost_estimate=cost(2 * 4 * 3 * sff * 512 * tokens, 10),
        name="shared_grads",
    )(hidden, out_grad, delta, act)


def sigmoid(value):
    return jax.nn.sigmoid(value)


def on_device(
    inputs,
    attention_gain,
    query_weight,
    latent_weight,
    latent_gain,
    expand_weight,
    output_weight,
    feedforward_gain,
    router_weight,
    shared_gate,
    shared_up,
    shared_down,
    expert_gate,
    expert_up,
    expert_down,
    routes,
    prefix,
    cotangent,
):
    row = lax.axis_index("row")
    col = lax.axis_index("col")
    prefix_len = prefix[0]
    cos_table, sin_table = rotary_tables(SEQ, ROPE // 2)
    first_gain = attention_gain.astype(f32)
    second_gain = feedforward_gain.astype(f32)
    compact_gain = latent_gain.astype(f32)
    residual_in = inputs.astype(f32)
    rows = inputs.shape[0]
    ff = expert_gate.shape[2]
    ff_pad = -(-ff // 128) * 128
    sff = shared_gate.shape[1] // 4
    sff_pad = 256

    gains = jnp.stack([attention_gain, feedforward_gain], axis=1)
    common = pad_to(jnp.concatenate([latent_weight[:, RANK:], router_weight, gains], axis=1), 1, 192)
    heads = query_weight.reshape(512, 4, NOPE + ROPE)

    def attention_piece(k):
        head = lax.dynamic_index_in_dim(heads, col ^ k, 1, False)
        return jnp.concatenate([latent_weight[:, :RANK], head, common], axis=1)

    attention_weights = jnp.concatenate(deal(attention_piece), axis=0)
    first_all = attention_weights[:, RANK + 256 + 8]
    second_all = attention_weights[:, RANK + 256 + 9]
    project_weight = attention_weights[:, : RANK + 256]

    gate_parts = expert_gate.reshape(4, 2, 512, ff)
    up_parts = expert_up.reshape(4, 2, 512, ff)
    down_parts = expert_down.reshape(4, 2, ff, 512)
    shared_gate_parts = shared_gate.reshape(512, 4, sff)
    shared_up_parts = shared_up.reshape(512, 4, sff)
    shared_down_parts = shared_down.reshape(4, sff, 512)

    def up_piece(k):
        gate = pad_to(lax.dynamic_index_in_dim(gate_parts, col ^ k, 0, False), 2, ff_pad)
        up = pad_to(lax.dynamic_index_in_dim(up_parts, col ^ k, 0, False), 2, ff_pad)
        low_gate = lax.dynamic_index_in_dim(shared_gate_parts, col ^ k, 1, False)
        low_gate = pad_to(jnp.concatenate([low_gate, router_weight], axis=1), 1, sff_pad)
        low_up = pad_to(
            lax.dynamic_index_in_dim(shared_up_parts, col ^ k, 1, False), 1, sff_pad
        )
        return jnp.concatenate([gate[0], up[0], gate[1], up[1], low_gate, low_up], axis=1)

    def down_piece(k):
        down = pad_to(lax.dynamic_index_in_dim(down_parts, col ^ k, 0, False), 1, ff_pad)
        low = pad_to(lax.dynamic_index_in_dim(shared_down_parts, col ^ k, 0, False), 0, sff_pad)
        return jnp.concatenate([down[0], down[1], low], axis=0)

    up_weight = jnp.concatenate(deal(up_piece), axis=0)
    down_weight = jnp.concatenate(deal(down_piece), axis=1)
    out_weight = jnp.concatenate(
        [lax.dynamic_slice_in_dim(output_weight, (col ^ k) * VDIM, VDIM, 0) for k in range(4)],
        axis=0,
    )
    order = col ^ jnp.arange(4, dtype=jnp.int32)

    input_rows = gather_grid(inputs, 0).astype(f32)
    scale_one = lax.rsqrt(jnp.mean(input_rows * input_rows, axis=1) + norm_eps)
    normed = (input_rows * scale_one[:, None] * first_all.astype(f32)[None, :]).astype(bf16)
    projected = dot("td,dq->tq", normed, project_weight)
    content = projected[:, :RANK]
    latent_scale = lax.rsqrt(jnp.mean(content * content, axis=1) + norm_eps)
    compact = (content * latent_scale[:, None] * compact_gain[None, :]).astype(bf16)
    shared_key = rotate(projected[:, RANK + 192 :], cos_table, sin_table).astype(bf16)
    key_value = dot("tr,rk->tk", compact, expand_weight, bf16)
    query_rot = jnp.concatenate(
        [
            projected[:, RANK : RANK + NOPE],
            rotate(projected[:, RANK + NOPE : RANK + 192], cos_table, sin_table),
        ],
        axis=1,
    ).astype(bf16)
    key_rows = jnp.concatenate([key_value[:, :NOPE], shared_key], axis=1)
    value_rows = key_value[:, NOPE:]
    head_result, log_total = attend_forward(query_rot, key_rows, value_rows, prefix_len)
    residual_mid, middle_rows, attended_rows = front_step(
        head_result.astype(bf16), out_weight, inputs
    )

    middle_rows = middle_rows.astype(f32)
    scale_two = lax.rsqrt(jnp.mean(middle_rows * middle_rows, axis=1) + norm_eps)
    hidden = (middle_rows * scale_two[:, None] * second_all.astype(f32)[None, :]).astype(bf16)
    out_grad = gather_grid(cotangent, 0)
    experts = jnp.arange(EXPERTS, dtype=jnp.int32)
    named = jnp.any(routes.T[None, :, :] == experts[:, None, None], axis=1).astype(f32)
    pre = dot("td,df->ft", hidden, up_weight)
    low = 4 * ff_pad
    router_probs = jax.nn.softmax(pre[low + sff : low + sff + EXPERTS], axis=0)
    weight_all = router_probs * named
    act_grad_all = dot("td,fd->ft", out_grad, down_weight)
    acts, deltas = [], []
    probs_part = jnp.zeros_like(router_probs)
    for e in range(3):
        if e < 2:
            size, base = ff_pad, 2 * e * ff_pad
            mine = (experts == 2 * col + e).astype(f32)[:, None]
            slot_weight = jnp.sum(weight_all * mine, axis=0, keepdims=True)
        else:
            size, base, slot_weight = sff_pad, low, 1.0
        gate_pre, up_pre = pre[base : base + size], pre[base + size : base + 2 * size]
        act_grad = act_grad_all[e * ff_pad : e * ff_pad + size]
        gate_sig = jax.nn.sigmoid(gate_pre)
        gate_silu = gate_pre * gate_sig
        acts.append((slot_weight * gate_silu * up_pre).astype(bf16))
        weighted = slot_weight * act_grad
        gate_delta = weighted * up_pre * (gate_sig * (1.0 + gate_pre * (1.0 - gate_sig)))
        up_delta = weighted * gate_silu
        if e < 2:
            named_sum = jnp.sum(act_grad * gate_silu * up_pre, axis=0, keepdims=True)
            probs_part = probs_part + named_sum * mine * named
            deltas += [gate_delta, up_delta]
        else:
            logits_part = router_probs * (
                probs_part - jnp.sum(router_probs * probs_part, axis=0, keepdims=True)
            )
            gate_delta = jnp.concatenate(
                [gate_delta[:sff], logits_part, gate_delta[sff + EXPERTS :]], axis=0
            )
            deltas += [gate_delta, up_delta]
    act = jnp.concatenate(acts, axis=0)
    delta = jnp.concatenate([value.astype(bf16) for value in deltas], axis=0)
    combined = dot("ft,fd->td", act, down_weight, bf16)
    hidden_grad = dot("ft,df->td", delta, up_weight, bf16)
    expert_grad = expert_grads(hidden, out_grad, delta, act, ff, ff_pad)
    shared_grad, router_part = shared_grads(hidden, out_grad, delta, act, sff, sff_pad)
    hidden_grad, expert_grad, shared_grad, combined = lax.optimization_barrier(
        (hidden_grad, expert_grad, shared_grad, combined)
    )
    expert_sum = lax.psum_scatter(expert_grad, "dp", scatter_dimension=0, tiled=True)[0]
    shared_home = jnp.stack(
        [shared_grad[0]] + [swap_chips(shared_grad[k], k, False) for k in (1, 2, 3)]
    )
    shared_sum = sum_sequences(shared_home)

    my_scale_one = lax.dynamic_slice_in_dim(scale_one, row * rows, rows, 0)[:, None]
    my_scale_two = lax.dynamic_slice_in_dim(scale_two, row * rows, rows, 0)[:, None]
    residual_grad, residual_rows, attended_grad, second_gain_part = middle_step(
        hidden_grad, residual_mid, cotangent, my_scale_two, second_gain[None, :], out_weight
    )
    output = (residual_mid + reduce_grid(combined, 1)).astype(bf16)
    head_grad = dot("th,td->hd", attended_rows, residual_rows, bf16)
    output_weight_grad = head_grad.reshape(4, VDIM, 512)[order].reshape(4 * VDIM, 512)
    query_rot_grad, key_grad, value_grad = attend_backward(
        query_rot, key_rows, value_rows, log_total, attended_grad, prefix_len
    )
    pair_grad = jnp.concatenate([key_grad[:, :NOPE], value_grad], axis=1).astype(bf16)
    expand_part = dot("tk,tr->kr", pair_grad, compact, bf16)
    compact_grad = dot("tk,rk->tr", pair_grad, expand_weight)
    weighted_compact = compact_grad * compact_gain[None, :]
    inner_sum = jnp.sum(weighted_compact * content, axis=1)
    content_grad = (
        latent_scale[:, None] * weighted_compact
        - content * (latent_scale * latent_scale * latent_scale * inner_sum / RANK)[:, None]
    )
    latent_gain_part = jnp.sum(compact_grad * content * latent_scale[:, None], axis=0)
    project_grad = jnp.concatenate(
        [
            content_grad,
            query_rot_grad[:, :NOPE],
            rotate(query_rot_grad[:, NOPE:], cos_table, -sin_table),
            rotate(key_grad[:, NOPE:], cos_table, -sin_table),
        ],
        axis=1,
    ).astype(bf16)
    normed_grad = dot("tq,dq->td", project_grad, project_weight, bf16)
    project_part = dot("tq,td->qd", project_grad, normed, bf16)
    latent_part = jnp.concatenate([project_part[:RANK], project_part[RANK + 192 :]], axis=0)
    extra = jnp.concatenate(
        [
            jnp.tile(latent_gain_part.astype(bf16)[None, :], (1, 4)),
            router_part[:EXPERTS],
            jnp.zeros((7, D), bf16),
        ],
        axis=0,
    )
    tail = jnp.concatenate(
        [
            normed_grad.reshape(4, rows, D),
            latent_part.reshape(4, -1, D),
            jnp.broadcast_to(extra[None], (4, 16, D)),
        ],
        axis=1,
    )
    inputs_grad, sums, narrow, gains, latent_small = tail_step(
        tail.reshape(-1, D),
        project_part[RANK : RANK + 192],
        jnp.concatenate([output_weight_grad, expand_part], axis=0),
        residual_grad,
        inputs,
        my_scale_one,
        first_gain[None, :],
        second_gain_part,
    )
    output_weight_grad = sums[:512].astype(f32)
    expand_grad = sums[512:768].T.astype(f32)
    query_weight_grad = sums[768:].T.astype(f32)
    latent_weight_grad = narrow.reshape(-1, 512).T.astype(f32)
    latent_gain_grad = latent_small[0, 0].astype(f32)
    router_grad = (
        lax.dynamic_index_in_dim(latent_small, col, 0, False)[1 : 1 + EXPERTS].T.astype(f32)
    )
    first_gain_grad, second_gain_grad = gains[0], gains[1]

    pairs = [
        (dp * 4 + c, (2 * c + dp // 4) * 4 + (c ^ (dp % 4))) for dp in range(8) for c in range(4)
    ]
    expert_sum = lax.ppermute(expert_sum, ("dp", "col"), pairs).astype(f32)
    expert_gate_grad = expert_sum[None, :ff].transpose(0, 2, 1)
    expert_up_grad = expert_sum[None, ff : 2 * ff].transpose(0, 2, 1)
    expert_down_grad = expert_sum[None, 2 * ff :]
    z = lax.rem(lax.axis_index("dp"), 4)
    shared_sum = shared_sum[lax.rem(z + 4 - order, 4)].astype(f32)
    shared_gate_grad = shared_sum[:, :sff].reshape(4 * sff, 512).T
    shared_up_grad = shared_sum[:, sff : 2 * sff].reshape(4 * sff, 512).T
    shared_down_grad = shared_sum[:, 2 * sff :].reshape(4 * sff, 512)
    return (
        output,
        inputs_grad,
        first_gain_grad,
        query_weight_grad,
        latent_weight_grad,
        latent_gain_grad,
        expand_grad,
        output_weight_grad,
        second_gain_grad,
        router_grad,
        shared_gate_grad,
        shared_up_grad,
        shared_down_grad,
        expert_gate_grad,
        expert_up_grad,
        expert_down_grad,
    )


def solution(mesh):
    placed = (
        P(("dp", "row"), "col"),
        P("col"),
        P("col", "row"),
        P("col", None),
        P(),
        P(None, ("row", "col")),
        P("row", "col"),
        P("col"),
        P("col", None),
        P("col", "row"),
        P("col", "row"),
        P("row", "col"),
        P(None, "col", "row"),
        P(None, "col", "row"),
        P(None, "row", "col"),
        P("dp", None),
        P("dp"),
        P(("dp", "row"), "col"),
    )
    return jax.shard_map(
        on_device,
        mesh=mesh,
        in_specs=placed,
        out_specs=(
            P(("dp", "row"), "col"),
            P(("dp", "row"), "col"),
            P("col"),
            P("col", "row"),
            P("col", None),
            P(),
            P(None, ("row", "col")),
            P("row", "col"),
            P("col"),
            P("col", None),
            P("col", "row"),
            P("col", "row"),
            P("row", "col"),
            P("dp", "col", "row"),
            P("dp", "col", "row"),
            P("dp", "row", "col"),
        ),
        check_vma=False,
    )
```

time: 954 us -> 705 us (0.74)
  waiting for transfers between devices: 283 us -> 64.9 us
  Pallas kernels: 244 us -> 384 us
  blocking collectives: 105 us -> 0 us
  matrix products: 101 us -> 58.6 us
  local copies, waits for them, and re-layouts: 96 us -> 68.4 us
  starting transfers between devices: 22.3 us -> 38.3 us
    pallas_call x0 -> x5, Pallas kernels: none -> 271 us  [the longest x1 113 us: tail_step(): pl.pallas_call(tail_kernel, out_shape=(jax.ShapeDtypeStruct((rows, column...]
    reduce_scatter x1, waiting for transfers between devices: 137 us -> 0.01 us  [on_device(): lax.psum_scatter(expert_grad, 'dp', scatter_dimension=0, tiled=True)[0]]
    psum x3 -> x0, blocking collectives: 92.5 us -> none  [the longest x1 80.7 us: on_device(): lax.psum((first_gain_part, second_gain_part), ('dp', 'row'))]
    pallas_call x3 -> x1, Pallas kernels: 126 us -> 40 us  [reduce_grid(): pl.pallas_call(reduce_kernel, out_shape=jax.ShapeDtypeStruct((rows, colum...]
    psum x2 -> x0, waiting for transfers between devices: 85 us -> none  [the longest x1 85 us: on_device(): lax.psum(shared_grad.astype(bf16), 'dp').reshape(4, 512, 3 * sff_pad)]
    ppermute x0 -> x7, waiting for transfers between devices: none -> 48.1 us  [across_dp(): return lax.ppermute(values, 'dp', pairs)]
    pallas_call x3 -> x2, Pallas kernels: 118 us -> 72.7 us  [gather_grid(): pl.pallas_call(gather_kernel, out_shape=jax.ShapeDtypeStruct((4 * rows, 4...]
    dot_general x28 -> x17, matrix products: 101 us -> 58.6 us  [dot(): jnp.einsum(spec, left, right, preferred_element_type=f32).astype(kind)]
  transfers between devices with their start and end apart: 27 -> 27, of which waited for: 7 -> 4; matrix products, arithmetic and copies ran while one was open for 21% -> 19% of each run, Pallas kernels for 22% -> 52%
where the time goes in v2:
time: 705 us; the launch traced here: 695 us
  Pallas kernels  384 us (54%)
  local copies, waits for them, and re-layouts  68.4 us (10%)
  waiting for transfers between devices  64.9 us (9%)
  other arithmetic  64.3 us (9%)
  matrix products  58.6 us (8%)
  starting transfers between devices  38.3 us (5%)
  between operations  16.9 us (2%)
    pallas_call x1, Pallas kernels, tail_step(): pl.pallas_call(tail_kernel, out_shape=(jax.ShapeDtypeStruct((rows, column...  113 us
    pallas_call x1, Pallas kernels, middle_step(): pl.pallas_call(middle_kernel, out_shape=(jax.ShapeDtypeStruct((rows, colu...  76.7 us
    pallas_call x2, Pallas kernels, gather_grid(): pl.pallas_call(gather_kernel, out_shape=jax.ShapeDtypeStruct((4 * rows, 4...  72.7 us
    dot_general x17, matrix products, dot(): jnp.einsum(spec, left, right, preferred_element_type=f32).astype(kind)  58.6 us
    pallas_call x1, Pallas kernels, front_step(): pl.pallas_call(front_kernel, out_shape=(jax.ShapeDtypeStruct((rows, colum...  57.5 us
    ppermute x7, waiting for transfers between devices, across_dp(): return lax.ppermute(values, 'dp', pairs)  48.1 us
    pallas_call x1, Pallas kernels, reduce_grid(): pl.pallas_call(reduce_kernel, out_shape=jax.ShapeDtypeStruct((rows, colum...  40 us
    unnamed x206, local copies, waits for them, and re-layouts  36.8 us
  transfers between devices with their start and end apart: 27, of which 4 were waited for; matrix products, arithmetic and copies ran while one was open for 19% of the time, Pallas kernels for 52%

profile of v2, /device:TPU:5, one launch (start us, length us, event | category | flops | bytes accessed | tf_op | source)
XLA Modules:
  0.0 695.4 jit_solution(383706423481379212)
XLA Ops:
  18.3 42.1 %gather_grid.2 = bf16[1024,2048]{1,0:T(8,128)(2,1)} custom-call(bf16[256,512]{1,0:T(8,128)(2,1)S(1)} %copy-done.3), custom_call_target="tpu_custom_call" | custom-call | bytes 83886080 | tf_op jit(solution)/shard_map/gather_grid/pallas_call | solution.py:132
  60.5 3.2 fusion
  91.7 30.5 %gather_grid.3.out_grad = bf16[1024,2048]{1,0:T(8,128)(2,1)} custom-call(bf16[256,512]{1,0:T(8,128)(2,1)S(1)} %copy-done.2), custom_call_target="tpu_custom_call" | custom-call | bytes 83886080 | tf_op jit(solution)/shard_map/gather_grid/pallas_call | solution.py:132
  122.3 2.8 fusion.119
  136.7 3.6 fusion.17
  145.2 57.5 %front_step.1 = (f32[256,512]{1,0:T(8,128)S(1)}, bf16[1024,2048]{1,0:T(8,128)(2,1)}, bf16[1024,512]{1,0:T(8,128)(2,1)}) custom-call(bf16[1024,128]{1,0:T(8,128)(2,1)S(1)} %fusion.31.attended, bf16[512,512]{1,0:T(8,128)(2,1)S(1)} %pad_maximum_fusion.16.weight, bf16[256,512]{1,0:T(8,128)(2,1)S(1)} %copy-done.3), custom_call_target="tpu_custom_call" | custom-call | flops 536870912 | bytes 157286400 | tf_op jit(solution)/shard_map/front_step/pallas_call | solution.py:574
  202.7 3.2 fusion.3
  212.7 17.1 %fusion.12 = bf16[1024,2048]{1,0:T(8,128)(2,1)S(1)} fusion(bf16[176,512]{1,0:T(8,128)(2,1)S(1)} %copy-done.40, bf16[512,512]{1,0:T(8,128)(2,1)S(1)} %collective-permute-done.14, bf16[512,512]{1,0:T(8,128)(2,1)} %collective-permute-done.13, bf16[512,512]{1,0:T(8,128)(2,1)} %collective-permute-done.12, bf16[512,512]{1,0:T(8,128)(2,1)} %collective-permute-done.11, ...), kind=kLoop, calls=%fused_computation.21 | loop fusion | flops 44040192 | bytes 8306688 | tf_op jit(solution)/shard_map/concatenate | solution.py:838
  229.9 4.5 fusion.126
  238.3 16.7 %collective-permute-done.8 = bf16[256,2048]{0,1:T(8,128)(2,1)S(1)} collective-permute-done((bf16[256,2048]{0,1:T(8,128)(2,1)}, bf16[256,2048]{0,1:T(8,128)(2,1)S(1)}, u32[]{:S(2)}, u32[]{:S(2)}) %collective-permute-start.8) | collective-permute-done | bytes 1048608 | tf_op jit(solution)/shard_map/ppermute | solution.py:627
  257.3 11.7 %fusion.125 = f32[2048,1024]{1,0:T(8,128)S(1)} fusion(bf16[2048,2048]{0,1:T(8,128)(2,1)} %constant_dynamic-update-slice_fusion.5, bf16[1024,2048]{1,0:T(8,128)(2,1)S(1)} %fusion.5.hidden), kind=kOutput, calls=%fused_computation.332 | convolution fusion | flops 8589934592 | bytes 20971520 | tf_op jit(solution)/shard_map/td,df->ft/dot_general | solution.py:599
  275.0 14.3 %convolution_convert_fusion.part = bf16[1024,2048]{1,0:T(8,128)(2,1)} fusion(bf16[2048,1024]{1,0:T(8,128)(2,1)S(1)} %fusion.45.delta, bf16[2048,2048]{0,1:T(8,128)(2,1)} %constant_dynamic-update-slice_fusion.5), kind=kOutput, calls=%fused_computation.30 | convolution fusion | flops 8592031744 | bytes 16777216 | tf_op jit(solution)/shard_map/ft,df->td/dot_general | solution.py:599
  290.8 16.8 %expert_grads.1 = bf16[8,1056,512]{2,1,0:T(8,128)(2,1)} custom-call(bf16[1024,2048]{1,0:T(8,128)(2,1)} %copy-done.10, bf16[1024,2048]{1,0:T(8,128)(2,1)} %gather_grid.3.out_grad, bf16[2048,1024]{1,0:T(8,128)(2,1)} %copy-done.14, bf16[1024,1024]{1,0:T(8,128)(2,1)} %pad_maximum_fusion.4.act), custom_call_target="tpu_custom_call" | custom-call | flops 8858370048 | bytes 20971520 | tf_op jit(solution)/shard_map/expert_grads/pallas_call | solution.py:713
  307.6 7.6 %shared_grads.1 = (bf16[4,528,512]{2,1,0:T(8,128)(2,1)}, bf16[16,2048]{1,0:T(8,128)(2,1)S(1)}) custom-call(bf16[1024,2048]{1,0:T(8,128)(2,1)} %copy-done.10, bf16[1024,2048]{1,0:T(8,128)(2,1)} %gather_grid.3.out_grad, bf16[2048,1024]{1,0:T(8,128)(2,1)} %copy-done.14, bf16[1024,1024]{1,0:T(8,128)(2,1)} %pad_maximum_fusion.4.act), custom_call_target="tpu_custom_call" | custom-call | flops 2214592512 | bytes 10485760 | tf_op jit(solution)/shard_map/shared_grads/pallas_call | solution.py:741
  315.2 6.4 convolution_convert_fusion.2.part
  326.0 76.7 %middle_step.1 = (f32[256,512]{1,0:T(8,128)S(1)}, bf16[1024,512]{1,0:T(8,128)(2,1)}, bf16[1024,128]{1,0:T(8,128)(2,1)S(1)}, f32[1,512]{1,0:T(1,128)S(1)}) custom-call(bf16[1024,2048]{1,0:T(8,128)(2,1)} %convolution_convert_fusion.part, f32[256,512]{1,0:T(8,128)S(1)} %get-tuple-element.34.middle, bf16[256,512]{1,0:T(8,128)(2,1)S(1)} %copy-done.2, ...), custom_call_target="tpu_custom_call" | custom-call | flops 536870912 | bytes 157286400 | tf_op jit(solution)/shard_map/middle_step/pallas_call | solution.py:340
  412.1 3.9 convolution_convert_fusion.3
  430.5 5.6 convolution_convert_fusion.1
  437.1 3.5 pad_maximum_fusion
  440.5 112.7 %tail_step.1 = (bf16[256,512]{1,0:T(8,128)(2,1)S(1)}, bf16[1536,512]{1,0:T(8,128)(2,1)}, bf16[4,144,512]{2,1,0:T(8,128)(2,1)S(1)}, f32[16,512]{1,0:T(8,128)S(1)}, bf16[4,16,512]{2,1,0:T(8,128)(2,1)S(1)}) custom-call(bf16[1664,2048]{1,0:T(8,128)(2,1)} %bitcast.243, bf16[192,2048]{1,0:T(8,128)(2,1)} %slice.420.query, ...), custom_call_target="tpu_custom_call" | custom-call | flops 1048576 | bytes 209715200 | tf_op jit(solution)/shard_map/tail_step/pallas_call | solution.py:483
  555.1 12.2 %collective-permute-start.20 = (bf16[528,512]{1,0:T(8,128)(2,1)S(1)}, bf16[528,512]{1,0:T(8,128)(2,1)S(1)}, u32[]{:S(2)}, u32[]{:S(2)}) collective-permute-start(bf16[528,512]{1,0:T(8,128)(2,1)S(1)} %get-tuple-element.136), channel_id=1, source_target_pairs={{0,48},{16,0},{32,16},{48,32},{64,112},{80,64},{96,80},{112,96},{1... | collective-permute-start | bytes 1622024 | tf_op jit(solution)/shard_map/ppermute | solution.py:686
  568.5 40.0 %reduce_grid.1 = f32[256,512]{1,0:T(8,128)S(1)} custom-call(bf16[1024,2048]{1,0:T(8,128)(2,1)} %convolution_convert_fusion.2.part), custom_call_target="tpu_custom_call" | custom-call | bytes 104857600 | tf_op jit(solution)/shard_map/reduce_grid/pallas_call | solution.py:233
  611.8 12.2 %collective-permute-done.21 = bf16[528,512]{1,0:T(8,128)(2,1)S(1)} collective-permute-done((bf16[528,512]{1,0:T(8,128)(2,1)S(1)}, bf16[528,512]{1,0:T(8,128)(2,1)S(1)}, u32[]{:S(2)}, u32[]{:S(2)}) %collective-permute-start.21) | collective-permute-done | bytes 540704 | tf_op jit(solution)/shard_map/ppermute | solution.py:686
  624.2 2.1 collective-permute-start.24
  628.3 4.6 collective-permute-start.25
  633.5 3.0 copy.48
  637.5 2.1 slice_convert_fusion.3
  640.9 21.9 %collective-permute-done.23 = bf16[528,512]{1,0:T(8,128)(2,1)} collective-permute-done((bf16[528,512]{1,0:T(8,128)(2,1)S(1)}, bf16[528,512]{1,0:T(8,128)(2,1)}, u32[]{:S(2)}, u32[]{:S(2)}) %collective-permute-start.23) | collective-permute-done | bytes 540704 | tf_op jit(solution)/shard_map/ppermute | solution.py:686
  662.8 14.0 %collective-permute-done.22 = bf16[528,512]{1,0:T(8,128)(2,1)} collective-permute-done((bf16[528,512]{1,0:T(8,128)(2,1)S(1)}, bf16[528,512]{1,0:T(8,128)(2,1)}, u32[]{:S(2)}, u32[]{:S(2)}) %collective-permute-start.22) | collective-permute-done | bytes 540704 | tf_op jit(solution)/shard_map/ppermute | solution.py:686
  676.8 3.0 pad_maximum_fusion.3
  679.8 2.4 gather_fusion.1
  682.2 2.2 fusion.117
  (366 shorter events, 118.1 us)
Async XLA Ops:
  7.2 134.0 %copy-start = (bf16[512,256]{1,0:T(8,128)(2,1)S(1)}, bf16[512,256]{1,0:T(8,128)(2,1)}, u32[]{:S(2)}) copy-start(bf16[512,256]{1,0:T(8,128)(2,1)} %param.23) | copy-start | bytes 786436
  7.2 621.1 %reduce-scatter.2.cloned.1.call-start = ((), (), s32[]{:S(2)}) async-start(), calls=%async_computation.1 | async-start | bytes 9732096 | tf_op jit(solution)/shard_map/reduce_scatter | solution.py:917
  11.8 113.8 %collective-permute-start = (bf16[512,896]{0,1:T(8,128)(2,1)}, bf16[512,896]{0,1:T(8,128)(2,1)}, u32[]{:S(2)}, u32[]{:S(2)}) collective-permute-start(bf16[512,896]{0,1:T(8,128)(2,1)} %get-tuple-element.175), channel_id=1, source_target_pairs={{0,1},{1,0},{2,3},{3,2},{16,17},{17,16},{18,19},{19,18},{32,33},{3... | collective-permute-start | bytes 2752520 | tf_op jit(solution)/shard_map/ppermute | solution.py:627
  13.5 113.9 %collective-permute-start.1 = (bf16[256,896]{0,1:T(8,128)(2,1)}, bf16[256,896]{0,1:T(8,128)(2,1)}, u32[]{:S(2)}, u32[]{:S(2)}) collective-permute-start(bf16[256,896]{0,1:T(8,128)(2,1)} %get-tuple-element.149), channel_id=1, source_target_pairs={{0,2},{1,3},{2,0},{3,1},{16,18},{17,19},{18,16},{19,17},{32,34},{3... | collective-permute-start | bytes 1376264 | tf_op jit(solution)/shard_map/ppermute | solution.py:627
  14.4 115.3 %collective-permute-start.2 = (bf16[256,896]{0,1:T(8,128)(2,1)}, bf16[256,896]{0,1:T(8,128)(2,1)}, u32[]{:S(2)}, u32[]{:S(2)}) collective-permute-start(bf16[256,896]{0,1:T(8,128)(2,1)} %get-tuple-element.148), channel_id=1, source_target_pairs={{0,66},{1,67},{2,64},{3,65},{16,82},{17,83},{18,80},{19,81},{32,98... | collective-permute-start | bytes 1376264 | tf_op jit(solution)/shard_map/ppermute | solution.py:627
  15.4 117.4 %collective-permute-start.3 = (bf16[256,896]{0,1:T(8,128)(2,1)}, bf16[256,896]{0,1:T(8,128)(2,1)}, u32[]{:S(2)}, u32[]{:S(2)}) collective-permute-start(bf16[256,896]{0,1:T(8,128)(2,1)} %get-tuple-element.147), channel_id=1, source_target_pairs={{0,3},{1,2},{2,1},{3,0},{16,19},{17,18},{18,17},{19,16},{32,35},{3... | collective-permute-start | bytes 1376264 | tf_op jit(solution)/shard_map/ppermute | solution.py:627
  17.3 117.2 %collective-permute-start.4 = (bf16[256,896]{0,1:T(8,128)(2,1)}, bf16[256,896]{0,1:T(8,128)(2,1)}, u32[]{:S(2)}, u32[]{:S(2)}) collective-permute-start(bf16[256,896]{0,1:T(8,128)(2,1)} %get-tuple-element.146), channel_id=1, source_target_pairs={{0,67},{1,66},{2,65},{3,64},{16,83},{17,82},{18,81},{19,80},{32,99... | collective-permute-start | bytes 1376264 | tf_op jit(solution)/shard_map/ppermute | solution.py:627
  63.7 72.9 %copy-start.74 = (f32[1024]{0:T(1024)}, f32[1024]{0:T(1024)S(1)}, u32[]{:S(2)}) copy-start(f32[1024]{0:T(1024)S(1)} %add_rsqrt_fusion.2) | copy-start | bytes 12292
  90.9 53.8 %copy-start.1 = (bf16[512,512]{1,0:T(8,128)(2,1)}, bf16[512,512]{1,0:T(8,128)(2,1)S(1)}, u32[]{:S(2)}) copy-start(bf16[512,512]{1,0:T(8,128)(2,1)S(1)} %pad_maximum_fusion.16.weight) | copy-start | bytes 1572868
  125.6 81.5 %collective-permute-start.14 = (bf16[512,512]{1,0:T(8,128)(2,1)}, bf16[512,512]{1,0:T(8,128)(2,1)S(1)}, u32[]{:S(2)}, u32[]{:S(2)}) collective-permute-start(bf16[512,512]{1,0:T(8,128)(2,1)} %get-tuple-element.185), channel_id=1, source_target_pairs={{0,67},{1,66},{2,65},{3,64},{16,83},{17,82},{18,81},{19,80},{32,99... | collective-permute-start | bytes 1572872 | tf_op jit(solution)/shard_map/ppermute | solution.py:627
  127.4 79.9 %collective-permute-start.13 = (bf16[512,512]{1,0:T(8,128)(2,1)}, bf16[512,512]{1,0:T(8,128)(2,1)}, u32[]{:S(2)}, u32[]{:S(2)}) collective-permute-start(bf16[512,512]{1,0:T(8,128)(2,1)} %get-tuple-element.184), channel_id=1, source_target_pairs={{0,3},{1,2},{2,1},{3,0},{16,19},{17,18},{18,17},{19,16},{32,35},{3... | collective-permute-start | bytes 1572872 | tf_op jit(solution)/shard_map/ppermute | solution.py:627
  129.8 78.5 %collective-permute-start.12 = (bf16[512,512]{1,0:T(8,128)(2,1)}, bf16[512,512]{1,0:T(8,128)(2,1)}, u32[]{:S(2)}, u32[]{:S(2)}) collective-permute-start(bf16[512,512]{1,0:T(8,128)(2,1)} %get-tuple-element.183), channel_id=1, source_target_pairs={{0,66},{1,67},{2,64},{3,65},{16,82},{17,83},{18,80},{19,81},{32,98... | collective-permute-start | bytes 1572872 | tf_op jit(solution)/shard_map/ppermute | solution.py:627
  132.8 77.3 %collective-permute-start.11 = (bf16[512,512]{1,0:T(8,128)(2,1)}, bf16[512,512]{1,0:T(8,128)(2,1)}, u32[]{:S(2)}, u32[]{:S(2)}) collective-permute-start(bf16[512,512]{1,0:T(8,128)(2,1)} %get-tuple-element.182), channel_id=1, source_target_pairs={{0,2},{1,3},{2,0},{3,1},{16,18},{17,19},{18,16},{19,17},{32,34},{3... | collective-permute-start | bytes 1572872 | tf_op jit(solution)/shard_map/ppermute | solution.py:627
  134.5 77.0 %collective-permute-start.10 = (bf16[1024,512]{1,0:T(8,128)(2,1)}, bf16[1024,512]{1,0:T(8,128)(2,1)S(1)}, u32[]{:S(2)}, u32[]{:S(2)}) collective-permute-start(bf16[1024,512]{1,0:T(8,128)(2,1)} %fusion.35), channel_id=1, source_target_pairs={{0,1},{1,0},{2,3},{3,2},{16,17},{17,16},{18,19},{19,18},{32,33},{3... | collective-permute-start | bytes 3145736 | tf_op jit(solution)/shard_map/ppermute | solution.py:627
  207.2 50.2 %copy-start.10 = (bf16[1024,2048]{1,0:T(8,128)(2,1)}, bf16[1024,2048]{1,0:T(8,128)(2,1)S(1)}, u32[]{:S(2)}) copy-start(bf16[1024,2048]{1,0:T(8,128)(2,1)S(1)} %fusion.5.hidden) | copy-start | bytes 12582916
  207.2 27.3 %collective-permute-start.5 = (bf16[512,2048]{0,1:T(8,128)(2,1)}, bf16[512,2048]{0,1:T(8,128)(2,1)S(1)}, u32[]{:S(2)}, u32[]{:S(2)}) collective-permute-start(bf16[512,2048]{0,1:T(8,128)(2,1)} %pad_dynamic-update-slice_fusion.4), channel_id=1, source_target_pairs={{0,1},{1,0},{2,3},{3,2},{16,17},{17,16},{18,19},{19,18},{32,33},{3... | collective-permute-start | bytes 6291464 | tf_op jit(solution)/shard_map/ppermute | solution.py:627
  207.4 28.6 %collective-permute-start.6 = (bf16[256,2048]{0,1:T(8,128)(2,1)S(1)}, bf16[256,2048]{0,1:T(8,128)(2,1)S(1)}, u32[]{:S(2)}, u32[]{:S(2)}) collective-permute-start(bf16[256,2048]{0,1:T(8,128)(2,1)S(1)} %copy-done.32), channel_id=1, source_target_pairs={{0,2},{1,3},{2,0},{3,1},{16,18},{17,19},{18,16},{19,17},{32,34},{3... | collective-permute-start | bytes 3145736 | tf_op jit(solution)/shard_map/ppermute | solution.py:627
  208.2 28.9 %collective-permute-start.7 = (bf16[256,2048]{0,1:T(8,128)(2,1)S(1)}, bf16[256,2048]{0,1:T(8,128)(2,1)S(1)}, u32[]{:S(2)}, u32[]{:S(2)}) collective-permute-start(bf16[256,2048]{0,1:T(8,128)(2,1)S(1)} %copy-done.31), channel_id=1, source_target_pairs={{0,66},{1,67},{2,64},{3,65},{16,82},{17,83},{18,80},{19,81},{32,98... | collective-permute-start | bytes 3145736 | tf_op jit(solution)/shard_map/ppermute | solution.py:627
  210.1 44.9 %collective-permute-start.8 = (bf16[256,2048]{0,1:T(8,128)(2,1)}, bf16[256,2048]{0,1:T(8,128)(2,1)S(1)}, u32[]{:S(2)}, u32[]{:S(2)}) collective-permute-start(bf16[256,2048]{0,1:T(8,128)(2,1)} %get-tuple-element.143), channel_id=1, source_target_pairs={{0,3},{1,2},{2,1},{3,0},{16,19},{17,18},{18,17},{19,16},{32,35},{3... | collective-permute-start | bytes 3145736 | tf_op jit(solution)/shard_map/ppermute | solution.py:627
  212.5 43.7 %collective-permute-start.9 = (bf16[256,2048]{0,1:T(8,128)(2,1)S(1)}, bf16[256,2048]{0,1:T(8,128)(2,1)S(1)}, u32[]{:S(2)}, u32[]{:S(2)}) collective-permute-start(bf16[256,2048]{0,1:T(8,128)(2,1)S(1)} %get-tuple-element.142), channel_id=1, source_target_pairs={{0,67},{1,66},{2,65},{3,64},{16,83},{17,82},{18,81},{19,80},{32,99... | collective-permute-start | bytes 3145736 | tf_op jit(solution)/shard_map/ppermute | solution.py:627
  326.0 76.7 %copy-start.5 = (f32[1024,1024]{0,1:T(8,128)S(1)}, f32[1024,1024]{0,1:T(8,128)}, u32[]{:S(2)}) copy-start(f32[1024,1024]{0,1:T(8,128)} %copy-done.4) | copy-start | bytes 12582916
  420.7 132.6 %collective-permute-start.17 = (bf16[528,512]{1,0:T(8,128)(2,1)}, bf16[528,512]{1,0:T(8,128)(2,1)}, u32[]{:S(2)}, u32[]{:S(2)}) collective-permute-start(bf16[528,512]{1,0:T(8,128)(2,1)} %get-tuple-element.139), channel_id=1, source_target_pairs={{0,3},{1,2},{2,1},{3,0},{16,19},{17,18},{18,17},{19,16},{32,35},{3... | collective-permute-start | bytes 1622024 | tf_op jit(solution)/shard_map/ppermute | solution.py:627
  422.1 131.2 %collective-permute-start.16 = (bf16[528,512]{1,0:T(8,128)(2,1)}, bf16[528,512]{1,0:T(8,128)(2,1)}, u32[]{:S(2)}, u32[]{:S(2)}) collective-permute-start(bf16[528,512]{1,0:T(8,128)(2,1)} %get-tuple-element.140), channel_id=1, source_target_pairs={{0,2},{1,3},{2,0},{3,1},{16,18},{17,19},{18,16},{19,17},{32,34},{3... | collective-permute-start | bytes 1622024 | tf_op jit(solution)/shard_map/ppermute | solution.py:627
  422.8 130.5 %collective-permute-start.15 = (bf16[528,512]{1,0:T(8,128)(2,1)}, bf16[528,512]{1,0:T(8,128)(2,1)}, u32[]{:S(2)}, u32[]{:S(2)}) collective-permute-start(bf16[528,512]{1,0:T(8,128)(2,1)} %get-tuple-element.141), channel_id=1, source_target_pairs={{0,1},{1,0},{2,3},{3,2},{16,17},{17,16},{18,19},{19,18},{32,33},{3... | collective-permute-start | bytes 1622024 | tf_op jit(solution)/shard_map/ppermute | solution.py:627
  555.1 54.2 %collective-permute-start.20 = (bf16[528,512]{1,0:T(8,128)(2,1)S(1)}, bf16[528,512]{1,0:T(8,128)(2,1)S(1)}, u32[]{:S(2)}, u32[]{:S(2)}) collective-permute-start(bf16[528,512]{1,0:T(8,128)(2,1)S(1)} %get-tuple-element.136), channel_id=1, source_target_pairs={{0,48},{16,0},{32,16},{48,32},{64,112},{80,64},{96,80},{112,96},{1... | collective-permute-start | bytes 1622024 | tf_op jit(solution)/shard_map/ppermute | solution.py:686
  567.3 42.0 %collective-permute-start.19 = (bf16[528,512]{1,0:T(8,128)(2,1)S(1)}, bf16[528,512]{1,0:T(8,128)(2,1)S(1)}, u32[]{:S(2)}, u32[]{:S(2)}) collective-permute-start(bf16[528,512]{1,0:T(8,128)(2,1)S(1)} %get-tuple-element.137), channel_id=1, source_target_pairs={{0,32},{16,48},{32,0},{48,16},{64,96},{80,112},{96,64},{112,80},{1... | collective-permute-start | bytes 1622024 | tf_op jit(solution)/shard_map/ppermute | solution.py:686
  567.3 42.0 %collective-permute-start.18 = (bf16[528,512]{1,0:T(8,128)(2,1)S(1)}, bf16[528,512]{1,0:T(8,128)(2,1)S(1)}, u32[]{:S(2)}, u32[]{:S(2)}) collective-permute-start(bf16[528,512]{1,0:T(8,128)(2,1)S(1)} %get-tuple-element.135), channel_id=1, source_target_pairs={{0,16},{16,32},{32,48},{48,0},{64,80},{80,96},{96,112},{112,64},{1... | collective-permute-start | bytes 1622024 | tf_op jit(solution)/shard_map/ppermute | solution.py:686
  609.6 14.5 %collective-permute-start.21 = (bf16[528,512]{1,0:T(8,128)(2,1)S(1)}, bf16[528,512]{1,0:T(8,128)(2,1)S(1)}, u32[]{:S(2)}, u32[]{:S(2)}) collective-permute-start(bf16[528,512]{1,0:T(8,128)(2,1)S(1)} %fusion.34), channel_id=1, source_target_pairs={{0,64},{16,80},{32,96},{48,112},{64,0},{80,16},{96,32},{112,48},{1... | collective-permute-start | bytes 1622024 | tf_op jit(solution)/shard_map/ppermute | solution.py:686
  624.2 16.7 %collective-permute-start.24 = (bf16[528,512]{1,0:T(8,128)(2,1)S(1)}, bf16[528,512]{1,0:T(8,128)(2,1)}, u32[]{:S(2)}, u32[]{:S(2)}) collective-permute-start(bf16[528,512]{1,0:T(8,128)(2,1)S(1)} %add_convert_fusion), channel_id=1, source_target_pairs={{0,48},{16,0},{32,16},{48,32},{64,112},{80,64},{96,80},{112,96},{1... | collective-permute-start | bytes 1622024 | tf_op jit(solution)/shard_map/ppermute | solution.py:686
  626.2 36.5 %collective-permute-start.23 = (bf16[528,512]{1,0:T(8,128)(2,1)S(1)}, bf16[528,512]{1,0:T(8,128)(2,1)}, u32[]{:S(2)}, u32[]{:S(2)}) collective-permute-start(bf16[528,512]{1,0:T(8,128)(2,1)S(1)} %add_convert_fusion), channel_id=1, source_target_pairs={{0,32},{16,48},{32,0},{48,16},{64,96},{80,112},{96,64},{112,80},{1... | collective-permute-start | bytes 1622024 | tf_op jit(solution)/shard_map/ppermute | solution.py:686
  628.3 48.5 %collective-permute-start.22 = (bf16[528,512]{1,0:T(8,128)(2,1)S(1)}, bf16[528,512]{1,0:T(8,128)(2,1)}, u32[]{:S(2)}, u32[]{:S(2)}) collective-permute-start(bf16[528,512]{1,0:T(8,128)(2,1)S(1)} %add_convert_fusion), channel_id=1, source_target_pairs={{0,16},{16,32},{32,48},{48,0},{64,80},{80,96},{96,112},{112,64},{1... | collective-permute-start | bytes 1622024 | tf_op jit(solution)/shard_map/ppermute | solution.py:686
  628.3 56.2 %collective-permute-start.25 = (bf16[1056,512]{1,0:T(8,128)(2,1)}, bf16[1056,512]{1,0:T(8,128)(2,1)}, u32[]{:S(2)}, u32[]{:S(2)}) collective-permute-start(bf16[1056,512]{1,0:T(8,128)(2,1)} %bitcast.269), channel_id=1, source_target_pairs={{0,0},{1,33},{2,66},{3,99},{16,1},{17,32},{18,67},{19,98},{32,2},{... | collective-permute-start | bytes 3244040 | tf_op jit(solution)/shard_map/ppermute | solution.py:995
  (82 other events, 404.6 us)
Sparse Core Ops, SparseCore 0:
  321.8 143.3 reduce-scatter.1

commit v3 on v2

v3 whole, which is shorter than its diff:
```python
import functools
import math

import jax
import jax.numpy as jnp
from jax import lax
from jax.experimental import pallas as pl
from jax.experimental.pallas import tpu as pltpu
from jax.sharding import PartitionSpec as P

D = 2048
NOPE = 128
ROPE = 64
VDIM = 128
RANK = 512
TOPK = 6
EXPERTS = 8
SEQ = 1024

norm_eps = 1e-06
masked_score = -1e30
bf16 = jnp.bfloat16
f32 = jnp.float32
MESH = pl.DeviceIdType.MESH
DMA = pltpu.SemaphoreType.DMA
VMEM = pl.BlockSpec(memory_space=pltpu.VMEM)
HBM = pl.BlockSpec(memory_space=pl.ANY)


def place():
    row = lax.axis_index("row")
    col = lax.axis_index("col")
    sibling = col + 1 - 2 * lax.rem(col, 2)
    across = lax.rem(col + 2, 4)
    return (row, sibling, across, lax.rem(sibling + 2, 4))


def xor(left, right):
    return lax.rem(lax.rem(left, 2) + lax.rem(right, 2), 2) + 2 * lax.rem(left // 2 + right // 2, 2)


def greet(columns, row, others=()):
    barrier = pltpu.get_barrier_semaphore()
    targets = [{"col": column} for column in columns]
    targets += [{"row": lax.rem(row + step, 4)} for step in (1, 2, 3)]
    targets += list(others)
    for target in targets:
        pl.semaphore_signal(barrier, inc=1, device_id=target, device_id_type=MESH)
    pl.semaphore_wait(barrier, len(targets))


def along_z(dp, step):
    return dp // 4 * 4 + lax.rem(lax.rem(dp, 4) + step, 4)


def remote(source, target, sems, at, **device):
    return pltpu.make_async_remote_copy(
        src_ref=source,
        dst_ref=target,
        send_sem=sems[0].at[at],
        recv_sem=sems[1].at[at],
        device_id=device,
        device_id_type=MESH,
    )


def starter(pending):
    def go(*arguments, **device):
        copy = remote(*arguments, **device)
        copy.start()
        pending.append(copy)
        return copy

    return go


def pair(*shape):
    return [DMA(shape), DMA(shape)]


def params(collective):
    return pltpu.CompilerParams(
        collective_id=collective, has_side_effects=True, vmem_limit_bytes=52 << 20
    )


def cost(flops, mebibytes):
    return pl.CostEstimate(flops=flops, bytes_accessed=mebibytes << 20, transcendentals=0)


class Gather:
    def __init__(self, own, full, sems, go, row, sibling, across):
        self.own, self.full, self.go = own, full, go
        self.xs, self.ys, self.cs = sems[0:2], sems[2:4], sems[4:6]
        self.row, self.sibling, self.across = row, sibling, across
        self.arrivals = []

    def block(self, at_row, at_col):
        rows, columns = self.own.shape
        start = pl.multiple_of(at_row * rows, rows)
        return self.full.at[pl.ds(start, rows), pl.ds(at_col * columns, columns)]

    def along(self, source, target, base):
        return [
            self.go(source, target, self.ys, base + k - 1, row=lax.rem(self.row + k, 4))
            for k in (1, 2, 3)
        ]

    def over(self, source, target):
        count = len(self.arrivals)
        self.arrivals.append(self.go(source, target, self.cs, count, col=self.sibling))

    def begin(self):
        row = self.row
        rows, columns = self.own.shape
        self.side = self.go(self.own, self.block(row, 2), self.xs, 0, col=self.across)
        self.first = self.along(self.own, self.block(row, 0), 0)
        self.over(self.own, self.block(row, 1))
        start = pl.multiple_of(row * rows, rows)
        self.full[pl.ds(start, rows), pl.ds(0, columns)] = self.own[...]

    def second(self):
        self.side.wait_recv()
        here = self.block(self.row, 2)
        self.rest = self.along(here, here, 3)
        self.over(here, self.block(self.row, 3))

    def forward(self, group, at_col):
        for k in (1, 3, 2):
            group[k - 1].wait_recv()
            source = lax.rem(self.row + 4 - k, 4)
            self.over(self.block(source, at_col), self.block(source, at_col + 1))

    def forward_first(self):
        self.forward(self.first, 0)

    def forward_rest(self):
        self.forward(self.rest, 2)

    def finish(self):
        for copy in self.arrivals:
            copy.wait_recv()


gather_scratch = pair(1) + pair(6) + pair(8)


class Deal:
    def __init__(self, sems, local_sems, pending, col, peers):
        self.go, self.sems, self.local_sems = starter(pending), sems, local_sems
        self.col, self.peers = col, peers
        self.far = lax.rem(lax.axis_index("dp") + 4, 8)
        self.copies, self.local, self.count = [], [], 0

    def send(self, source, target, flip):
        n = self.count
        self.count += 1
        copy = pltpu.make_async_copy(source(self.col), target(0), self.local_sems.at[n])
        copy.start()
        self.local.append(copy)
        for k, peer in ((2, self.peers[1]), (3, self.peers[2]), (1, self.peers[0])):
            place_at = {"col": peer}
            if flip and k != 1:
                place_at["dp"] = self.far
            self.copies.append(
                self.go(source(peer), target(k), self.sems, (k - 1, n), **place_at)
            )

    def finish(self):
        for copy in self.local:
            copy.wait()
        for copy in self.copies:
            copy.wait_recv()


def deal_scratch(count):
    return pair(3, count) + [DMA((count,))]


def deal_peers(peers):
    far = lax.rem(lax.axis_index("dp") + 4, 8)
    return [{"dp": far, "col": peer} for peer in peers[1:]]


def lanes(array, start, size):
    return lambda k: array.at[pl.ds(start, size), pl.ds(512 * k, 512)]


def rows_at(array, size):
    return lambda column: array.at[pl.ds(pl.multiple_of(column * size, size), size)]


def start_kernel(
    inputs, cotangent, common, query, gate, low_gate, low_up, router, low_down,
    full, out_grad, project, gates, lows, *sems,
):
    row, sibling, across, corner = place()
    col = lax.axis_index("col")
    peers = (sibling, across, corner)
    greet(peers, row, deal_peers(peers))
    pending = []
    go = starter(pending)
    gather = Gather(inputs, full, sems[0:6], go, row, sibling, across)
    beside = Gather(cotangent, out_grad, sems[6:12], go, row, sibling, across)
    deal = Deal(sems[12:14], sems[14], pending, col, peers)
    ff = gate.shape[1]
    low = low_down.shape[0] // 4
    gather.begin()
    deal.send(lambda column: common.at[pl.ds(0, RANK)], lanes(project, 0, RANK), True)
    deal.send(rows_at(query, 192), lanes(project, RANK, 192), False)
    deal.send(lambda column: common.at[pl.ds(RANK, 80)], lanes(project, RANK + 192, 80), False)
    beside.begin()
    gather.second()
    for e in (0, 1):
        deal.send(lambda column, e=e: gate.at[2 * column + e], lanes(gates, e * ff, ff), e == 1)
    beside.second()
    deal.send(rows_at(low_gate, low), lanes(lows, 0, low), True)
    deal.send(rows_at(low_up, low), lanes(lows, low, low), False)
    deal.send(lambda column: router, lanes(lows, 2 * low, 16), True)
    deal.send(rows_at(low_down, low), lanes(lows, 2 * low + 16, low), True)
    gather.forward_first()
    gather.forward_rest()
    beside.forward_first()
    beside.forward_rest()
    gather.finish()
    beside.finish()
    deal.finish()
    for copy in pending:
        copy.wait_send()


def start_step(inputs, cotangent, common, query, gate, low_gate, low_up, router, low_down):
    rows, columns = inputs.shape
    low = low_down.shape[0] // 4
    wide = jax.ShapeDtypeStruct((4 * rows, 4 * columns), bf16)
    return pl.pallas_call(
        start_kernel,
        out_shape=(
            wide,
            wide,
            jax.ShapeDtypeStruct((RANK + 272, 4 * columns), bf16),
            jax.ShapeDtypeStruct((2 * gate.shape[1], 4 * columns), bf16),
            jax.ShapeDtypeStruct((3 * low + 16, 4 * columns), bf16),
        ),
        in_specs=[VMEM] * 2 + [HBM] * 7,
        out_specs=(VMEM, VMEM, HBM, HBM, HBM),
        scratch_shapes=[*gather_scratch, *gather_scratch, *deal_scratch(9)],
        compiler_params=params(0),
        cost_estimate=cost(0, 150),
        name="start_step",
    )(inputs, cotangent, common, query, gate, low_gate, low_up, router, low_down)


def reduce_scratch(rows, columns):
    return [
        pltpu.VMEM((4, 2, rows, columns), bf16),
        pltpu.VMEM((3, 2, rows, columns), bf16),
        pltpu.VMEM((3, 2, rows, columns), bf16),
        pltpu.VMEM((2, rows, columns), f32),
        pltpu.VMEM((2, rows, columns), bf16),
        *pair(1),
        *pair(3, 2),
        *pair(4, 2),
    ]


class Reduction:
    order = (2, 1, 3, 0)

    def __init__(self, part, scratch, row, sibling, across):
        self.part = part
        self.held, self.out_buf, self.in_buf, self.acc, self.side_buf = scratch[:5]
        self.xs, self.ys, self.cs = scratch[5:7], scratch[7:9], scratch[9:11]
        self.row, self.sibling, self.across = row, sibling, across
        self.rows, self.columns = self.acc.shape[1:]

    def rows_of(self, k):
        start = lax.rem(self.row + k, 4) * self.rows
        return pl.ds(pl.multiple_of(start, self.rows), self.rows)

    def pair_copy(self, k, x):
        return remote(
            self.part.at[self.rows_of(k), pl.ds((2 * x + 1) * self.columns, self.columns)],
            self.held.at[k, x],
            self.cs,
            (k, x),
            col=self.sibling,
        )

    def along_copy(self, k, x):
        return remote(
            self.out_buf.at[k - 1, x],
            self.in_buf.at[k - 1, x],
            self.ys,
            (k - 1, x),
            row=lax.rem(self.row + k, 4),
        )

    def side_copy(self):
        return remote(self.side_buf.at[0], self.side_buf.at[1], self.xs, 0, col=self.across)

    def start(self):
        for k in self.order:
            for x in (0, 1):
                self.pair_copy(k, x).start()

    def along(self, order=(2, 1, 3, 0)):
        for k in order:
            for x in (0, 1):
                self.pair_copy(k, x).wait_recv()
                mine = self.part[self.rows_of(k), pl.ds(2 * x * self.columns, self.columns)]
                value = mine.astype(f32) + self.held[k, x].astype(f32)
                if k:
                    self.out_buf[k - 1, x] = value.astype(bf16)
                    self.along_copy(k, x).start()
                else:
                    self.acc[x] = value

    def side(self):
        for x in (1, 0):
            for k in (1, 3, 2):
                self.along_copy(k, x).wait_recv()
                self.acc[x] += self.in_buf[k - 1, x].astype(f32)
            if x:
                self.side_buf[0] = self.acc[1].astype(bf16)
                self.side_copy().start()

    def total(self):
        self.side_copy().wait_recv()
        return self.acc[0] + self.side_buf[1].astype(f32)

    def finish(self):
        for k in self.order:
            for x in (0, 1):
                self.pair_copy(k, x).wait_send()
                if k:
                    self.along_copy(k, x).wait_send()
        self.side_copy().wait_send()


def product(left, right):
    return jnp.dot(left, right, preferred_element_type=f32).astype(bf16)


def times_rows(left, right):
    return lax.dot_general(left, right, (((1,), (1,)), ((), ())), preferred_element_type=f32)


def over_units(left, right):
    return lax.dot_general(left, right, (((0,), (0,)), ((), ())), preferred_element_type=f32)


def expert_kernel(
    middle, out_grad, gates, ups, downs, lows, gain, named, mine, hidden, scale, act, delta
):
    values = middle[...].astype(f32)
    scales = lax.rsqrt(jnp.mean(values * values, axis=1, keepdims=True) + norm_eps)
    scale[...] = jnp.broadcast_to(scales, scale.shape)
    normal = (values * scales * gain[...]).astype(bf16)
    hidden[...] = normal
    upstream = out_grad[...]
    ff = gates.shape[0] // 2
    low = (lows.shape[0] - 16) // 3
    low_pre = times_rows(lows[pl.ds(0, 2 * low + 16), :], normal)
    logits = low_pre[2 * low : 2 * low + EXPERTS]
    powers = jnp.exp(logits - jnp.max(logits, axis=0, keepdims=True))
    probs = powers / jnp.sum(powers, axis=0, keepdims=True)
    names = named[...]
    probs_part = jnp.zeros_like(probs)
    for e in range(3):
        if e < 2:
            size, at = ff, pl.ds(e * ff, ff)
            gate_pre = times_rows(gates[at, :], normal)
            up_pre = times_rows(ups[at, :], normal)
            act_grad = times_rows(downs[at, :], upstream)
            own = mine[:, e : e + 1]
            weight = jnp.sum(probs * names * own, axis=0, keepdims=True)
            gate_at, up_at, act_at = e * ff, (2 + e) * ff, e * ff
        else:
            size = low
            gate_pre, up_pre = low_pre[:low], low_pre[low : 2 * low]
            act_grad = times_rows(lows[pl.ds(2 * low + 16, low), :], upstream)
            weight = 1.0
            gate_at, up_at, act_at = 4 * ff, 4 * ff + low, 2 * ff
        sig = 1.0 / (1.0 + jnp.exp(-gate_pre))
        silu = gate_pre * sig
        both = silu * up_pre
        act[pl.ds(act_at, size), :] = (weight * both).astype(bf16)
        weighted = weight * act_grad
        delta[pl.ds(gate_at, size), :] = (
            weighted * up_pre * (sig * (1.0 + gate_pre * (1.0 - sig)))
        ).astype(bf16)
        delta[pl.ds(up_at, size), :] = (weighted * silu).astype(bf16)
        if e < 2:
            named_sum = jnp.sum(act_grad * both, axis=0, keepdims=True)
            probs_part = probs_part + named_sum * own * names
    logits_part = probs * (probs_part - jnp.sum(probs * probs_part, axis=0, keepdims=True))
    delta[pl.ds(4 * ff + 2 * low, 16), :] = jnp.concatenate(
        [logits_part, jnp.zeros_like(logits_part)], axis=0
    ).astype(bf16)


def whole(value):
    return pl.BlockSpec(value.shape, lambda i: (0,) * len(value.shape))


def expert_step(middle, out_grad, gates, ups, downs, lows, gain, named, mine):
    tile = 256
    tokens, width = middle.shape
    wide = pl.BlockSpec((tile, width), lambda i: (i, 0))

    def tall(rows):
        return pl.BlockSpec((rows, tile), lambda i: (0, i))

    acts = downs.shape[0] + (lows.shape[0] - 16) // 3
    deltas = gates.shape[0] + ups.shape[0] + 2 * (lows.shape[0] - 16) // 3 + 16
    return pl.pallas_call(
        expert_kernel,
        grid=(tokens // tile,),
        out_shape=(
            jax.ShapeDtypeStruct((tokens, width), bf16),
            jax.ShapeDtypeStruct((tokens, 128), f32),
            jax.ShapeDtypeStruct((acts, tokens), bf16),
            jax.ShapeDtypeStruct((deltas, tokens), bf16),
        ),
        in_specs=[
            wide,
            wide,
            whole(gates),
            whole(ups),
            whole(downs),
            whole(lows),
            whole(gain),
            tall(EXPERTS),
            whole(mine),
        ],
        out_specs=(
            wide,
            pl.BlockSpec((tile, 128), lambda i: (i, 0)),
            tall(acts),
            tall(deltas),
        ),
        compiler_params=pltpu.CompilerParams(vmem_limit_bytes=56 << 20),
        cost_estimate=cost(2 * 5 * gates.shape[0] * width * tokens, 30),
        name="expert_step",
    )(middle, out_grad, gates, ups, downs, lows, gain, named, mine)


def back_kernel(act, delta, gates, ups, downs, lows, combined, hidden_grad):
    ff = gates.shape[0]
    low = (lows.shape[0] - 16) // 3
    combined[...] = (
        over_units(act[pl.ds(0, ff), :], downs[...])
        + over_units(act[pl.ds(ff, low), :], lows[pl.ds(2 * low + 16, low), :])
    ).astype(bf16)
    hidden_grad[...] = (
        over_units(delta[pl.ds(0, ff), :], gates[...])
        + over_units(delta[pl.ds(ff, ff), :], ups[...])
        + over_units(delta[pl.ds(2 * ff, 2 * low + 16), :], lows[pl.ds(0, 2 * low + 16), :])
    ).astype(bf16)


def back_step(act, delta, gates, ups, downs, lows):
    tile = 256
    tokens, width = act.shape[1], gates.shape[1]
    wide = pl.BlockSpec((tile, width), lambda i: (i, 0))
    return pl.pallas_call(
        back_kernel,
        grid=(tokens // tile,),
        out_shape=(jax.ShapeDtypeStruct((tokens, width), bf16),) * 2,
        in_specs=[
            pl.BlockSpec((act.shape[0], tile), lambda i: (0, i)),
            pl.BlockSpec((delta.shape[0], tile), lambda i: (0, i)),
            whole(gates),
            whole(ups),
            whole(downs),
            whole(lows),
        ],
        out_specs=(wide, wide),
        compiler_params=pltpu.CompilerParams(vmem_limit_bytes=56 << 20),
        cost_estimate=cost(2 * 4 * gates.shape[0] * width * tokens, 30),
        name="back_step",
    )(act, delta, gates, ups, downs, lows)


def grads_kernel(hidden, out_grad, delta, act, grads, *, ff):
    for e in (0, 1):

        @pl.when(pl.program_id(0) // 4 == e)
        def _(e=e):
            at = e * ff
            grads[0, pl.ds(0, ff), :] = product(delta[pl.ds(at, ff), :], hidden[...])
            grads[0, pl.ds(ff, ff), :] = product(delta[pl.ds(2 * ff + at, ff), :], hidden[...])
            grads[0, pl.ds(2 * ff, ff), :] = product(act[pl.ds(at, ff), :], out_grad[...])


def grads_step(hidden, out_grad, delta, act, ff):
    tokens = hidden.shape[0]
    wide = pl.BlockSpec((tokens, 512), lambda i: (0, i % 4))
    return pl.pallas_call(
        functools.partial(grads_kernel, ff=ff),
        grid=(8,),
        out_shape=jax.ShapeDtypeStruct((8, 3 * ff, 512), bf16),
        in_specs=[wide, wide, whole(delta), whole(act)],
        out_specs=pl.BlockSpec((1, 3 * ff, 512), lambda i: (i, 0, 0)),
        compiler_params=pltpu.CompilerParams(vmem_limit_bytes=56 << 20),
        cost_estimate=cost(2 * 8 * 3 * ff * 512 * tokens, 30),
        name="grads_step",
    )(hidden, out_grad, delta, act)


def shared_kernel(hidden, out_grad, delta, act, grads, router, *, ff, low):
    base = 4 * ff
    grads[0, pl.ds(0, low), :] = product(delta[pl.ds(base, low), :], hidden[...])
    grads[0, pl.ds(low, low), :] = product(delta[pl.ds(base + low, low), :], hidden[...])
    router[...] = product(delta[pl.ds(base + 2 * low, 16), :], hidden[...])
    grads[0, pl.ds(2 * low, low), :] = product(act[pl.ds(2 * ff, low), :], out_grad[...])


def shared_step(hidden, out_grad, delta, act, ff, low):
    tokens = hidden.shape[0]
    wide = pl.BlockSpec((tokens, 512), lambda i: (0, i))
    return pl.pallas_call(
        functools.partial(shared_kernel, ff=ff, low=low),
        grid=(4,),
        out_shape=(
            jax.ShapeDtypeStruct((4, 3 * low, 512), bf16),
            jax.ShapeDtypeStruct((16, D), bf16),
        ),
        in_specs=[wide, wide, whole(delta), whole(act)],
        out_specs=(
            pl.BlockSpec((1, 3 * low, 512), lambda i: (i, 0, 0)),
            pl.BlockSpec((16, 512), lambda i: (0, i)),
        ),
        compiler_params=pltpu.CompilerParams(vmem_limit_bytes=56 << 20),
        cost_estimate=cost(2 * 4 * 3 * low * 512 * tokens, 15),
        name="shared_step",
    )(hidden, out_grad, delta, act)


class ColumnSum:
    def __init__(self, value, buf, sems, go, peers):
        self.buf, self.own = buf, value
        buf[0] = jnp.broadcast_to(value, buf.shape[1:])
        self.sent = [
            go(buf.at[0], buf.at[k + 1], sems, k, col=peer) for k, peer in enumerate(peers)
        ]

    def total(self):
        for copy in self.sent:
            copy.wait_recv()
        buf = self.buf
        return ((buf[0] + buf[1]) + (buf[2] + buf[3]))[:, :1]


def middle_kernel(
    part, combined, middle, cotangent, scale, gain, weight, shared,
    residual_grad, residual_rows, attended_grad, gain_part, shared_sum, output,
    sum_buf, out_buf, in_buf, acc, chunk_in, ss, sr, rs, rr, hs, hr, ps, pr, *scratch,
):
    row, sibling, across, corner = place()
    dp = lax.axis_index("dp")
    z = lax.rem(dp, 4)
    far = lax.rem(dp + 4, 8)
    peers = (sibling, across, corner)
    greet(peers, row, [{"dp": along_z(dp, k)} for k in (1, 2, 3)] + [{"dp": far}])
    pending = []
    go = starter(pending)
    count = len(scratch) // 2
    steps = Reduction(part, scratch[:count], row, sibling, across)
    beside = Reduction(combined, scratch[count:], row, sibling, across)
    rows, columns = middle.shape
    head = attended_grad.shape[1]
    steps.start()
    scattered = [
        go(
            shared.at[lax.rem(z + k, 4)], chunk_in.at[k - 1], (ps, pr), k - 1, dp=along_z(dp, k)
        )
        for k in (1, 2, 3)
    ]
    steps.along()
    beside.start()
    steps.side()
    upstream = steps.total()
    weighted = upstream * gain[...]
    values = middle[...]
    scales = scale[...]
    inner = ColumnSum(
        jnp.sum(weighted * values, axis=1, keepdims=True), sum_buf, (ss, sr), go, peers
    )
    gain_part[...] = jnp.sum(upstream * values * scales, axis=0, keepdims=True)
    base = cotangent[...].astype(f32) + scales * weighted
    grad = base - values * (scales * scales * scales * inner.total() / D)
    residual_grad[...] = grad

    def block(at_row):
        return pl.ds(pl.multiple_of(at_row * rows, rows), rows)

    residual_rows[block(row), :] = grad.astype(bf16)
    sent = [
        go(
            residual_rows.at[block(row)],
            residual_rows.at[block(row)],
            (rs, rr),
            k - 1,
            row=lax.rem(row + k, 4),
        )
        for k in (1, 2, 3)
    ]
    beside.along()
    got = []
    for k in (0, 1, 3, 2):
        source = lax.rem(row + 4 - k, 4)
        if k:
            sent[k - 1].wait_recv()
        result = times_rows(residual_rows[block(source), :], weight[...])
        acc[block(source), :] = result[:, :head]
        for j, peer in enumerate(peers):
            out_buf[j, block(source), :] = result[:, (j + 1) * head : (j + 2) * head].astype(bf16)
            got.append(
                go(
                    out_buf.at[j, block(source)],
                    in_buf.at[j, block(source)],
                    (hs, hr),
                    (j, k),
                    col=peer,
                )
            )
    total = shared[z].astype(f32)
    for k in (1, 2, 3):
        scattered[k - 1].wait_recv()
        total += chunk_in[k - 1].astype(f32)
    chunk_in[3] = total.astype(bf16)
    halves = go(chunk_in.at[3], chunk_in.at[4], (ps, pr), 3, dp=far)
    beside.side()
    for copy in got:
        copy.wait_recv()
    attended_grad[...] = (
        acc[...] + in_buf[0].astype(f32) + in_buf[1].astype(f32) + in_buf[2].astype(f32)
    ).astype(bf16)
    output[...] = (beside.total() + values).astype(bf16)
    halves.wait_recv()
    shared_sum[...] = (chunk_in[3].astype(f32) + chunk_in[4].astype(f32)).astype(bf16)
    for copy in pending:
        copy.wait_send()
    steps.finish()
    beside.finish()


def middle_step(part, combined, middle, cotangent, scale, gain, weight, shared):
    rows, columns = middle.shape
    piece = shared.shape[1]
    return pl.pallas_call(
        middle_kernel,
        out_shape=(
            jax.ShapeDtypeStruct((rows, columns), f32),
            jax.ShapeDtypeStruct((4 * rows, columns), bf16),
            jax.ShapeDtypeStruct((4 * rows, VDIM), bf16),
            jax.ShapeDtypeStruct((1, columns), f32),
            jax.ShapeDtypeStruct((piece, columns), bf16),
            jax.ShapeDtypeStruct((rows, columns), bf16),
        ),
        in_specs=[VMEM] * 8,
        out_specs=(VMEM,) * 6,
        scratch_shapes=[
            pltpu.VMEM((4, rows, 128), f32),
            pltpu.VMEM((3, 4 * rows, VDIM), bf16),
            pltpu.VMEM((3, 4 * rows, VDIM), bf16),
            pltpu.VMEM((4 * rows, VDIM), f32),
            pltpu.VMEM((5, piece, columns), bf16),
            *pair(3),
            *pair(3),
            *pair(3, 4),
            *pair(4),
            *reduce_scratch(rows, columns),
            *reduce_scratch(rows, columns),
        ],
        compiler_params=params(3),
        cost_estimate=cost(1 << 29, 200),
        name="middle_step",
    )(part, combined, middle, cotangent, scale, gain, weight, shared)


def tail_kernel(
    part, query, ready, residual_grad, inputs, scale, gain, gain_part, shared_sum,
    inputs_grad, sums, narrow, gains, latent_gain, shared_all,
    chunk_in, all_parts, narrow_all, lat_buf, lat_half, sum_buf,
    qs, qr, ps, pr, as_, ar, ls, lr, ns, nr, ss, sr, gs, gr, ws, wr, *scratch,
):
    row, sibling, across, corner = place()
    col = lax.axis_index("col")
    dp = lax.axis_index("dp")
    z = lax.rem(dp, 4)
    far = lax.rem(dp + 4, 8)
    peers = (sibling, across, corner)
    others = [{"dp": along_z(dp, k)} for k in (1, 2, 3)] + [{"dp": far}]
    others += [
        {"dp": along_z(dp, 4 - k), "col": xor(col, lax.rem(z + 4 - k, 4))} for k in (1, 2, 3)
    ]
    greet(peers, row, others)
    pending = []
    go = starter(pending)
    steps = Reduction(part, scratch, row, sibling, across)
    rows, columns = inputs.shape
    piece = query.shape[0]
    lat = narrow_all.shape[1]

    def head(at):
        return pl.ds(pl.multiple_of(at * piece, piece), piece)

    def chunk(at):
        return pl.ds(pl.multiple_of(at * 2 * piece, 2 * piece), 2 * piece)

    steps.start()
    dealt = [
        go(
            query.at[:, pl.ds((j + 1) * columns, columns)],
            all_parts.at[head(4 + col)],
            (qs, qr),
            j,
            col=peer,
        )
        for j, peer in enumerate(peers)
    ]
    all_parts[pl.ds(0, 4 * piece), :] = ready[...]
    all_parts[head(4 + col), :] = query[:, pl.ds(0, columns)]
    goal = xor(col, z)
    spread_shared = [
        go(shared_sum, shared_all.at[z], (ws, wr), k - 1, dp=along_z(dp, k), col=goal)
        for k in (1, 2, 3)
    ]

    def own_block():
        return remote(shared_sum, shared_all.at[z], (ws, wr), 3, col=goal)

    @pl.when(z == 0)
    def _():
        shared_all[0] = shared_sum[...]

    @pl.when(z != 0)
    def _():
        own_block().start()

    steps.along()
    for copy in dealt:
        copy.wait_recv()
    scattered = [
        go(
            all_parts.at[chunk(lax.rem(z + k, 4))],
            chunk_in.at[k - 1],
            (ps, pr),
            k - 1,
            dp=along_z(dp, k),
        )
        for k in (1, 2, 3)
    ]
    steps.side()
    total = all_parts[chunk(z), :].astype(f32)
    for k in (1, 2, 3):
        scattered[k - 1].wait_recv()
        total += chunk_in[k - 1].astype(f32)
    chunk_in[3] = total.astype(bf16)
    halves = go(chunk_in.at[3], chunk_in.at[4], (ps, pr), 3, dp=far)
    whole = steps.total()
    upstream = whole[:rows]
    weighted = upstream * gain[...]
    values = inputs[...].astype(f32)
    scales = scale[...]
    inner = ColumnSum(
        jnp.sum(weighted * values, axis=1, keepdims=True), sum_buf, (ss, sr), go, peers
    )
    first_part = jnp.sum(upstream * values * scales, axis=0, keepdims=True)
    extra = jnp.concatenate([first_part, gain_part[...], jnp.zeros((14, columns), f32)], axis=0)
    lat_buf[z] = jnp.concatenate([whole[rows:], extra], axis=0).astype(bf16)
    along = [
        go(lat_buf.at[z], lat_buf.at[z], (ls, lr), k - 1, dp=along_z(dp, k)) for k in (1, 2, 3)
    ]
    halves.wait_recv()
    sums[chunk(z), :] = (chunk_in[3].astype(f32) + chunk_in[4].astype(f32)).astype(bf16)
    shared = [
        go(sums.at[chunk(z)], sums.at[chunk(z)], (as_, ar), k - 1, dp=along_z(dp, k))
        for k in (1, 2, 3)
    ]
    for copy in along:
        copy.wait_recv()
    lat_half[0] = (
        (lat_buf[0].astype(f32) + lat_buf[1].astype(f32))
        + (lat_buf[2].astype(f32) + lat_buf[3].astype(f32))
    ).astype(bf16)
    other = go(lat_half.at[0], lat_half.at[1], (ls, lr), 3, dp=far)
    inputs_grad[...] = (
        residual_grad[...]
        + scales * weighted
        - values * (scales * scales * scales * inner.total() / D)
    ).astype(bf16)
    other.wait_recv()
    narrow_all[row] = (lat_half[0].astype(f32) + lat_half[1].astype(f32)).astype(bf16)
    spread = [
        go(narrow_all.at[row], narrow_all.at[row], (ns, nr), k - 1, row=lax.rem(row + k, 4))
        for k in (1, 2, 3)
    ]
    for copy in spread:
        copy.wait_recv()
    keep = lat - 32
    narrow[...] = narrow_all[:, :keep, :]
    latent_gain[col] = narrow_all[0, pl.ds(keep, 16), :]
    last = [
        go(latent_gain.at[col], latent_gain.at[col], (gs, gr), j, col=peer)
        for j, peer in enumerate(peers)
    ]
    edge = pl.ds(keep + 16, 16)
    gains[...] = (
        narrow_all[0, edge, :].astype(f32)
        + narrow_all[1, edge, :].astype(f32)
        + narrow_all[2, edge, :].astype(f32)
        + narrow_all[3, edge, :].astype(f32)
    )
    for copy in last + shared + spread_shared:
        copy.wait_recv()

    @pl.when(z != 0)
    def _():
        own_block().wait()

    for copy in pending:
        copy.wait_send()
    steps.finish()


def tail_step(part, query, ready, residual_grad, inputs, scale, gain, gain_part, shared_sum):
    rows, columns = inputs.shape
    piece = query.shape[0]
    all_rows = part.shape[0] // 4
    lat = all_rows - rows + 16
    return pl.pallas_call(
        tail_kernel,
        out_shape=(
            jax.ShapeDtypeStruct((rows, columns), bf16),
            jax.ShapeDtypeStruct((8 * piece, columns), bf16),
            jax.ShapeDtypeStruct((4, lat - 32, columns), bf16),
            jax.ShapeDtypeStruct((16, columns), f32),
            jax.ShapeDtypeStruct((4, 16, columns), bf16),
            jax.ShapeDtypeStruct((4,) + shared_sum.shape, bf16),
        ),
        in_specs=[VMEM] * 9,
        out_specs=(VMEM,) * 6,
        scratch_shapes=[
            pltpu.VMEM((5, 2 * piece, columns), bf16),
            pltpu.VMEM((8 * piece, columns), bf16),
            pltpu.VMEM((4, lat, columns), bf16),
            pltpu.VMEM((4, lat, columns), bf16),
            pltpu.VMEM((2, lat, columns), bf16),
            pltpu.VMEM((4, rows, 128), f32),
            *pair(3),
            *pair(4),
            *pair(3),
            *pair(4),
            *pair(3),
            *pair(3),
            *pair(3),
            *pair(4),
            *reduce_scratch(all_rows, columns),
        ],
        compiler_params=params(4),
        cost_estimate=cost(1 << 20, 200),
        name="tail_step",
    )(part, query, ready, residual_grad, inputs, scale, gain, gain_part, shared_sum)


def front_kernel(
    attended, weight, inputs, up, down, middle, full, attended_rows, ups, downs,
    own, out_buf, in_buf, acc, as_, ar, ps, pr, *sems,
):
    row, sibling, across, corner = place()
    peers = (sibling, across, corner)
    greet(peers, row, deal_peers(peers))
    pending = []
    go = starter(pending)
    rows, columns = inputs.shape
    head = attended.shape[1]
    order = (2, 1, 3, 0)

    def block(k):
        return pl.ds(pl.multiple_of(lax.rem(row + k, 4) * rows, rows), rows)

    def slot(k):
        return pl.ds(k * head, head)

    got = {}
    for k in order:
        got[2, k] = go(
            attended.at[block(k)], attended_rows.at[block(k), slot(2)], (as_, ar), (1, k), col=across
        )
    for k in order:
        got[1, k] = go(
            attended.at[block(k)], attended_rows.at[block(k), slot(1)], (as_, ar), (0, k), col=sibling
        )
    attended_rows[:, slot(0)] = attended[...]
    deal = Deal(sems[6:8], sems[8], pending, lax.axis_index("col"), peers)
    ff = up.shape[1]
    for k in order:
        got[2, k].wait_recv()
        view = attended_rows.at[block(k), slot(2)]
        got[3, k] = go(
            view, attended_rows.at[block(k), slot(3)], (as_, ar), (2, k), col=sibling
        )
    for e in (0, 1):
        deal.send(lambda column, e=e: up.at[2 * column + e], lanes(ups, e * ff, ff), e == 1)
        deal.send(lambda column, e=e: down.at[2 * column + e], lanes(downs, e * ff, ff), e == 1)
    sent = {}
    for k in order:
        got[1, k].wait_recv()
        got[3, k].wait_recv()
        product = jnp.dot(attended_rows[block(k), :], weight[...], preferred_element_type=f32)
        if k:
            out_buf[k - 1] = product.astype(bf16)
            sent[k] = go(
                out_buf.at[k - 1], in_buf.at[k - 1], (ps, pr), k - 1, row=lax.rem(row + k, 4)
            )
        else:
            acc[...] = product + inputs[...].astype(f32)
    total = acc[...]
    for k in (1, 3, 2):
        sent[k].wait_recv()
        total += in_buf[k - 1].astype(f32)
    middle[...] = total
    own[...] = total.astype(bf16)
    gather = Gather(own, full, sems[:6], go, row, sibling, across)
    gather.begin()
    gather.second()
    gather.forward_first()
    gather.forward_rest()
    gather.finish()
    deal.finish()
    for copy in pending:
        copy.wait_send()


def front_step(attended, weight, inputs, up, down):
    rows, columns = inputs.shape
    dealt = jax.ShapeDtypeStruct((2 * up.shape[1], 4 * columns), bf16)
    return pl.pallas_call(
        front_kernel,
        out_shape=(
            jax.ShapeDtypeStruct((rows, columns), f32),
            jax.ShapeDtypeStruct((4 * rows, 4 * columns), bf16),
            jax.ShapeDtypeStruct((4 * rows, columns), bf16),
            dealt,
            dealt,
        ),
        in_specs=[VMEM] * 3 + [HBM] * 2,
        out_specs=(VMEM,) * 3 + (HBM,) * 2,
        scratch_shapes=[
            pltpu.VMEM((rows, columns), bf16),
            pltpu.VMEM((3, rows, columns), bf16),
            pltpu.VMEM((3, rows, columns), bf16),
            pltpu.VMEM((rows, columns), f32),
            *pair(3, 4),
            *pair(3),
            *gather_scratch,
            *deal_scratch(4),
        ],
        compiler_params=params(5),
        cost_estimate=cost(1 << 29, 150),
        name="front_step",
    )(attended, weight, inputs, up, down)


def dot(spec, left, right, kind=f32):
    return jnp.einsum(spec, left, right, preferred_element_type=f32).astype(kind)


def rotary_tables(length, half_width):
    position = jnp.arange(length, dtype=f32)[:, None]
    frequency = jnp.exp(jnp.arange(half_width, dtype=f32) * (-math.log(10000.0) / half_width))
    angles = position * frequency[None, :]
    return (jnp.cos(angles), jnp.sin(angles))


def rotate(values, cos_table, sin_table):
    half_width = cos_table.shape[-1]
    first_half = values[..., :half_width]
    second_half = values[..., half_width:]
    return jnp.concatenate(
        [
            first_half * cos_table - second_half * sin_table,
            second_half * cos_table + first_half * sin_table,
        ],
        axis=-1,
    )


def pad_to(values, axis, size):
    widths = [(0, 0)] * values.ndim
    widths[axis] = (0, size - values.shape[axis])
    return jnp.pad(values, widths)


def visible_mask(offset, block_rows, prefix_len):
    query_pos = offset + jnp.arange(block_rows, dtype=jnp.int32)
    key_pos = jnp.arange(SEQ, dtype=jnp.int32)
    return (key_pos[None, :] <= query_pos[:, None]) | (key_pos[None, :] < prefix_len)


def attend_forward(queries, key_rows, value_rows, prefix_len):
    score_scale = (NOPE + ROPE) ** (-0.5)
    scores = dot("qd,kd->qk", queries, key_rows) * score_scale
    scores = jnp.where(visible_mask(0, SEQ, prefix_len), scores, masked_score)
    top_score = jnp.max(scores, axis=1, keepdims=True)
    exp_scores = jnp.exp(scores - top_score)
    row_total = jnp.sum(exp_scores, axis=1, keepdims=True)
    weights = (exp_scores / row_total).astype(bf16)
    result = dot("qk,kd->qd", weights, value_rows)
    return (result, (top_score + jnp.log(row_total))[:, 0])


def attend_backward(queries, key_rows, value_rows, log_total, out_grad, prefix_len):
    score_scale = (NOPE + ROPE) ** (-0.5)
    scores = dot("qd,kd->qk", queries, key_rows) * score_scale
    scores = jnp.where(visible_mask(0, SEQ, prefix_len), scores, masked_score)
    weights = jnp.exp(scores - log_total[:, None])
    value_grad = dot("qk,qd->kd", weights.astype(bf16), out_grad)
    weight_grad = dot("qd,kd->qk", out_grad, value_rows)
    centre = jnp.sum(weights * weight_grad, axis=1, keepdims=True)
    score_grad = (weights * (weight_grad - centre)).astype(bf16)
    query_grad = dot("qk,kd->qd", score_grad, key_rows) * score_scale
    key_grad = dot("qk,qd->kd", score_grad, queries) * score_scale
    return (query_grad, key_grad, value_grad)


def on_device(
    inputs,
    attention_gain,
    query_weight,
    latent_weight,
    latent_gain,
    expand_weight,
    output_weight,
    feedforward_gain,
    router_weight,
    shared_gate,
    shared_up,
    shared_down,
    expert_gate,
    expert_up,
    expert_down,
    routes,
    prefix,
    cotangent,
):
    row = lax.axis_index("row")
    col = lax.axis_index("col")
    prefix_len = prefix[0]
    cos_table, sin_table = rotary_tables(SEQ, ROPE // 2)
    first_gain = attention_gain.astype(f32)
    second_gain = feedforward_gain.astype(f32)
    compact_gain = latent_gain.astype(f32)
    residual_in = inputs.astype(f32)
    rows = inputs.shape[0]
    ff = expert_gate.shape[2]
    low = shared_down.shape[0] // 4

    gains = jnp.stack([attention_gain, feedforward_gain])
    common = jnp.concatenate([latent_weight.T, pad_to(gains, 0, 16)], axis=0)
    input_rows, out_grad, project_all, gates, lows = start_step(
        inputs,
        cotangent,
        common,
        query_weight.T,
        expert_gate.transpose(0, 2, 1),
        shared_gate.T,
        shared_up.T,
        pad_to(router_weight.T, 0, 16),
        shared_down,
    )
    project_weight = project_all[: RANK + 256]
    first_all = project_all[RANK + 256].astype(f32)
    second_all = project_all[RANK + 257].astype(f32)
    out_weight = jnp.concatenate(
        [lax.dynamic_slice_in_dim(output_weight, (col ^ k) * VDIM, VDIM, 0) for k in range(4)],
        axis=0,
    )
    order = col ^ jnp.arange(4, dtype=jnp.int32)

    input_rows = input_rows.astype(f32)
    scale_one = lax.rsqrt(jnp.mean(input_rows * input_rows, axis=1) + norm_eps)
    normed = (input_rows * scale_one[:, None] * first_all[None, :]).astype(bf16)
    projected = dot("td,qd->tq", normed, project_weight)
    content = projected[:, :RANK]
    latent_scale = lax.rsqrt(jnp.mean(content * content, axis=1) + norm_eps)
    compact = (content * latent_scale[:, None] * compact_gain[None, :]).astype(bf16)
    shared_key = rotate(projected[:, RANK + 192 :], cos_table, sin_table).astype(bf16)
    key_value = dot("tr,rk->tk", compact, expand_weight, bf16)
    query_rot = jnp.concatenate(
        [
            projected[:, RANK : RANK + NOPE],
            rotate(projected[:, RANK + NOPE : RANK + 192], cos_table, sin_table),
        ],
        axis=1,
    ).astype(bf16)
    key_rows = jnp.concatenate([key_value[:, :NOPE], shared_key], axis=1)
    value_rows = key_value[:, NOPE:]
    head_result, log_total = attend_forward(query_rot, key_rows, value_rows, prefix_len)
    residual_mid, middle_rows, attended_rows, ups, downs = front_step(
        head_result.astype(bf16), out_weight, inputs, expert_up.transpose(0, 2, 1), expert_down
    )

    experts = jnp.arange(EXPERTS, dtype=jnp.int32)
    named = jnp.any(routes.T[None, :, :] == experts[:, None, None], axis=1).astype(f32)
    mine = (experts[:, None] == 2 * col + jnp.arange(128, dtype=jnp.int32)[None, :]).astype(f32)
    hidden, scale_two, act, delta = expert_step(
        middle_rows, out_grad, gates, ups, downs, lows, second_all[None, :], named, mine
    )
    expert_grad = grads_step(hidden, out_grad, delta, act, ff)
    expert_sum = lax.psum_scatter(expert_grad, "dp", scatter_dimension=0, tiled=True)[0]
    act, delta, expert_grad = lax.optimization_barrier((act, delta, expert_grad))
    combined, hidden_grad = back_step(act, delta, gates, ups, downs, lows)
    shared_grad, router_part = shared_step(hidden, out_grad, delta, act, ff, low)

    my_scale_one = lax.dynamic_slice_in_dim(scale_one, row * rows, rows, 0)[:, None]
    my_scale_two = lax.dynamic_slice_in_dim(scale_two[:, :1], row * rows, rows, 0)
    residual_grad, residual_rows, attended_grad, second_gain_part, shared_sum, output = middle_step(
        hidden_grad,
        combined,
        residual_mid,
        cotangent,
        my_scale_two,
        second_gain[None, :],
        out_weight,
        shared_grad,
    )
    head_grad = dot("th,td->hd", attended_rows, residual_rows, bf16)
    output_weight_grad = head_grad.reshape(4, VDIM, 512)[order].reshape(4 * VDIM, 512)
    query_rot_grad, key_grad, value_grad = attend_backward(
        query_rot, key_rows, value_rows, log_total, attended_grad, prefix_len
    )
    pair_grad = jnp.concatenate([key_grad[:, :NOPE], value_grad], axis=1).astype(bf16)
    expand_part = dot("tk,tr->kr", pair_grad, compact, bf16)
    compact_grad = dot("tk,rk->tr", pair_grad, expand_weight)
    weighted_compact = compact_grad * compact_gain[None, :]
    inner_sum = jnp.sum(weighted_compact * content, axis=1)
    content_grad = (
        latent_scale[:, None] * weighted_compact
        - content * (latent_scale * latent_scale * latent_scale * inner_sum / RANK)[:, None]
    )
    latent_gain_part = jnp.sum(compact_grad * content * latent_scale[:, None], axis=0)
    project_grad = jnp.concatenate(
        [
            content_grad,
            query_rot_grad[:, :NOPE],
            rotate(query_rot_grad[:, NOPE:], cos_table, -sin_table),
            rotate(key_grad[:, NOPE:], cos_table, -sin_table),
        ],
        axis=1,
    ).astype(bf16)
    normed_grad = dot("tq,qd->td", project_grad, project_weight, bf16)
    project_part = dot("tq,td->qd", project_grad, normed, bf16)
    latent_part = jnp.concatenate([project_part[:RANK], project_part[RANK + 192 :]], axis=0)
    extra = jnp.concatenate(
        [
            jnp.tile(latent_gain_part.astype(bf16)[None, :], (1, 4)),
            router_part[:EXPERTS],
            jnp.zeros((7, D), bf16),
        ],
        axis=0,
    )
    tail = jnp.concatenate(
        [
            normed_grad.reshape(4, rows, D),
            latent_part.reshape(4, -1, D),
            jnp.broadcast_to(extra[None], (4, 16, D)),
        ],
        axis=1,
    )
    inputs_grad, sums, narrow, gains, latent_small, shared_all = tail_step(
        tail.reshape(-1, D),
        project_part[RANK : RANK + 192],
        jnp.concatenate([output_weight_grad, expand_part], axis=0),
        residual_grad,
        inputs,
        my_scale_one,
        first_gain[None, :],
        second_gain_part,
        shared_sum,
    )
    output_weight_grad = sums[:512].astype(f32)
    expand_grad = sums[512:768].T.astype(f32)
    query_weight_grad = sums[768:].T.astype(f32)
    latent_weight_grad = narrow.reshape(-1, 512).T.astype(f32)
    latent_gain_grad = latent_small[0, 0].astype(f32)
    router_grad = (
        lax.dynamic_index_in_dim(latent_small, col, 0, False)[1 : 1 + EXPERTS].T.astype(f32)
    )
    first_gain_grad, second_gain_grad = gains[0], gains[1]

    pairs = [
        (dp * 4 + c, (2 * c + dp // 4) * 4 + (c ^ (dp % 4))) for dp in range(8) for c in range(4)
    ]
    expert_sum = lax.ppermute(expert_sum, ("dp", "col"), pairs).astype(f32)
    expert_gate_grad = expert_sum[None, :ff].transpose(0, 2, 1)
    expert_up_grad = expert_sum[None, ff : 2 * ff].transpose(0, 2, 1)
    expert_down_grad = expert_sum[None, 2 * ff :]
    shared_sum = shared_all[order].astype(f32)
    shared_gate_grad = shared_sum[:, :low].reshape(4 * low, 512).T
    shared_up_grad = shared_sum[:, low : 2 * low].reshape(4 * low, 512).T
    shared_down_grad = shared_sum[:, 2 * low :].reshape(4 * low, 512)
    return (
        output,
        inputs_grad,
        first_gain_grad,
        query_weight_grad,
        latent_weight_grad,
        latent_gain_grad,
        expand_grad,
        output_weight_grad,
        second_gain_grad,
        router_grad,
        shared_gate_grad,
        shared_up_grad,
        shared_down_grad,
        expert_gate_grad,
        expert_up_grad,
        expert_down_grad,
    )


def solution(mesh):
    placed = (
        P(("dp", "row"), "col"),
        P("col"),
        P("col", "row"),
        P("col", None),
        P(),
        P(None, ("row", "col")),
        P("row", "col"),
        P("col"),
        P("col", None),
        P("col", "row"),
        P("col", "row"),
        P("row", "col"),
        P(None, "col", "row"),
        P(None, "col", "row"),
        P(None, "row", "col"),
        P("dp", None),
        P("dp"),
        P(("dp", "row"), "col"),
    )
    return jax.shard_map(
        on_device,
        mesh=mesh,
        in_specs=placed,
        out_specs=(
            P(("dp", "row"), "col"),
            P(("dp", "row"), "col"),
            P("col"),
            P("col", "row"),
            P("col", None),
            P(),
            P(None, ("row", "col")),
            P("row", "col"),
            P("col"),
            P("col", None),
            P("col", "row"),
            P("col", "row"),
            P("row", "col"),
            P("dp", "col", "row"),
            P("dp", "col", "row"),
            P("dp", "row", "col"),
        ),
        check_vma=False,
    )
```

time: 705 us -> 548 us (0.78)
  the two profiles are of different devices: /device:TPU:5 before, /device:TPU:37 now
where the time goes in v3:
time: 548 us; the launch traced here: 541 us
  Pallas kernels  427 us (78%)
  local copies, waits for them, and re-layouts  25.3 us (5%)
  matrix products  24.7 us (5%)
  other arithmetic  24.1 us (4%)
  waiting for transfers between devices  22 us (4%)
  between operations  15.8 us (3%)
    pallas_call x1, Pallas kernels, tail_step(): pl.pallas_call(tail_kernel, out_shape=(jax.ShapeDtypeStruct((rows, column...  127 us
    pallas_call x1, Pallas kernels, middle_step(): pl.pallas_call(middle_kernel, out_shape=(jax.ShapeDtypeStruct((rows, colu...  105 us
    pallas_call x1, Pallas kernels, front_step(): pl.pallas_call(front_kernel, out_shape=(jax.ShapeDtypeStruct((rows, colum...  66.1 us
    pallas_call x1, Pallas kernels, start_step(): pl.pallas_call(start_kernel, out_shape=(wide, wide, jax.ShapeDtypeStruct(...  62.9 us
    dot_general x13, matrix products, dot(): jnp.einsum(spec, left, right, preferred_element_type=f32).astype(kind)  24.7 us
    ppermute x1, waiting for transfers between devices, on_device(): expert_sum = lax.ppermute(expert_sum, ('dp', 'col'), pairs).astype(f32)  22 us
    pallas_call x1, Pallas kernels, expert_step(): pl.pallas_call(expert_kernel, grid=(tokens // tile,), out_shape=(jax.Shap...  20.4 us
    pallas_call x1, Pallas kernels, back_step(): pl.pallas_call(back_kernel, grid=(tokens // tile,), out_shape=(jax.ShapeD...  19.8 us
  transfers between devices with their start and end apart: 2, of which 1 were waited for; matrix products, arithmetic and copies ran while one was open for 8% of the time, Pallas kernels for 48%

profile of v3, /device:TPU:37, one launch (start us, length us, event | category | flops | bytes accessed | tf_op | source)
XLA Modules:
  0.0 540.6 jit_solution(16882794513258050614)
XLA Ops:
  8.8 2.3 copy.41
  11.8 1.1 pad_maximum_fusion.3.common
  12.9 62.9 %start_step.1 = (bf16[1024,2048]{1,0:T(8,128)(2,1)}, bf16[1024,2048]{1,0:T(8,128)(2,1)}, bf16[784,2048]{1,0:T(8,128)(2,1)}, bf16[704,2048]{1,0:T(8,128)(2,1)}, bf16[544,2048]{1,0:T(8,128)(2,1)}) custom-call(bf16[256,512]{1,0:T(8,128)(2,1)S(1)} %copy-done.2, bf16[256,512]{1,0:T(8,128)(2,1)S(1)} %copy-done.3, bf16[592,512]{1,0:T(8,128)(2,1)S(1)} %pad_maximum_fusion.3.common, ...), custom_call_target="tpu_custom_call" | custom-call | bytes 157286400 | tf_op jit(solution)/shard_map/start_step/pallas_call | solution.py:236
  75.8 3.2 fusion
  79.1 1.4 slice_convert_fusion.4
  80.5 5.6 %fusion.7 = f32[1024,768]{0,1:T(8,128)S(1)} fusion(bf16[784,2048]{1,0:T(8,128)(2,1)} %get-tuple-element.49, bf16[1024,2048]{1,0:T(8,128)(2,1)S(1)} %copy-done.12, f32[2048]{0:T(1024)S(1)} %bitcast.89, f32[1024]{0:T(1024)S(1)} %add_rsqrt_fusion.1), kind=kOutput, calls=%fused_computation.21 | convolution fusion | flops 3229614080 | bytes 10498048 | tf_op jit(solution)/shard_map/td,qd->tq/dot_general | solution.py:970
  89.6 1.2 fusion.47
  91.4 1.3 copy-done.6
  93.9 66.1 %front_step.1 = (f32[256,512]{1,0:T(8,128)S(1)}, bf16[1024,2048]{1,0:T(8,128)(2,1)}, bf16[1024,512]{1,0:T(8,128)(2,1)}, bf16[704,2048]{1,0:T(8,128)(2,1)}, bf16[704,2048]{1,0:T(8,128)(2,1)}) custom-call(bf16[1024,128]{1,0:T(8,128)(2,1)S(1)} %fusion.18.attended, bf16[512,512]{1,0:T(8,128)(2,1)S(1)} %pad_maximum_fusion.4.weight, ...), custom_call_target="tpu_custom_call" | custom-call | flops 536870912 | bytes 157286400 | tf_op jit(solution)/shard_map/front_step/pallas_call | solution.py:942
  160.0 20.4 %expert_step.1 = (bf16[1024,2048]{1,0:T(8,128)(2,1)}, f32[1024,128]{1,0:T(8,128)}, bf16[880,1024]{1,0:T(8,128)(2,1)}, bf16[1776,1024]{1,0:T(8,128)(2,1)}) custom-call(bf16[1024,2048]{1,0:T(8,128)(2,1)} %get-tuple-element.50.middle, bf16[1024,2048]{1,0:T(8,128)(2,1)} %get-tuple-element.51.out_grad, bf16[704,2048]{1,0:T(8,128)(2,1)} %get-tuple-element.52.gates, ...), custom_call_target="tpu_custom_call" | custom-call | flops 14763950080 | bytes 31457280 | tf_op jit(solution)/shard_map/expert_step/pallas_call | solution.py:417
  180.3 17.0 %grads_step.1 = bf16[8,1056,512]{2,1,0:T(8,128)(2,1)} custom-call(bf16[1024,2048]{1,0:T(8,128)(2,1)} %get-tuple-element.58.hidden, bf16[1024,2048]{1,0:T(8,128)(2,1)} %get-tuple-element.51.out_grad, bf16[1776,1024]{1,0:T(8,128)(2,1)} %get-tuple-element.60.delta, bf16[880,1024]{1,0:T(8,128)(2,1)} %get-tuple-element.59.act), custom_call_target="tpu_custom_call" | custom-call | flops 8858370048 | bytes 31457280 | tf_op jit(solution)/shard_map/grads_step/pallas_call | solution.py:500
  199.0 8.7 %shared_step.1 = (bf16[4,528,512]{2,1,0:T(8,128)(2,1)}, bf16[16,2048]{1,0:T(8,128)(2,1)}) custom-call(bf16[1024,2048]{1,0:T(8,128)(2,1)} %get-tuple-element.58.hidden, bf16[1024,2048]{1,0:T(8,128)(2,1)} %get-tuple-element.51.out_grad, bf16[1776,1024]{1,0:T(8,128)(2,1)} %get-tuple-element.60.delta, bf16[880,1024]{1,0:T(8,128)(2,1)} %get-tuple-element.59.act), custom_call_target="tpu_custom_call" | custom-call | flops 2214592512 | bytes 15728640 | tf_op jit(solution)/shard_map/shared_step/pallas_call | solution.py:523
  207.7 19.8 %back_step.1 = (bf16[1024,2048]{1,0:T(8,128)(2,1)}, bf16[1024,2048]{1,0:T(8,128)(2,1)}) custom-call(bf16[880,1024]{1,0:T(8,128)(2,1)} %get-tuple-element.59.act, bf16[1776,1024]{1,0:T(8,128)(2,1)} %get-tuple-element.60.delta, bf16[704,2048]{1,0:T(8,128)(2,1)} %get-tuple-element.52.gates, bf16[704,2048]{1,0:T(8,128)(2,1)} %get-tuple-element.53.ups, ...), custom_call_target="tpu_custom_call" | custom-call | flops 11811160064 | bytes 31457280 | tf_op jit(solution)/shard_map/back_step/pallas_call | solution.py:467
  227.5 105.1 %middle_step.1 = (f32[256,512]{1,0:T(8,128)S(1)}, bf16[1024,512]{1,0:T(8,128)(2,1)}, bf16[1024,128]{1,0:T(8,128)(2,1)S(1)}, f32[1,512]{1,0:T(1,128)S(1)}, bf16[5...) custom-call(bf16[1024,2048]{1,0:T(8,128)(2,1)} %get-tuple-element.61.part, ...), custom_call_target="tpu_custom_call" | custom-call | flops 536870912 | bytes 209715200 | tf_op jit(solution)/shard_map/middle_step/pallas_call | solution.py:653
  333.6 1.1 multiply_convert_fusion
  341.5 4.1 convolution_convert_fusion.1
  346.6 1.5 slice.174
  348.4 2.3 convolution_convert_fusion.3
  351.4 2.3 convolution_convert_fusion.4
  355.4 1.0 copy-done.23
  356.4 3.8 convolution_convert_fusion
  360.2 3.3 pad_maximum_fusion
  363.5 126.5 %tail_step.1 = (bf16[256,512]{1,0:T(8,128)(2,1)S(1)}, bf16[1536,512]{1,0:T(8,128)(2,1)}, bf16[4,144,512]{2,1,0:T(8,128)(2,1)}, f32[16,512]{1,0:T(8,128)S(1)}, bf...) custom-call(bf16[1664,2048]{1,0:T(8,128)(2,1)} %bitcast.72, bf16[192,2048]{1,0:T(8,128)(2,1)} %slice.176.query, ...), custom_call_target="tpu_custom_call" | custom-call | flops 1048576 | bytes 209715200 | tf_op jit(solution)/shard_map/tail_step/pallas_call | solution.py:835
  492.1 1.3 convert_bitcast_fusion
  493.4 1.6 copy.43
  495.0 3.7 gather_fusion.1
  500.0 2.0 collective-permute-start
  502.6 2.1 slice_convert_fusion.3
  504.8 1.2 convert_bitcast_fusion.1
  506.0 2.2 fusion.45
  508.2 22.0 %collective-permute-done = bf16[1056,512]{1,0:T(8,128)(2,1)S(1)} collective-permute-done((bf16[1056,512]{1,0:T(8,128)(2,1)}, bf16[1056,512]{1,0:T(8,128)(2,1)S(1)}, u32[]{:S(2)}, u32[]{:S(2)}) %collective-permute-start) | collective-permute-done | bytes 1081376 | tf_op jit(solution)/shard_map/ppermute | solution.py:1199
  530.5 1.4 slice_bitcast_fusion
  (112 shorter events, 24.9 us)
Async XLA Ops:
  7.2 81.8 %copy-start = (bf16[512,256]{1,0:T(8,128)(2,1)S(1)}, bf16[512,256]{1,0:T(8,128)(2,1)}, u32[]{:S(2)}) copy-start(bf16[512,256]{1,0:T(8,128)(2,1)} %param.23) | copy-start | bytes 786436
  7.2 5.7 %copy-start.2 = (bf16[256,512]{1,0:T(8,128)(2,1)S(1)}, bf16[256,512]{1,0:T(8,128)(2,1)}, u32[]{:S(2)}) copy-start(bf16[256,512]{1,0:T(8,128)(2,1)} %inputs.5) | copy-start | bytes 786436
  7.2 5.7 %copy-start.3 = (bf16[256,512]{1,0:T(8,128)(2,1)S(1)}, bf16[256,512]{1,0:T(8,128)(2,1)}, u32[]{:S(2)}) copy-start(bf16[256,512]{1,0:T(8,128)(2,1)} %cotangent.3) | copy-start | bytes 786436
  7.2 5.7 %copy-start.4 = (bf16[512,704]{0,1:T(8,128)(2,1)S(1)}, bf16[512,704]{0,1:T(8,128)(2,1)}, u32[]{:S(2)}) copy-start(bf16[512,704]{0,1:T(8,128)(2,1)} %param.27) | copy-start | bytes 2162692
  7.2 492.7 %reduce-scatter.2.cloned.1.call-start = ((), (), s32[]{:S(2)}) async-start(), calls=%async_computation.1 | async-start | bytes 9732096 | tf_op jit(solution)/shard_map/reduce_scatter | solution.py:1115
  75.8 4.7 copy-start.12
  80.5 6.5 %copy-start.22 = (bf16[512]{0:T(512)(128)(2,1)S(1)}, bf16[512]{0:T(512)(128)(2,1)}, u32[]{:S(2)}) copy-start(bf16[512]{0:T(512)(128)(2,1)} %param.22) | copy-start | bytes 3076
  80.5 7.2 %copy-start.18 = (s32[1024,6]{0,1:T(8,128)S(1)}, s32[1024,6]{0,1:T(8,128)}, u32[]{:S(2)}) copy-start(s32[1024,6]{0,1:T(8,128)} %param.33) | copy-start | bytes 73732
  86.1 3.5 copy-start.8
  90.8 1.9 copy-start.6
  92.7 1.0 copy-start.17
  93.9 66.1 %copy-start.1 = (bf16[512,512]{1,0:T(8,128)(2,1)}, bf16[512,512]{1,0:T(8,128)(2,1)S(1)}, u32[]{:S(2)}) copy-start(bf16[512,512]{1,0:T(8,128)(2,1)S(1)} %pad_maximum_fusion.4.weight) | copy-start | bytes 1572868
  197.4 0.7 copy-start.20
  227.5 105.1 %copy-start.7 = (f32[1024,1024]{0,1:T(8,128)S(1)}, f32[1024,1024]{0,1:T(8,128)}, u32[]{:S(2)}) copy-start(f32[1024,1024]{0,1:T(8,128)} %copy-done.6) | copy-start | bytes 12582916
  335.6 1.9 copy-start.9
  338.8 2.7 copy-start.13
  341.5 4.1 copy-start.14
  345.7 2.6 copy-start.19
  348.4 2.9 copy-start.21
  351.3 3.3 copy-start.11
  353.7 1.7 copy-start.15
  353.7 2.7 copy-start.23
  360.2 3.3 copy-start.5
  495.0 9.7 %copy-start.16 = (bf16[4,144,512]{2,1,0:T(8,128)(2,1)S(1)}, bf16[4,144,512]{2,1,0:T(8,128)(2,1)}, u32[]{:S(2)}) copy-start(bf16[4,144,512]{2,1,0:T(8,128)(2,1)} %get-tuple-element.77) | copy-start | bytes 1769476
  500.0 6.0 %copy-start.10 = (bf16[4,528,512]{2,1,0:T(8,128)(2,1)S(1)}, bf16[4,528,512]{2,1,0:T(8,128)(2,1)}, u32[]{:S(2)}) copy-start(bf16[4,528,512]{2,1,0:T(8,128)(2,1)} %gather_fusion.1) | copy-start | bytes 6488068
  500.0 30.2 %collective-permute-start = (bf16[1056,512]{1,0:T(8,128)(2,1)}, bf16[1056,512]{1,0:T(8,128)(2,1)S(1)}, u32[]{:S(2)}, u32[]{:S(2)}) collective-permute-start(bf16[1056,512]{1,0:T(8,128)(2,1)} %bitcast.95), channel_id=1, source_target_pairs={{0,0},{1,33},{2,66},{3,99},{16,1},{17,32},{18,67},{19,98},{32,2},{... | collective-permute-start | bytes 3244040 | tf_op jit(solution)/shard_map/ppermute | solution.py:1199
Sparse Core Ops, SparseCore 0:
  197.5 163.3 reduce-scatter.1

commit v4 on v3

--- a/solution.py
+++ b/solution.py
@@ -33,10 +33,6 @@
     sibling = col + 1 - 2 * lax.rem(col, 2)
     across = lax.rem(col + 2, 4)
     return (row, sibling, across, lax.rem(sibling + 2, 4))
-
-
-def xor(left, right):
-    return lax.rem(lax.rem(left, 2) + lax.rem(right, 2), 2) + 2 * lax.rem(left // 2 + right // 2, 2)
 
 
 def greet(columns, row, others=()):
@@ -300,30 +296,38 @@
         return remote(self.side_buf.at[0], self.side_buf.at[1], self.xs, 0, col=self.across)
 
     def start(self):
-        for k in self.order:
-            for x in (0, 1):
+        for x in (1, 0):
+            for k in self.order:
                 self.pair_copy(k, x).start()
 
-    def along(self, order=(2, 1, 3, 0)):
-        for k in order:
-            for x in (0, 1):
-                self.pair_copy(k, x).wait_recv()
-                mine = self.part[self.rows_of(k), pl.ds(2 * x * self.columns, self.columns)]
-                value = mine.astype(f32) + self.held[k, x].astype(f32)
-                if k:
-                    self.out_buf[k - 1, x] = value.astype(bf16)
-                    self.along_copy(k, x).start()
-                else:
-                    self.acc[x] = value
+    def along_one(self, k, x):
+        self.pair_copy(k, x).wait_recv()
+        mine = self.part[self.rows_of(k), pl.ds(2 * x * self.columns, self.columns)]
+        value = mine.astype(f32) + self.held[k, x].astype(f32)
+        if k:
+            self.out_buf[k - 1, x] = value.astype(bf16)
+            self.along_copy(k, x).start()
+        else:
+            self.acc[x] = value
+
+    def along(self):
+        for x in (1, 0):
+            for k in self.order:
+                self.along_one(k, x)
+
+    def collect(self, x):
+        for k in (1, 3, 2):
+            self.along_copy(k, x).wait_recv()
+            self.acc[x] += self.in_buf[k - 1, x].astype(f32)
+
+    def over(self):
+        self.collect(1)
+        self.side_buf[0] = self.acc[1].astype(bf16)
+        self.side_copy().start()
 
     def side(self):
-        for x in (1, 0):
-            for k in (1, 3, 2):
-                self.along_copy(k, x).wait_recv()
-                self.acc[x] += self.in_buf[k - 1, x].astype(f32)
-            if x:
-                self.side_buf[0] = self.acc[1].astype(bf16)
-                self.side_copy().start()
+        self.over()
+        self.collect(0)
 
     def total(self):
         self.side_copy().wait_recv()
@@ -351,7 +355,8 @@
 
 
 def expert_kernel(
-    middle, out_grad, gates, ups, downs, lows, gain, named, mine, hidden, scale, act, delta
+    middle, out_grad, gates, ups, downs, lows, gain, named, mine,
+    hidden, scale, act, delta, combined,
 ):
     values = middle[...].astype(f32)
     scales = lax.rsqrt(jnp.mean(values * values, axis=1, keepdims=True) + norm_eps)
@@ -398,6 +403,10 @@
     delta[pl.ds(4 * ff + 2 * low, 16), :] = jnp.concatenate(
         [logits_part, jnp.zeros_like(logits_part)], axis=0
     ).astype(bf16)
+    combined[...] = (
+        over_units(act[pl.ds(0, 2 * ff), :], downs[...])
+        + over_units(act[pl.ds(2 * ff, low), :], lows[pl.ds(2 * low + 16, low), :])
+    ).astype(bf16)
 
 
 def whole(value):
@@ -422,6 +431,7 @@
             jax.ShapeDtypeStruct((tokens, 128), f32),
             jax.ShapeDtypeStruct((acts, tokens), bf16),
             jax.ShapeDtypeStruct((deltas, tokens), bf16),
+            jax.ShapeDtypeStruct((tokens, width), bf16),
         ),
         in_specs=[
             wide,
@@ -439,6 +449,7 @@
             pl.BlockSpec((tile, 128), lambda i: (i, 0)),
             tall(acts),
             tall(deltas),
+            wide,
         ),
         compiler_params=pltpu.CompilerParams(vmem_limit_bytes=56 << 20),
         cost_estimate=cost(2 * 5 * gates.shape[0] * width * tokens, 30),
@@ -446,102 +457,159 @@
     )(middle, out_grad, gates, ups, downs, lows, gain, named, mine)
 
 
-def back_kernel(act, delta, gates, ups, downs, lows, combined, hidden_grad):
+def back_kernel(delta, gates, ups, lows, hidden_grad):
     ff = gates.shape[0]
-    low = (lows.shape[0] - 16) // 3
-    combined[...] = (
-        over_units(act[pl.ds(0, ff), :], downs[...])
-        + over_units(act[pl.ds(ff, low), :], lows[pl.ds(2 * low + 16, low), :])
-    ).astype(bf16)
+    low = lows.shape[0] - 16 - (lows.shape[0] - 16) // 3 + 16
     hidden_grad[...] = (
         over_units(delta[pl.ds(0, ff), :], gates[...])
         + over_units(delta[pl.ds(ff, ff), :], ups[...])
-        + over_units(delta[pl.ds(2 * ff, 2 * low + 16), :], lows[pl.ds(0, 2 * low + 16), :])
+        + over_units(delta[pl.ds(2 * ff, low), :], lows[pl.ds(0, low), :])
     ).astype(bf16)
 
 
-def back_step(act, delta, gates, ups, downs, lows):
+def back_step(delta, gates, ups, lows):
     tile = 256
-    tokens, width = act.shape[1], gates.shape[1]
-    wide = pl.BlockSpec((tile, width), lambda i: (i, 0))
+    tokens, width = delta.shape[1], gates.shape[1]
     return pl.pallas_call(
         back_kernel,
         grid=(tokens // tile,),
-        out_shape=(jax.ShapeDtypeStruct((tokens, width), bf16),) * 2,
+        out_shape=jax.ShapeDtypeStruct((tokens, width), bf16),
         in_specs=[
-            pl.BlockSpec((act.shape[0], tile), lambda i: (0, i)),
             pl.BlockSpec((delta.shape[0], tile), lambda i: (0, i)),
             whole(gates),
             whole(ups),
-            whole(downs),
             whole(lows),
         ],
-        out_specs=(wide, wide),
+        out_specs=pl.BlockSpec((tile, width), lambda i: (i, 0)),
         compiler_params=pltpu.CompilerParams(vmem_limit_bytes=56 << 20),
-        cost_estimate=cost(2 * 4 * gates.shape[0] * width * tokens, 30),
+        cost_estimate=cost(2 * 3 * gates.shape[0] * width * tokens, 30),
         name="back_step",
-    )(act, delta, gates, ups, downs, lows)
-
-
-def grads_kernel(hidden, out_grad, delta, act, grads, *, ff):
+    )(delta, gates, ups, lows)
+
+
+def grads_kernel(
+    hidden, out_grad, delta, act, combined, grads, shared, router, total,
+    own_shared, chunk_in, ps, pr, *scratch, ff, low,
+):
+    step = pl.program_id(0)
+    row, sibling, across, corner = place()
+    dp = lax.axis_index("dp")
+    z = lax.rem(dp, 4)
+    steps = Reduction(combined, scratch, row, sibling, across)
+    piece = shared.shape[1]
+
+    def quarter(at):
+        return pl.ds(pl.multiple_of(at * piece, piece), piece)
+
+    def scattered(k):
+        return remote(
+            own_shared.at[:, quarter(lax.rem(z + k, 4))],
+            chunk_in.at[k - 1],
+            (ps, pr),
+            k - 1,
+            dp=along_z(dp, k),
+        )
+
+    @pl.when(step == 0)
+    def _():
+        greet((sibling, across), row, [{"dp": along_z(dp, k)} for k in (1, 2, 3)])
+        steps.start()
+
+    for at, blocks in (
+        (1, ((2, 1), (1, 1), (3, 1))),
+        (2, ((0, 1), (2, 0), (1, 0))),
+        (3, ((3, 0), (0, 0))),
+    ):
+
+        @pl.when(step == at)
+        def _(blocks=blocks):
+            for k, x in blocks:
+                steps.along_one(k, x)
+
+    @pl.when(step == 8)
+    def _():
+        steps.over()
+
+    for k in range(4):
+
+        @pl.when(step == k)
+        def _(k=k):
+            base = 4 * ff
+            own_shared[k, pl.ds(0, low), :] = product(delta[pl.ds(base, low), :], hidden[...])
+            own_shared[k, pl.ds(low, low), :] = product(
+                delta[pl.ds(base + low, low), :], hidden[...]
+            )
+            router[...] = product(delta[pl.ds(base + 2 * low, 16), :], hidden[...])
+            own_shared[k, pl.ds(2 * low, low), :] = product(
+                act[pl.ds(2 * ff, low), :], out_grad[...]
+            )
+            spare = 4 * piece - 3 * low
+            own_shared[k, pl.ds(3 * low, spare), :] = jnp.zeros((spare, 512), bf16)
+
+    @pl.when(step == 3)
+    def _():
+        for k in (1, 2, 3):
+            scattered(k).start()
+
     for e in (0, 1):
 
-        @pl.when(pl.program_id(0) // 4 == e)
+        @pl.when(step // 4 == e + 1)
         def _(e=e):
             at = e * ff
             grads[0, pl.ds(0, ff), :] = product(delta[pl.ds(at, ff), :], hidden[...])
             grads[0, pl.ds(ff, ff), :] = product(delta[pl.ds(2 * ff + at, ff), :], hidden[...])
             grads[0, pl.ds(2 * ff, ff), :] = product(act[pl.ds(at, ff), :], out_grad[...])
 
-
-def grads_step(hidden, out_grad, delta, act, ff):
+    @pl.when(step == 11)
+    def _():
+        steps.collect(0)
+        total[...] = steps.total()
+        summed = own_shared[:, quarter(z), :].astype(f32)
+        for k in (1, 2, 3):
+            scattered(k).wait_recv()
+            summed += chunk_in[k - 1].astype(f32)
+        shared[...] = summed.astype(bf16)
+        for k in (1, 2, 3):
+            scattered(k).wait_send()
+        steps.finish()
+
+
+def grads_step(hidden, out_grad, delta, act, combined, ff, low):
     tokens = hidden.shape[0]
+    piece = -(-3 * low // 64) * 16
     wide = pl.BlockSpec((tokens, 512), lambda i: (0, i % 4))
     return pl.pallas_call(
-        functools.partial(grads_kernel, ff=ff),
-        grid=(8,),
-        out_shape=jax.ShapeDtypeStruct((8, 3 * ff, 512), bf16),
-        in_specs=[wide, wide, whole(delta), whole(act)],
-        out_specs=pl.BlockSpec((1, 3 * ff, 512), lambda i: (i, 0, 0)),
-        compiler_params=pltpu.CompilerParams(vmem_limit_bytes=56 << 20),
-        cost_estimate=cost(2 * 8 * 3 * ff * 512 * tokens, 30),
+        functools.partial(grads_kernel, ff=ff, low=low),
+        grid=(12,),
+        out_shape=(
+            jax.ShapeDtypeStruct((8, 3 * ff, 512), bf16),
+            jax.ShapeDtypeStruct((4, piece, 512), bf16),
+            jax.ShapeDtypeStruct((16, D), bf16),
+            jax.ShapeDtypeStruct((tokens // 4, 512), f32),
+        ),
+        in_specs=[wide, wide, whole(delta), whole(act), whole(combined)],
+        out_specs=(
+            pl.BlockSpec((1, 3 * ff, 512), lambda i: (jnp.maximum(i - 4, 0), 0, 0)),
+            pl.BlockSpec((4, piece, 512), lambda i: (0, 0, 0)),
+            pl.BlockSpec((16, 512), lambda i: (0, jnp.minimum(i, 3))),
+            pl.BlockSpec((tokens // 4, 512), lambda i: (0, 0)),
+        ),
+        scratch_shapes=[
+            pltpu.VMEM((4, 4 * piece, 512), bf16),
+            pltpu.VMEM((3, 4, piece, 512), bf16),
+            *pair(3),
+            *reduce_scratch(tokens // 4, 512),
+        ],
+        compiler_params=params(1),
+        cost_estimate=cost(2 * 8 * 4 * ff * 512 * tokens, 60),
         name="grads_step",
-    )(hidden, out_grad, delta, act)
-
-
-def shared_kernel(hidden, out_grad, delta, act, grads, router, *, ff, low):
-    base = 4 * ff
-    grads[0, pl.ds(0, low), :] = product(delta[pl.ds(base, low), :], hidden[...])
-    grads[0, pl.ds(low, low), :] = product(delta[pl.ds(base + low, low), :], hidden[...])
-    router[...] = product(delta[pl.ds(base + 2 * low, 16), :], hidden[...])
-    grads[0, pl.ds(2 * low, low), :] = product(act[pl.ds(2 * ff, low), :], out_grad[...])
-
-
-def shared_step(hidden, out_grad, delta, act, ff, low):
-    tokens = hidden.shape[0]
-    wide = pl.BlockSpec((tokens, 512), lambda i: (0, i))
-    return pl.pallas_call(
-        functools.partial(shared_kernel, ff=ff, low=low),
-        grid=(4,),
-        out_shape=(
-            jax.ShapeDtypeStruct((4, 3 * low, 512), bf16),
-            jax.ShapeDtypeStruct((16, D), bf16),
-        ),
-        in_specs=[wide, wide, whole(delta), whole(act)],
-        out_specs=(
-            pl.BlockSpec((1, 3 * low, 512), lambda i: (i, 0, 0)),
-            pl.BlockSpec((16, 512), lambda i: (0, i)),
-        ),
-        compiler_params=pltpu.CompilerParams(vmem_limit_bytes=56 << 20),
-        cost_estimate=cost(2 * 4 * 3 * low * 512 * tokens, 15),
-        name="shared_step",
-    )(hidden, out_grad, delta, act)
+    )(hidden, out_grad, delta, act, combined)
 
 
 class ColumnSum:
     def __init__(self, value, buf, sems, go, peers):
-        self.buf, self.own = buf, value
-        buf[0] = jnp.broadcast_to(value, buf.shape[1:])
+        self.buf = buf
+        buf[0] = jnp.broadcast_to(value, (value.shape[0], 128)).T[:8]
         self.sent = [
             go(buf.at[0], buf.at[k + 1], sems, k, col=peer) for k, peer in enumerate(peers)
         ]
@@ -550,13 +618,14 @@
         for copy in self.sent:
             copy.wait_recv()
         buf = self.buf
-        return ((buf[0] + buf[1]) + (buf[2] + buf[3]))[:, :1]
+        total = (buf[0] + buf[1]) + (buf[2] + buf[3])
+        return jnp.broadcast_to(total[:1], (128, total.shape[1])).T[:, :1]
 
 
 def middle_kernel(
-    part, combined, middle, cotangent, scale, gain, weight, shared,
-    residual_grad, residual_rows, attended_grad, gain_part, shared_sum, output,
-    sum_buf, out_buf, in_buf, acc, chunk_in, ss, sr, rs, rr, hs, hr, ps, pr, *scratch,
+    part, middle, cotangent, scale, gain, weight, shared,
+    residual_grad, residual_rows, attended_grad, gain_part, shared_all,
+    sum_buf, out_buf, in_buf, acc, chunk_in, both, ss, sr, rs, rr, hs, hr, ps, pr, *scratch,
 ):
     row, sibling, across, corner = place()
     dp = lax.axis_index("dp")
@@ -566,21 +635,21 @@
     greet(peers, row, [{"dp": along_z(dp, k)} for k in (1, 2, 3)] + [{"dp": far}])
     pending = []
     go = starter(pending)
-    count = len(scratch) // 2
-    steps = Reduction(part, scratch[:count], row, sibling, across)
-    beside = Reduction(combined, scratch[count:], row, sibling, across)
+    steps = Reduction(part, scratch, row, sibling, across)
     rows, columns = middle.shape
     head = attended_grad.shape[1]
     steps.start()
-    scattered = [
-        go(
-            shared.at[lax.rem(z + k, 4)], chunk_in.at[k - 1], (ps, pr), k - 1, dp=along_z(dp, k)
-        )
-        for k in (1, 2, 3)
+    halves = go(shared, chunk_in, (ps, pr), 0, dp=far)
+    steps.along()
+    steps.over()
+    halves.wait_recv()
+    both[...] = (shared[...].astype(f32) + chunk_in[...].astype(f32)).astype(bf16)
+    shared_all[z, 0] = both[0]
+    home = [
+        go(both.at[j + 1], shared_all.at[z, j + 1], (ps, pr), 1 + j, col=peer)
+        for j, peer in enumerate(peers)
     ]
-    steps.along()
-    beside.start()
-    steps.side()
+    steps.collect(0)
     upstream = steps.total()
     weighted = upstream * gain[...]
     values = middle[...]
@@ -589,6 +658,12 @@
         jnp.sum(weighted * values, axis=1, keepdims=True), sum_buf, (ss, sr), go, peers
     )
     gain_part[...] = jnp.sum(upstream * values * scales, axis=0, keepdims=True)
+    for copy in home:
+        copy.wait_recv()
+    spread = [
+        go(shared_all.at[z], shared_all.at[z], (ps, pr), 3 + k, dp=along_z(dp, k))
+        for k in (1, 2, 3)
+    ]
     base = cotangent[...].astype(f32) + scales * weighted
     grad = base - values * (scales * scales * scales * inner.total() / D)
     residual_grad[...] = grad
@@ -607,7 +682,6 @@
         )
         for k in (1, 2, 3)
     ]
-    beside.along()
     got = []
     for k in (0, 1, 3, 2):
         source = lax.rem(row + 4 - k, 4)
@@ -626,28 +700,19 @@
                     col=peer,
                 )
             )
-    total = shared[z].astype(f32)
-    for k in (1, 2, 3):
-        scattered[k - 1].wait_recv()
-        total += chunk_in[k - 1].astype(f32)
-    chunk_in[3] = total.astype(bf16)
-    halves = go(chunk_in.at[3], chunk_in.at[4], (ps, pr), 3, dp=far)
-    beside.side()
     for copy in got:
         copy.wait_recv()
     attended_grad[...] = (
         acc[...] + in_buf[0].astype(f32) + in_buf[1].astype(f32) + in_buf[2].astype(f32)
     ).astype(bf16)
-    output[...] = (beside.total() + values).astype(bf16)
-    halves.wait_recv()
-    shared_sum[...] = (chunk_in[3].astype(f32) + chunk_in[4].astype(f32)).astype(bf16)
+    for copy in spread:
+        copy.wait_recv()
     for copy in pending:
         copy.wait_send()
     steps.finish()
-    beside.finish()
-
-
-def middle_step(part, combined, middle, cotangent, scale, gain, weight, shared):
+
+
+def middle_step(part, middle, cotangent, scale, gain, weight, shared):
     rows, columns = middle.shape
     piece = shared.shape[1]
     return pl.pallas_call(
@@ -657,35 +722,34 @@
             jax.ShapeDtypeStruct((4 * rows, columns), bf16),
             jax.ShapeDtypeStruct((4 * rows, VDIM), bf16),
             jax.ShapeDtypeStruct((1, columns), f32),
-            jax.ShapeDtypeStruct((piece, columns), bf16),
-            jax.ShapeDtypeStruct((rows, columns), bf16),
+            jax.ShapeDtypeStruct((4, 4, piece, columns), bf16),
         ),
-        in_specs=[VMEM] * 8,
-        out_specs=(VMEM,) * 6,
+        in_specs=[VMEM] * 7,
+        out_specs=(VMEM,) * 5,
         scratch_shapes=[
-            pltpu.VMEM((4, rows, 128), f32),
+            pltpu.VMEM((4, 8, rows), f32),
             pltpu.VMEM((3, 4 * rows, VDIM), bf16),
             pltpu.VMEM((3, 4 * rows, VDIM), bf16),
             pltpu.VMEM((4 * rows, VDIM), f32),
-            pltpu.VMEM((5, piece, columns), bf16),
+            pltpu.VMEM((4, piece, columns), bf16),
+            pltpu.VMEM((4, piece, columns), bf16),
             *pair(3),
             *pair(3),
             *pair(3, 4),
-            *pair(4),
-            *reduce_scratch(rows, columns),
+            *pair(7),
             *reduce_scratch(rows, columns),
         ],
         compiler_params=params(3),
         cost_estimate=cost(1 << 29, 200),
         name="middle_step",
-    )(part, combined, middle, cotangent, scale, gain, weight, shared)
+    )(part, middle, cotangent, scale, gain, weight, shared)
 
 
 def tail_kernel(
-    part, query, ready, residual_grad, inputs, scale, gain, gain_part, shared_sum,
-    inputs_grad, sums, narrow, gains, latent_gain, shared_all,
+    part, narrow_part, query, ready, residual_grad, inputs, scale, gain, gain_part,
+    inputs_grad, sums, narrow, gains, latent_gain,
     chunk_in, all_parts, narrow_all, lat_buf, lat_half, sum_buf,
-    qs, qr, ps, pr, as_, ar, ls, lr, ns, nr, ss, sr, gs, gr, ws, wr, *scratch,
+    qs, qr, ps, pr, as_, ar, ls, lr, ns, nr, ss, sr, gs, gr, *scratch,
 ):
     row, sibling, across, corner = place()
     col = lax.axis_index("col")
@@ -693,17 +757,16 @@
     z = lax.rem(dp, 4)
     far = lax.rem(dp + 4, 8)
     peers = (sibling, across, corner)
-    others = [{"dp": along_z(dp, k)} for k in (1, 2, 3)] + [{"dp": far}]
-    others += [
-        {"dp": along_z(dp, 4 - k), "col": xor(col, lax.rem(z + 4 - k, 4))} for k in (1, 2, 3)
-    ]
-    greet(peers, row, others)
+    greet(peers, row, [{"dp": along_z(dp, k)} for k in (1, 2, 3)] + [{"dp": far}])
     pending = []
     go = starter(pending)
-    steps = Reduction(part, scratch, row, sibling, across)
+    count = len(scratch) // 2
+    steps = Reduction(part, scratch[:count], row, sibling, across)
+    before = Reduction(narrow_part, scratch[count:], row, sibling, across)
     rows, columns = inputs.shape
     piece = query.shape[0]
     lat = narrow_all.shape[1]
+    keep = lat - 32
 
     def head(at):
         return pl.ds(pl.multiple_of(at * piece, piece), piece)
@@ -711,7 +774,7 @@
     def chunk(at):
         return pl.ds(pl.multiple_of(at * 2 * piece, 2 * piece), 2 * piece)
 
-    steps.start()
+    before.start()
     dealt = [
         go(
             query.at[:, pl.ds((j + 1) * columns, columns)],
@@ -722,26 +785,10 @@
         )
         for j, peer in enumerate(peers)
     ]
+    steps.start()
     all_parts[pl.ds(0, 4 * piece), :] = ready[...]
     all_parts[head(4 + col), :] = query[:, pl.ds(0, columns)]
-    goal = xor(col, z)
-    spread_shared = [
-        go(shared_sum, shared_all.at[z], (ws, wr), k - 1, dp=along_z(dp, k), col=goal)
-        for k in (1, 2, 3)
-    ]
-
-    def own_block():
-        return remote(shared_sum, shared_all.at[z], (ws, wr), 3, col=goal)
-
-    @pl.when(z == 0)
-    def _():
-        shared_all[0] = shared_sum[...]
-
-    @pl.when(z != 0)
-    def _():
-        own_block().start()
-
-    steps.along()
+    before.along()
     for copy in dealt:
         copy.wait_recv()
     scattered = [
@@ -754,33 +801,21 @@
         )
         for k in (1, 2, 3)
     ]
-    steps.side()
+    steps.along()
+    before.side()
+    lat_buf[z] = jnp.concatenate(
+        [before.total(), gain_part[...], jnp.zeros((15, columns), f32)], axis=0
+    ).astype(bf16)
+    along = [
+        go(lat_buf.at[z], lat_buf.at[z], (ls, lr), k - 1, dp=along_z(dp, k)) for k in (1, 2, 3)
+    ]
     total = all_parts[chunk(z), :].astype(f32)
     for k in (1, 2, 3):
         scattered[k - 1].wait_recv()
         total += chunk_in[k - 1].astype(f32)
     chunk_in[3] = total.astype(bf16)
     halves = go(chunk_in.at[3], chunk_in.at[4], (ps, pr), 3, dp=far)
-    whole = steps.total()
-    upstream = whole[:rows]
-    weighted = upstream * gain[...]
-    values = inputs[...].astype(f32)
-    scales = scale[...]
-    inner = ColumnSum(
-        jnp.sum(weighted * values, axis=1, keepdims=True), sum_buf, (ss, sr), go, peers
-    )
-    first_part = jnp.sum(upstream * values * scales, axis=0, keepdims=True)
-    extra = jnp.concatenate([first_part, gain_part[...], jnp.zeros((14, columns), f32)], axis=0)
-    lat_buf[z] = jnp.concatenate([whole[rows:], extra], axis=0).astype(bf16)
-    along = [
-        go(lat_buf.at[z], lat_buf.at[z], (ls, lr), k - 1, dp=along_z(dp, k)) for k in (1, 2, 3)
-    ]
-    halves.wait_recv()
-    sums[chunk(z), :] = (chunk_in[3].astype(f32) + chunk_in[4].astype(f32)).astype(bf16)
-    shared = [
-        go(sums.at[chunk(z)], sums.at[chunk(z)], (as_, ar), k - 1, dp=along_z(dp, k))
-        for k in (1, 2, 3)
-    ]
+    steps.over()
     for copy in along:
         copy.wait_recv()
     lat_half[0] = (
@@ -788,20 +823,33 @@
         + (lat_buf[2].astype(f32) + lat_buf[3].astype(f32))
     ).astype(bf16)
     other = go(lat_half.at[0], lat_half.at[1], (ls, lr), 3, dp=far)
-    inputs_grad[...] = (
-        residual_grad[...]
-        + scales * weighted
-        - values * (scales * scales * scales * inner.total() / D)
-    ).astype(bf16)
+    steps.collect(0)
+    halves.wait_recv()
+    sums[chunk(z), :] = (chunk_in[3].astype(f32) + chunk_in[4].astype(f32)).astype(bf16)
+    shared = [
+        go(sums.at[chunk(z)], sums.at[chunk(z)], (as_, ar), k - 1, dp=along_z(dp, k))
+        for k in (1, 2, 3)
+    ]
+    upstream = steps.total()
+    weighted = upstream * gain[...]
+    values = inputs[...].astype(f32)
+    scales = scale[...]
+    inner = ColumnSum(
+        jnp.sum(weighted * values, axis=1, keepdims=True), sum_buf, (ss, sr), go, peers
+    )
     other.wait_recv()
     narrow_all[row] = (lat_half[0].astype(f32) + lat_half[1].astype(f32)).astype(bf16)
     spread = [
         go(narrow_all.at[row], narrow_all.at[row], (ns, nr), k - 1, row=lax.rem(row + k, 4))
         for k in (1, 2, 3)
     ]
+    inputs_grad[...] = (
+        residual_grad[...]
+        + scales * weighted
+        - values * (scales * scales * scales * inner.total() / D)
+    ).astype(bf16)
     for copy in spread:
         copy.wait_recv()
-    keep = lat - 32
     narrow[...] = narrow_all[:, :keep, :]
     latent_gain[col] = narrow_all[0, pl.ds(keep, 16), :]
     last = [
@@ -815,23 +863,21 @@
         + narrow_all[2, edge, :].astype(f32)
         + narrow_all[3, edge, :].astype(f32)
     )
-    for copy in last + shared + spread_shared:
+    for copy in last + shared:
         copy.wait_recv()
-
-    @pl.when(z != 0)
-    def _():
-        own_block().wait()
-
     for copy in pending:
         copy.wait_send()
     steps.finish()
-
-
-def tail_step(part, query, ready, residual_grad, inputs, scale, gain, gain_part, shared_sum):
+    before.finish()
+
+
+def tail_step(
+    part, narrow_part, query, ready, residual_grad, inputs, scale, gain, gain_part
+):
     rows, columns = inputs.shape
     piece = query.shape[0]
-    all_rows = part.shape[0] // 4
-    lat = all_rows - rows + 16
+    narrow_rows = narrow_part.shape[0] // 4
+    lat = narrow_rows + 16
     return pl.pallas_call(
         tail_kernel,
         out_shape=(
@@ -840,17 +886,16 @@
             jax.ShapeDtypeStruct((4, lat - 32, columns), bf16),
             jax.ShapeDtypeStruct((16, columns), f32),
             jax.ShapeDtypeStruct((4, 16, columns), bf16),
-            jax.ShapeDtypeStruct((4,) + shared_sum.shape, bf16),
         ),
         in_specs=[VMEM] * 9,
-        out_specs=(VMEM,) * 6,
+        out_specs=(VMEM,) * 5,
         scratch_shapes=[
             pltpu.VMEM((5, 2 * piece, columns), bf16),
             pltpu.VMEM((8 * piece, columns), bf16),
             pltpu.VMEM((4, lat, columns), bf16),
             pltpu.VMEM((4, lat, columns), bf16),
             pltpu.VMEM((2, lat, columns), bf16),
-            pltpu.VMEM((4, rows, 128), f32),
+            pltpu.VMEM((4, 8, rows), f32),
             *pair(3),
             *pair(4),
             *pair(3),
@@ -858,13 +903,13 @@
             *pair(3),
             *pair(3),
             *pair(3),
-            *pair(4),
-            *reduce_scratch(all_rows, columns),
+            *reduce_scratch(rows, columns),
+            *reduce_scratch(narrow_rows, columns),
         ],
         compiler_params=params(4),
         cost_estimate=cost(1 << 20, 200),
         name="tail_step",
-    )(part, query, ready, residual_grad, inputs, scale, gain, gain_part, shared_sum)
+    )(part, narrow_part, query, ready, residual_grad, inputs, scale, gain, gain_part)
 
 
 def front_kernel(
@@ -1108,20 +1153,21 @@
     experts = jnp.arange(EXPERTS, dtype=jnp.int32)
     named = jnp.any(routes.T[None, :, :] == experts[:, None, None], axis=1).astype(f32)
     mine = (experts[:, None] == 2 * col + jnp.arange(128, dtype=jnp.int32)[None, :]).astype(f32)
-    hidden, scale_two, act, delta = expert_step(
+    hidden, scale_two, act, delta, combined = expert_step(
         middle_rows, out_grad, gates, ups, downs, lows, second_all[None, :], named, mine
     )
-    expert_grad = grads_step(hidden, out_grad, delta, act, ff)
+    expert_grad, shared_grad, router_part, combined_sum = grads_step(
+        hidden, out_grad, delta, act, combined, ff, low
+    )
+    output = (residual_mid + combined_sum).astype(bf16)
     expert_sum = lax.psum_scatter(expert_grad, "dp", scatter_dimension=0, tiled=True)[0]
-    act, delta, expert_grad = lax.optimization_barrier((act, delta, expert_grad))
-    combined, hidden_grad = back_step(act, delta, gates, ups, downs, lows)
-    shared_grad, router_part = shared_step(hidden, out_grad, delta, act, ff, low)
+    delta, expert_grad = lax.optimization_barrier((delta, expert_grad))
+    hidden_grad = back_step(delta, gates, ups, lows)
 
     my_scale_one = lax.dynamic_slice_in_dim(scale_one, row * rows, rows, 0)[:, None]
     my_scale_two = lax.dynamic_slice_in_dim(scale_two[:, :1], row * rows, rows, 0)
-    residual_grad, residual_rows, attended_grad, second_gain_part, shared_sum, output = middle_step(
+    residual_grad, residual_rows, attended_grad, second_gain_part, shared_all = middle_step(
         hidden_grad,
-        combined,
         residual_mid,
         cotangent,
         my_scale_two,
@@ -1156,24 +1202,29 @@
     normed_grad = dot("tq,qd->td", project_grad, project_weight, bf16)
     project_part = dot("tq,td->qd", project_grad, normed, bf16)
     latent_part = jnp.concatenate([project_part[:RANK], project_part[RANK + 192 :]], axis=0)
+    first_part = jnp.sum(
+        normed_grad.astype(f32) * (input_rows * scale_one[:, None]), axis=0, keepdims=True
+    )
     extra = jnp.concatenate(
         [
-            jnp.tile(latent_gain_part.astype(bf16)[None, :], (1, 4)),
+            jnp.tile(latent_gain_part[None, :], (1, 4)).astype(bf16),
+            first_part.astype(bf16),
             router_part[:EXPERTS],
-            jnp.zeros((7, D), bf16),
+            jnp.zeros((6, D), bf16),
         ],
         axis=0,
     )
-    tail = jnp.concatenate(
-        [
-            normed_grad.reshape(4, rows, D),
-            latent_part.reshape(4, -1, D),
-            jnp.broadcast_to(extra[None], (4, 16, D)),
-        ],
-        axis=1,
-    )
-    inputs_grad, sums, narrow, gains, latent_small, shared_all = tail_step(
-        tail.reshape(-1, D),
+    narrow_part = jnp.concatenate(
+        [latent_part.reshape(4, -1, D), jnp.broadcast_to(extra[None], (4, 16, D))], axis=1
+    )
+    narrow_part, expert_sum = lax.optimization_barrier((narrow_part, expert_sum))
+    pairs = [
+        (dp * 4 + c, (2 * c + dp // 4) * 4 + (c ^ (dp % 4))) for dp in range(8) for c in range(4)
+    ]
+    expert_sum = lax.ppermute(expert_sum, ("dp", "col"), pairs)
+    inputs_grad, sums, narrow, gains, latent_small = tail_step(
+        normed_grad,
+        narrow_part.reshape(-1, D),
         project_part[RANK : RANK + 192],
         jnp.concatenate([output_weight_grad, expand_part], axis=0),
         residual_grad,
@@ -1181,29 +1232,25 @@
         my_scale_one,
         first_gain[None, :],
         second_gain_part,
-        shared_sum,
     )
     output_weight_grad = sums[:512].astype(f32)
     expand_grad = sums[512:768].T.astype(f32)
     query_weight_grad = sums[768:].T.astype(f32)
     latent_weight_grad = narrow.reshape(-1, 512).T.astype(f32)
     latent_gain_grad = latent_small[0, 0].astype(f32)
-    router_grad = (
-        lax.dynamic_index_in_dim(latent_small, col, 0, False)[1 : 1 + EXPERTS].T.astype(f32)
-    )
-    first_gain_grad, second_gain_grad = gains[0], gains[1]
-
-    pairs = [
-        (dp * 4 + c, (2 * c + dp // 4) * 4 + (c ^ (dp % 4))) for dp in range(8) for c in range(4)
-    ]
-    expert_sum = lax.ppermute(expert_sum, ("dp", "col"), pairs).astype(f32)
+    own_small = lax.dynamic_index_in_dim(latent_small, col, 0, False).astype(f32)
+    first_gain_grad = own_small[1]
+    router_grad = own_small[2 : 2 + EXPERTS].T
+    second_gain_grad = gains[0]
+
+    expert_sum = expert_sum.astype(f32)
     expert_gate_grad = expert_sum[None, :ff].transpose(0, 2, 1)
     expert_up_grad = expert_sum[None, ff : 2 * ff].transpose(0, 2, 1)
     expert_down_grad = expert_sum[None, 2 * ff :]
-    shared_sum = shared_all[order].astype(f32)
+    shared_sum = shared_all.transpose(1, 0, 2, 3).reshape(4, -1, 512)[order].astype(f32)
     shared_gate_grad = shared_sum[:, :low].reshape(4 * low, 512).T
     shared_up_grad = shared_sum[:, low : 2 * low].reshape(4 * low, 512).T
-    shared_down_grad = shared_sum[:, 2 * low :].reshape(4 * low, 512)
+    shared_down_grad = shared_sum[:, 2 * low : 3 * low].reshape(4 * low, 512)
     return (
         output,
         inputs_grad,

time: 548 us -> 505 us (0.922)
  the two profiles are of different devices: /device:TPU:37 before, /device:TPU:5 now
where the time goes in v4:
time: 505 us; the launch traced here: 495 us
  Pallas kernels  359 us (71%)
  local copies, waits for them, and re-layouts  31.9 us (6%)
  matrix products  31.2 us (6%)
  waiting for transfers between devices  27.2 us (5%)
  other arithmetic  24.6 us (5%)
  between operations  15.8 us (3%)
  starting transfers between devices  5.09 us (1%)
    pallas_call x1, Pallas kernels, middle_step(): pl.pallas_call(middle_kernel, out_shape=(jax.ShapeDtypeStruct((rows, colu...  75.5 us
    pallas_call x1, Pallas kernels, tail_step(): pl.pallas_call(tail_kernel, out_shape=(jax.ShapeDtypeStruct((rows, column...  71.9 us
    pallas_call x1, Pallas kernels, front_step(): pl.pallas_call(front_kernel, out_shape=(jax.ShapeDtypeStruct((rows, colum...  66.1 us
    pallas_call x1, Pallas kernels, start_step(): pl.pallas_call(start_kernel, out_shape=(wide, wide, jax.ShapeDtypeStruct(...  62.9 us
    pallas_call x1, Pallas kernels, grads_step(): pl.pallas_call(functools.partial(grads_kernel, ff=ff, low=low), grid=(12,...  43.2 us
    dot_general x13, matrix products, dot(): jnp.einsum(spec, left, right, preferred_element_type=f32).astype(kind)  31.2 us
    pallas_call x1, Pallas kernels, expert_step(): pl.pallas_call(expert_kernel, grid=(tokens // tile,), out_shape=(jax.Shap...  25.5 us
    ppermute x1, waiting for transfers between devices, on_device(): expert_sum = lax.ppermute(expert_sum, ('dp', 'col'), pairs)  19.9 us
  transfers between devices with their start and end apart: 2, of which 2 were waited for; matrix products, arithmetic and copies ran while one was open for 10% of the time, Pallas kernels for 18%

profile of v4, /device:TPU:5, one launch (start us, length us, event | category | flops | bytes accessed | tf_op | source)
XLA Modules:
  0.0 495.2 jit_solution(14750045533747588653)
XLA Ops:
  7.3 2.4 copy.42
  12.9 62.9 %start_step.1 = (bf16[1024,2048]{1,0:T(8,128)(2,1)}, bf16[1024,2048]{1,0:T(8,128)(2,1)}, bf16[784,2048]{1,0:T(8,128)(2,1)}, bf16[704,2048]{1,0:T(8,128)(2,1)}, bf16[544,2048]{1,0:T(8,128)(2,1)}) custom-call(bf16[256,512]{1,0:T(8,128)(2,1)S(1)} %copy-done.2, bf16[256,512]{1,0:T(8,128)(2,1)S(1)} %copy-done.3, bf16[592,512]{1,0:T(8,128)(2,1)S(1)} %pad_maximum_fusion.3.common, ...), custom_call_target="tpu_custom_call" | custom-call | bytes 157286400 | tf_op jit(solution)/shard_map/start_step/pallas_call | solution.py:232
  75.8 3.2 fusion.4
  79.1 1.4 slice_convert_fusion.4
  80.5 5.6 %fusion.9 = f32[1024,768]{0,1:T(8,128)S(1)} fusion(bf16[784,2048]{1,0:T(8,128)(2,1)} %get-tuple-element.49, bf16[1024,2048]{1,0:T(8,128)(2,1)S(1)} %copy-done.12, f32[2048]{0:T(1024)S(1)} %bitcast.88, f32[1024]{0:T(1024)S(1)} %add_rsqrt_fusion.1), kind=kOutput, calls=%fused_computation.22 | convolution fusion | flops 3229614080 | bytes 10498048 | tf_op jit(solution)/shard_map/td,qd->tq/dot_general | solution.py:1015
  86.3 1.4 copy-done.8
  87.8 2.1 convolution_convert_fusion.2
  90.0 1.8 subtract_convert_fusion.4
  97.0 66.1 %front_step.1 = (f32[256,512]{1,0:T(8,128)S(1)}, bf16[1024,2048]{1,0:T(8,128)(2,1)}, bf16[1024,512]{1,0:T(8,128)(2,1)}, bf16[704,2048]{1,0:T(8,128)(2,1)}, bf16[704,2048]{1,0:T(8,128)(2,1)}) custom-call(bf16[1024,128]{1,0:T(8,128)(2,1)S(1)} %fusion.20.attended, bf16[512,512]{1,0:T(8,128)(2,1)S(1)} %pad_maximum_fusion.4.weight, ...), custom_call_target="tpu_custom_call" | custom-call | flops 536870912 | bytes 157286400 | tf_op jit(solution)/shard_map/front_step/pallas_call | solution.py:987
  163.1 25.5 %expert_step.1 = (bf16[1024,2048]{1,0:T(8,128)(2,1)}, f32[1024,128]{1,0:T(8,128)}, bf16[880,1024]{1,0:T(8,128)(2,1)}, bf16[1776,1024]{1,0:T(8,128)(2,1)}, bf16[1024,2048]{1,0:T(8,128)(2,1)}) custom-call(bf16[1024,2048]{1,0:T(8,128)(2,1)} %get-tuple-element.51.middle, bf16[1024,2048]{1,0:T(8,128)(2,1)} %get-tuple-element.52.out_grad, ...), custom_call_target="tpu_custom_call" | custom-call | flops 14763950080 | bytes 31457280 | tf_op jit(solution)/shard_map/expert_step/pallas_call | solution.py:426
  188.6 43.2 %grads_step.1 = (bf16[8,1056,512]{2,1,0:T(8,128)(2,1)}, bf16[4,144,512]{2,1,0:T(8,128)(2,1)S(1)}, bf16[16,2048]{1,0:T(8,128)(2,1)S(1)}, f32[256,512]{1,0:T(8,128)S(1)}) custom-call(bf16[1024,2048]{1,0:T(8,128)(2,1)} %get-tuple-element.57.hidden, bf16[1024,2048]{1,0:T(8,128)(2,1)} %get-tuple-element.52.out_grad, bf16[1776,1024]{1,0:T(8,128)(2,1)} %get-tuple-element.63.delta, ...), custom_call_target="tpu_custom_call" | custom-call | flops 11811160064 | bytes 62914560 | tf_op jit(solution)/shard_map/grads_step/pallas_call | solution.py:581
  234.3 14.3 %back_step.1.part = bf16[1024,2048]{1,0:T(8,128)(2,1)} custom-call(bf16[1776,1024]{1,0:T(8,128)(2,1)} %get-tuple-element.63.delta, bf16[704,2048]{1,0:T(8,128)(2,1)} %get-tuple-element.53.gates, bf16[704,2048]{1,0:T(8,128)(2,1)} %get-tuple-element.54.ups, bf16[544,2048]{1,0:T(8,128)(2,1)} %get-tuple-element.56.lows), custom_call_target="tpu_custom_call" | custom-call | flops 8858370048 | bytes 31457280 | tf_op jit(solution)/shard_map/back_step/pallas_call | solution.py:473
  248.6 75.5 %middle_step.1 = (f32[256,512]{1,0:T(8,128)S(1)}, bf16[1024,512]{1,0:T(8,128)(2,1)}, bf16[1024,128]{1,0:T(8,128)(2,1)S(1)}, f32[1,512]{1,0:T(1,128)S(1)}, bf16[4,4,144,512]{3,2,1,0:T(8,128)(2,1)}) custom-call(bf16[1024,2048]{1,0:T(8,128)(2,1)} %back_step.1.part, f32[256,512]{1,0:T(8,128)S(1)} %get-tuple-element.50.middle, bf16[256,512]{1,0:T(8,128)(2,1)S(1)} %copy-done.3, ...), custom_call_target="tpu_custom_call" | custom-call | flops 536870912 | bytes 209715200 | tf_op jit(solution)/shard_map/middle_step/pallas_call | solution.py:718
  333.4 4.1 convolution_convert_fusion.1
  339.5 9.5 %fusion.3 = (bf16[2048]{0:T(1024)(128)(2,1)S(1)}, bf16[1024,2048]{1,0:T(8,128)(2,1)}) fusion(bf16[1024,2048]{1,0:T(8,128)(2,1)} %get-tuple-element.48, f32[1024]{0:T(1024)S(1)} %copy-done.26, bf16[1024,768]{0,1:T(8,128)(2,1)} %copy-done.14, bf16[784,2048]{1,0:T(8,128)(2,1)} %get-tuple-element.49), kind=kOutput, calls=%fused_computation.7 | convolution fusion | flops 3233806336 | bytes 13115392 | tf_op jit(solution)/shard_map/tq,qd->td/dot_general | solution.py:1015
  349.2 3.5 copy.44
  352.8 1.5 convolution_convert_fusion.3
  354.3 1.6 gather_fusion
  355.9 3.8 gather_fusion.1
  359.8 2.3 convolution_convert_fusion.4
  364.1 1.7 pad_maximum_fusion
  366.7 2.2 fusion.47
  368.9 7.3 %reduce-scatter.2.cloned.1.call-done = bf16[1,1056,512]{2,1,0:T(8,128)(2,1)} async-done(((bf16[8,1056,512]{2,1,0:T(8,128)(2,1)}), bf16[1,1056,512]{2,1,0:T(8,128)(2,1)}) %reduce-scatter.2.cloned.1.call-update) | async-done | bytes 1081360 | tf_op jit(solution)/shard_map/reduce_scatter | solution.py:1163
  376.2 71.9 %tail_step.1 = (bf16[256,512]{1,0:T(8,128)(2,1)S(1)}, bf16[1536,512]{1,0:T(8,128)(2,1)}, bf16[4,144,512]{2,1,0:T(8,128)(2,1)S(1)}, f32[16,512]{1,0:T(8,128)S(1)}, bf16[4,16,512]{2,1,0:T(8,128)(2,1)S(1)}) custom-call(bf16[1024,2048]{1,0:T(8,128)(2,1)} %get-tuple-element.152.part, bf16[640,2048]{1,0:T(8,128)(2,1)} %bitcast.70, ...), custom_call_target="tpu_custom_call" | custom-call | flops 1048576 | bytes 209715200 | tf_op jit(solution)/shard_map/tail_step/pallas_call | solution.py:881
  448.1 1.3 convert_bitcast_fusion
  449.4 1.8 convert_bitcast_fusion.2
  451.2 1.6 copy.45
  452.8 2.0 copy.46
  454.9 5.1 %collective-permute-start = (bf16[1056,512]{1,0:T(8,128)(2,1)}, bf16[1056,512]{1,0:T(8,128)(2,1)S(1)}, u32[]{:S(2)}, u32[]{:S(2)}) collective-permute-start(bf16[1056,512]{1,0:T(8,128)(2,1)} %bitcast.94), channel_id=1, source_target_pairs={{0,0},{1,33},{2,66},{3,99},{16,1},{17,32},{18,67},{19,98},{32,2},{... | collective-permute-start | bytes 3244040 | tf_op jit(solution)/shard_map/ppermute | solution.py:1224
  462.3 2.1 slice_convert_fusion.3
  465.7 19.9 %collective-permute-done = bf16[1056,512]{1,0:T(8,128)(2,1)S(1)} collective-permute-done((bf16[1056,512]{1,0:T(8,128)(2,1)}, bf16[1056,512]{1,0:T(8,128)(2,1)S(1)}, u32[]{:S(2)}, u32[]{:S(2)}) %collective-permute-start) | collective-permute-done | bytes 1081376 | tf_op jit(solution)/shard_map/ppermute | solution.py:1224
  485.9 1.4 slice_bitcast_fusion
  (133 shorter events, 29.1 us)
Async XLA Ops:
  7.2 80.6 %copy-start = (bf16[512,256]{1,0:T(8,128)(2,1)S(1)}, bf16[512,256]{1,0:T(8,128)(2,1)}, u32[]{:S(2)}) copy-start(bf16[512,256]{1,0:T(8,128)(2,1)} %param.23) | copy-start | bytes 786436
  7.2 5.7 %copy-start.4 = (bf16[512,704]{0,1:T(8,128)(2,1)S(1)}, bf16[512,704]{0,1:T(8,128)(2,1)}, u32[]{:S(2)}) copy-start(bf16[512,704]{0,1:T(8,128)(2,1)} %param.27) | copy-start | bytes 2162692
  7.2 5.7 %copy-start.2 = (bf16[256,512]{1,0:T(8,128)(2,1)S(1)}, bf16[256,512]{1,0:T(8,128)(2,1)}, u32[]{:S(2)}) copy-start(bf16[256,512]{1,0:T(8,128)(2,1)} %inputs.5) | copy-start | bytes 786436
  7.2 5.7 %copy-start.3 = (bf16[256,512]{1,0:T(8,128)(2,1)S(1)}, bf16[256,512]{1,0:T(8,128)(2,1)}, u32[]{:S(2)}) copy-start(bf16[256,512]{1,0:T(8,128)(2,1)} %cotangent.3) | copy-start | bytes 786436
  7.2 369.0 %reduce-scatter.2.cloned.1.call-start = ((), (), s32[]{:S(2)}) async-start(), calls=%async_computation.1 | async-start | bytes 9732096 | tf_op jit(solution)/shard_map/reduce_scatter | solution.py:1163
  7.3 82.7 %copy-start.21 = (f32[32]{0:T(128)}, f32[32]{0:T(128)S(1)}, u32[]{:S(2)}) copy-start(f32[32]{0:T(128)S(1)} %multiply_exponential_fusion) | copy-start | bytes 388
  75.8 4.7 copy-start.12
  79.0 7.0 %copy-start.25 = (f32[1024]{0:T(1024)}, f32[1024]{0:T(1024)S(1)}, u32[]{:S(2)}) copy-start(f32[1024]{0:T(1024)S(1)} %add_rsqrt_fusion.1) | copy-start | bytes 12292
  80.5 5.6 %copy-start.23 = (f32[1,2048]{1,0:T(1,128)}, f32[1,2048]{1,0:T(1,128)S(1)}, u32[]{:S(2)}) copy-start(f32[1,2048]{1,0:T(1,128)S(1)} %get-tuple-element.131) | copy-start | bytes 24580
  80.5 7.3 %copy-start.29 = (bf16[512]{0:T(512)(128)(2,1)S(1)}, bf16[512]{0:T(512)(128)(2,1)}, u32[]{:S(2)}) copy-start(bf16[512]{0:T(512)(128)(2,1)} %param.22) | copy-start | bytes 3076
  86.1 1.6 copy-start.8
  87.8 2.2 copy-start.18
  90.0 3.7 copy-start.16
  93.7 1.9 copy-start.6
  94.3 1.9 copy-start.20
  94.3 2.6 copy-start.15
  97.0 66.1 %copy-start.1 = (bf16[512,512]{1,0:T(8,128)(2,1)}, bf16[512,512]{1,0:T(8,128)(2,1)S(1)}, u32[]{:S(2)}) copy-start(bf16[512,512]{1,0:T(8,128)(2,1)S(1)} %pad_maximum_fusion.4.weight) | copy-start | bytes 1572868
  248.6 75.6 %copy-start.7 = (f32[1024,1024]{0,1:T(8,128)S(1)}, f32[1024,1024]{0,1:T(8,128)}, u32[]{:S(2)}) copy-start(f32[1024,1024]{0,1:T(8,128)} %copy-done.6) | copy-start | bytes 12582916
  327.0 1.9 copy-start.9
  327.0 1.9 copy-start.19
  330.5 2.9 copy-start.13
  330.5 2.9 copy-start.24
  330.5 2.9 copy-start.26
  333.4 4.1 copy-start.14
  337.6 1.9 copy-start.11
  349.2 3.5 copy-start.30
  349.2 3.5 copy-start.31
  354.3 5.5 %copy-start.28 = (bf16[512]{0:T(512)(128)(2,1)S(1)}, bf16[512]{0:T(512)(128)(2,1)}, u32[]{:S(2)}) copy-start(bf16[512]{0:T(512)(128)(2,1)} %param.19) | copy-start | bytes 3076
  359.8 4.0 slice-start
  359.8 4.0 slice-start.1
  364.0 2.7 copy-start.10
  454.9 30.7 %collective-permute-start = (bf16[1056,512]{1,0:T(8,128)(2,1)}, bf16[1056,512]{1,0:T(8,128)(2,1)S(1)}, u32[]{:S(2)}, u32[]{:S(2)}) collective-permute-start(bf16[1056,512]{1,0:T(8,128)(2,1)} %bitcast.94), channel_id=1, source_target_pairs={{0,0},{1,33},{2,66},{3,99},{16,1},{17,32},{18,67},{19,98},{32,2},{... | collective-permute-start | bytes 3244040 | tf_op jit(solution)/shard_map/ppermute | solution.py:1224
  (4 other events, 3.1 us)
Sparse Core Ops, SparseCore 0:
  232.8 143.3 reduce-scatter.1

commit v5 on v4

--- a/solution.py
+++ b/solution.py
@@ -89,7 +89,7 @@
         self.own, self.full, self.go = own, full, go
         self.xs, self.ys, self.cs = sems[0:2], sems[2:4], sems[4:6]
         self.row, self.sibling, self.across = row, sibling, across
-        self.arrivals = []
+        self.arrivals, self.halves = [], []
 
     def block(self, at_row, at_col):
         rows, columns = self.own.shape
@@ -98,8 +98,8 @@
 
     def along(self, source, target, base):
         return [
-            self.go(source, target, self.ys, base + k - 1, row=lax.rem(self.row + k, 4))
-            for k in (1, 2, 3)
+            self.go(source, target, self.ys, base + n, row=lax.rem(self.row + k, 4))
+            for n, k in enumerate((1, 3))
         ]
 
     def over(self, source, target):
@@ -118,27 +118,38 @@
     def second(self):
         self.side.wait_recv()
         here = self.block(self.row, 2)
-        self.rest = self.along(here, here, 3)
+        self.rest = self.along(here, here, 2)
         self.over(here, self.block(self.row, 3))
 
-    def forward(self, group, at_col):
-        for k in (1, 3, 2):
-            group[k - 1].wait_recv()
+    def forward(self, group, at_col, base):
+        rows, columns = self.own.shape
+        for n, k in enumerate((1, 3)):
+            group[n].wait_recv()
             source = lax.rem(self.row + 4 - k, 4)
+            start = pl.multiple_of(source * rows + n * (rows // 2), rows // 2)
+            half = self.full.at[pl.ds(start, rows // 2), pl.ds(at_col * columns, columns)]
+            self.halves.append(
+                self.go(half, half, self.ys, base + n, row=lax.rem(self.row + k, 4))
+            )
             self.over(self.block(source, at_col), self.block(source, at_col + 1))
 
     def forward_first(self):
-        self.forward(self.first, 0)
+        self.forward(self.first, 0, 4)
 
     def forward_rest(self):
-        self.forward(self.rest, 2)
+        self.forward(self.rest, 2, 6)
 
     def finish(self):
+        facing = lax.rem(self.row + 2, 4)
+        for n, at_col in enumerate((0, 2)):
+            for copy in self.halves[2 * n : 2 * n + 2]:
+                copy.wait_recv()
+            self.over(self.block(facing, at_col), self.block(facing, at_col + 1))
         for copy in self.arrivals:
             copy.wait_recv()
 
 
-gather_scratch = pair(1) + pair(6) + pair(8)
+gather_scratch = pair(1) + pair(8) + pair(8)
 
 
 class Deal:
@@ -187,8 +198,7 @@
 
 
 def start_kernel(
-    inputs, cotangent, common, query, gate, low_gate, low_up, router, low_down,
-    full, out_grad, project, gates, lows, *sems,
+    inputs, common, query, gate, full, project, gates, *sems,
 ):
     row, sibling, across, corner = place()
     col = lax.axis_index("col")
@@ -197,54 +207,39 @@
     pending = []
     go = starter(pending)
     gather = Gather(inputs, full, sems[0:6], go, row, sibling, across)
-    beside = Gather(cotangent, out_grad, sems[6:12], go, row, sibling, across)
-    deal = Deal(sems[12:14], sems[14], pending, col, peers)
+    deal = Deal(sems[6:8], sems[8], pending, col, peers)
     ff = gate.shape[1]
-    low = low_down.shape[0] // 4
     gather.begin()
     deal.send(lambda column: common.at[pl.ds(0, RANK)], lanes(project, 0, RANK), True)
     deal.send(rows_at(query, 192), lanes(project, RANK, 192), False)
     deal.send(lambda column: common.at[pl.ds(RANK, 80)], lanes(project, RANK + 192, 80), False)
-    beside.begin()
     gather.second()
     for e in (0, 1):
         deal.send(lambda column, e=e: gate.at[2 * column + e], lanes(gates, e * ff, ff), e == 1)
-    beside.second()
-    deal.send(rows_at(low_gate, low), lanes(lows, 0, low), True)
-    deal.send(rows_at(low_up, low), lanes(lows, low, low), False)
-    deal.send(lambda column: router, lanes(lows, 2 * low, 16), True)
-    deal.send(rows_at(low_down, low), lanes(lows, 2 * low + 16, low), True)
     gather.forward_first()
     gather.forward_rest()
-    beside.forward_first()
-    beside.forward_rest()
     gather.finish()
-    beside.finish()
     deal.finish()
     for copy in pending:
         copy.wait_send()
 
 
-def start_step(inputs, cotangent, common, query, gate, low_gate, low_up, router, low_down):
+def start_step(inputs, common, query, gate):
     rows, columns = inputs.shape
-    low = low_down.shape[0] // 4
-    wide = jax.ShapeDtypeStruct((4 * rows, 4 * columns), bf16)
     return pl.pallas_call(
         start_kernel,
         out_shape=(
-            wide,
-            wide,
+            jax.ShapeDtypeStruct((4 * rows, 4 * columns), bf16),
             jax.ShapeDtypeStruct((RANK + 272, 4 * columns), bf16),
             jax.ShapeDtypeStruct((2 * gate.shape[1], 4 * columns), bf16),
-            jax.ShapeDtypeStruct((3 * low + 16, 4 * columns), bf16),
         ),
-        in_specs=[VMEM] * 2 + [HBM] * 7,
-        out_specs=(VMEM, VMEM, HBM, HBM, HBM),
-        scratch_shapes=[*gather_scratch, *gather_scratch, *deal_scratch(9)],
+        in_specs=[VMEM] + [HBM] * 3,
+        out_specs=(VMEM, HBM, HBM),
+        scratch_shapes=[*gather_scratch, *deal_scratch(5)],
         compiler_params=params(0),
         cost_estimate=cost(0, 150),
         name="start_step",
-    )(inputs, cotangent, common, query, gate, low_gate, low_up, router, low_down)
+    )(inputs, common, query, gate)
 
 
 def reduce_scratch(rows, columns):
@@ -413,6 +408,12 @@
     return pl.BlockSpec(value.shape, lambda i: (0,) * len(value.shape))
 
 
+def once(value):
+    return pl.BlockSpec(
+        value.shape, lambda i: (0,) * len(value.shape), pipeline_mode=pl.Buffered(1)
+    )
+
+
 def expert_step(middle, out_grad, gates, ups, downs, lows, gain, named, mine):
     tile = 256
     tokens, width = middle.shape
@@ -457,38 +458,9 @@
     )(middle, out_grad, gates, ups, downs, lows, gain, named, mine)
 
 
-def back_kernel(delta, gates, ups, lows, hidden_grad):
-    ff = gates.shape[0]
-    low = lows.shape[0] - 16 - (lows.shape[0] - 16) // 3 + 16
-    hidden_grad[...] = (
-        over_units(delta[pl.ds(0, ff), :], gates[...])
-        + over_units(delta[pl.ds(ff, ff), :], ups[...])
-        + over_units(delta[pl.ds(2 * ff, low), :], lows[pl.ds(0, low), :])
-    ).astype(bf16)
-
-
-def back_step(delta, gates, ups, lows):
-    tile = 256
-    tokens, width = delta.shape[1], gates.shape[1]
-    return pl.pallas_call(
-        back_kernel,
-        grid=(tokens // tile,),
-        out_shape=jax.ShapeDtypeStruct((tokens, width), bf16),
-        in_specs=[
-            pl.BlockSpec((delta.shape[0], tile), lambda i: (0, i)),
-            whole(gates),
-            whole(ups),
-            whole(lows),
-        ],
-        out_specs=pl.BlockSpec((tile, width), lambda i: (i, 0)),
-        compiler_params=pltpu.CompilerParams(vmem_limit_bytes=56 << 20),
-        cost_estimate=cost(2 * 3 * gates.shape[0] * width * tokens, 30),
-        name="back_step",
-    )(delta, gates, ups, lows)
-
-
 def grads_kernel(
-    hidden, out_grad, delta, act, combined, grads, shared, router, total,
+    hidden, out_grad, delta, act, combined, gates, ups, lows,
+    grads, shared, router, total, hidden_grad,
     own_shared, chunk_in, ps, pr, *scratch, ff, low,
 ):
     step = pl.program_id(0)
@@ -560,7 +532,16 @@
             grads[0, pl.ds(ff, ff), :] = product(delta[pl.ds(2 * ff + at, ff), :], hidden[...])
             grads[0, pl.ds(2 * ff, ff), :] = product(act[pl.ds(at, ff), :], out_grad[...])
 
-    @pl.when(step == 11)
+    @pl.when(step >= 12)
+    def _():
+        at = pl.ds(pl.multiple_of((step - 12) * 256, 256), 256)
+        hidden_grad[...] = (
+            over_units(delta[pl.ds(0, 2 * ff), at], gates[...])
+            + over_units(delta[pl.ds(2 * ff, 2 * ff), at], ups[...])
+            + over_units(delta[pl.ds(4 * ff, 2 * low + 16), at], lows[pl.ds(0, 2 * low + 16), :])
+        ).astype(bf16)
+
+    @pl.when(step == 15)
     def _():
         steps.collect(0)
         total[...] = steps.total()
@@ -574,25 +555,28 @@
         steps.finish()
 
 
-def grads_step(hidden, out_grad, delta, act, combined, ff, low):
+def grads_step(hidden, out_grad, delta, act, combined, gates, ups, lows):
     tokens = hidden.shape[0]
+    ff, low = gates.shape[0] // 2, (lows.shape[0] - 16) // 3
     piece = -(-3 * low // 64) * 16
     wide = pl.BlockSpec((tokens, 512), lambda i: (0, i % 4))
     return pl.pallas_call(
         functools.partial(grads_kernel, ff=ff, low=low),
-        grid=(12,),
+        grid=(16,),
         out_shape=(
             jax.ShapeDtypeStruct((8, 3 * ff, 512), bf16),
             jax.ShapeDtypeStruct((4, piece, 512), bf16),
             jax.ShapeDtypeStruct((16, D), bf16),
             jax.ShapeDtypeStruct((tokens // 4, 512), f32),
+            jax.ShapeDtypeStruct((tokens, D), bf16),
         ),
-        in_specs=[wide, wide, whole(delta), whole(act), whole(combined)],
+        in_specs=[wide, wide] + [once(v) for v in (delta, act, combined, gates, ups, lows)],
         out_specs=(
-            pl.BlockSpec((1, 3 * ff, 512), lambda i: (jnp.maximum(i - 4, 0), 0, 0)),
+            pl.BlockSpec((1, 3 * ff, 512), lambda i: (jnp.clip(i - 4, 0, 7), 0, 0)),
             pl.BlockSpec((4, piece, 512), lambda i: (0, 0, 0)),
             pl.BlockSpec((16, 512), lambda i: (0, jnp.minimum(i, 3))),
             pl.BlockSpec((tokens // 4, 512), lambda i: (0, 0)),
+            pl.BlockSpec((256, D), lambda i: (jnp.maximum(i - 12, 0), 0)),
         ),
         scratch_shapes=[
             pltpu.VMEM((4, 4 * piece, 512), bf16),
@@ -603,7 +587,7 @@
         compiler_params=params(1),
         cost_estimate=cost(2 * 8 * 4 * ff * 512 * tokens, 60),
         name="grads_step",
-    )(hidden, out_grad, delta, act, combined)
+    )(hidden, out_grad, delta, act, combined, gates, ups, lows)
 
 
 class ColumnSum:
@@ -630,6 +614,9 @@
     row, sibling, across, corner = place()
     dp = lax.axis_index("dp")
     z = lax.rem(dp, 4)
+    col = lax.axis_index("col")
+    piece = shared.shape[1]
+    quarter = pl.ds(pl.multiple_of(z * piece, piece), piece)
     far = lax.rem(dp + 4, 8)
     peers = (sibling, across, corner)
     greet(peers, row, [{"dp": along_z(dp, k)} for k in (1, 2, 3)] + [{"dp": far}])
@@ -644,9 +631,9 @@
     steps.over()
     halves.wait_recv()
     both[...] = (shared[...].astype(f32) + chunk_in[...].astype(f32)).astype(bf16)
-    shared_all[z, 0] = both[0]
+    shared_all[col, quarter, :] = both[0]
     home = [
-        go(both.at[j + 1], shared_all.at[z, j + 1], (ps, pr), 1 + j, col=peer)
+        go(both.at[j + 1], shared_all.at[col, quarter], (ps, pr), 1 + j, col=peer)
         for j, peer in enumerate(peers)
     ]
     steps.collect(0)
@@ -661,7 +648,13 @@
     for copy in home:
         copy.wait_recv()
     spread = [
-        go(shared_all.at[z], shared_all.at[z], (ps, pr), 3 + k, dp=along_z(dp, k))
+        go(
+            shared_all.at[:, quarter],
+            shared_all.at[:, quarter],
+            (ps, pr),
+            3 + k,
+            dp=along_z(dp, k),
+        )
         for k in (1, 2, 3)
     ]
     base = cotangent[...].astype(f32) + scales * weighted
@@ -722,7 +715,7 @@
             jax.ShapeDtypeStruct((4 * rows, columns), bf16),
             jax.ShapeDtypeStruct((4 * rows, VDIM), bf16),
             jax.ShapeDtypeStruct((1, columns), f32),
-            jax.ShapeDtypeStruct((4, 4, piece, columns), bf16),
+            jax.ShapeDtypeStruct((4, 4 * piece, columns), bf16),
         ),
         in_specs=[VMEM] * 7,
         out_specs=(VMEM,) * 5,
@@ -912,9 +905,29 @@
     )(part, narrow_part, query, ready, residual_grad, inputs, scale, gain, gain_part)
 
 
+score_scale = (NOPE + ROPE) ** (-0.5)
+
+
+def swap_halves(values):
+    lane = lax.broadcasted_iota(jnp.int32, values.shape, 1)
+    return jnp.where(
+        lax.rem(lane, 64) < 32, pltpu.roll(values, 96, 1), pltpu.roll(values, 32, 1)
+    )
+
+
+def masked_scores(queries, keys, early, start):
+    scores = times_rows(queries, keys) * score_scale
+    query_pos = start + lax.broadcasted_iota(jnp.int32, scores.shape, 0)
+    key_pos = lax.broadcasted_iota(jnp.int32, scores.shape, 1)
+    return jnp.where((key_pos <= query_pos) | (early > 0.0), scores, masked_score)
+
+
 def front_kernel(
-    attended, weight, inputs, up, down, middle, full, attended_rows, ups, downs,
-    own, out_buf, in_buf, acc, as_, ar, ps, pr, *sems,
+    input_rows, project, expand, weight, inputs, cotangent, cosine, sine, early, gain,
+    up, down, low_gate, low_up, router, low_down,
+    middle, full, attended_rows, out_grad, normed, scale, content, latent_scale, compact,
+    queries, keys, values, log_total, ups, downs, lows,
+    attended, own, out_buf, in_buf, acc, as_, ar, ps, pr, *sems,
 ):
     row, sibling, across, corner = place()
     peers = (sibling, across, corner)
@@ -924,46 +937,94 @@
     rows, columns = inputs.shape
     head = attended.shape[1]
     order = (2, 1, 3, 0)
+    beside = Gather(cotangent, out_grad, sems[6:12], go, row, sibling, across)
+    deal = Deal(sems[12:14], sems[14], pending, lax.axis_index("col"), peers)
+    ff = up.shape[1]
+    low = low_down.shape[0] // 4
+    beside.begin()
+    for e in (0, 1):
+        deal.send(lambda column, e=e: up.at[2 * column + e], lanes(ups, e * ff, ff), e == 1)
+
+    first_gain = project[pl.ds(RANK + 256, 16), :].astype(f32)[:1]
+    for i in range(4):
+        at = pl.ds(i * rows, rows)
+        wide = input_rows[at, :].astype(f32)
+        scales = lax.rsqrt(jnp.mean(wide * wide, axis=1, keepdims=True) + norm_eps)
+        scale[at, :] = scales
+        normal = (wide * scales * first_gain).astype(bf16)
+        normed[at, :] = normal
+        projected = times_rows(normal, project[pl.ds(0, RANK + 256), :])
+        inner = projected[:, :RANK]
+        inner_scale = lax.rsqrt(jnp.mean(inner * inner, axis=1, keepdims=True) + norm_eps)
+        content[at, :] = inner
+        latent_scale[at, :] = inner_scale
+        narrow = (inner * inner_scale * gain[...]).astype(bf16)
+        compact[at, :] = narrow
+        pair_rows = jnp.dot(narrow, expand[...], preferred_element_type=f32)
+        both = projected[:, RANK + NOPE :]
+        both = both * cosine[at, :] + swap_halves(both) * sine[at, :]
+        lane = lax.broadcasted_iota(jnp.int32, both.shape, 1)
+        queries[at, pl.ds(0, NOPE)] = projected[:, RANK : RANK + NOPE].astype(bf16)
+        queries[at, pl.ds(NOPE, 128)] = jnp.where(lane < ROPE, both, 0.0).astype(bf16)
+        keys[at, pl.ds(0, NOPE)] = pair_rows[:, :NOPE].astype(bf16)
+        keys[at, pl.ds(NOPE, 128)] = jnp.where(
+            lane < ROPE, pltpu.roll(both, 64, 1), 0.0
+        ).astype(bf16)
+        values[at, :] = pair_rows[:, NOPE:].astype(bf16)
+    beside.second()
+    deal.send(rows_at(low_gate, low), lanes(lows, 0, low), True)
+    deal.send(rows_at(low_up, low), lanes(lows, low, low), False)
+    deal.send(lambda column: router, lanes(lows, 2 * low, 16), True)
+    deal.send(rows_at(low_down, low), lanes(lows, 2 * low + 16, low), True)
+
+    def start_of(k):
+        return pl.multiple_of(lax.rem(row + k, 4) * rows, rows)
 
     def block(k):
-        return pl.ds(pl.multiple_of(lax.rem(row + k, 4) * rows, rows), rows)
+        return pl.ds(start_of(k), rows)
 
     def slot(k):
         return pl.ds(k * head, head)
 
     got = {}
     for k in order:
-        got[2, k] = go(
-            attended.at[block(k)], attended_rows.at[block(k), slot(2)], (as_, ar), (1, k), col=across
-        )
-    for k in order:
-        got[1, k] = go(
-            attended.at[block(k)], attended_rows.at[block(k), slot(1)], (as_, ar), (0, k), col=sibling
-        )
-    attended_rows[:, slot(0)] = attended[...]
-    deal = Deal(sems[6:8], sems[8], pending, lax.axis_index("col"), peers)
-    ff = up.shape[1]
+        scores = masked_scores(queries[block(k), :], keys[...], early[...], start_of(k))
+        top = jnp.max(scores, axis=1, keepdims=True)
+        powers = jnp.exp(scores - top)
+        power_sum = jnp.sum(powers, axis=1, keepdims=True)
+        log_total[block(k), :] = top + jnp.log(power_sum)
+        probs = (powers / power_sum).astype(bf16)
+        attended[block(k), :] = jnp.dot(
+            probs, values[...], preferred_element_type=f32
+        ).astype(bf16)
+        for j, peer in ((2, across), (1, sibling)):
+            got[j, k] = go(
+                attended.at[block(k)],
+                attended_rows.at[block(k), slot(j)],
+                (as_, ar),
+                (j - 1, k),
+                col=peer,
+            )
+        attended_rows[block(k), slot(0)] = attended[block(k), :]
+    beside.forward_first()
     for k in order:
         got[2, k].wait_recv()
         view = attended_rows.at[block(k), slot(2)]
-        got[3, k] = go(
-            view, attended_rows.at[block(k), slot(3)], (as_, ar), (2, k), col=sibling
-        )
+        got[3, k] = go(view, attended_rows.at[block(k), slot(3)], (as_, ar), (2, k), col=sibling)
     for e in (0, 1):
-        deal.send(lambda column, e=e: up.at[2 * column + e], lanes(ups, e * ff, ff), e == 1)
         deal.send(lambda column, e=e: down.at[2 * column + e], lanes(downs, e * ff, ff), e == 1)
     sent = {}
     for k in order:
         got[1, k].wait_recv()
         got[3, k].wait_recv()
-        product = jnp.dot(attended_rows[block(k), :], weight[...], preferred_element_type=f32)
+        result = jnp.dot(attended_rows[block(k), :], weight[...], preferred_element_type=f32)
         if k:
-            out_buf[k - 1] = product.astype(bf16)
+            out_buf[k - 1] = result.astype(bf16)
             sent[k] = go(
                 out_buf.at[k - 1], in_buf.at[k - 1], (ps, pr), k - 1, row=lax.rem(row + k, 4)
             )
         else:
-            acc[...] = product + inputs[...].astype(f32)
+            acc[...] = result + inputs[...].astype(f32)
     total = acc[...]
     for k in (1, 3, 2):
         sent[k].wait_recv()
@@ -972,30 +1033,52 @@
     own[...] = total.astype(bf16)
     gather = Gather(own, full, sems[:6], go, row, sibling, across)
     gather.begin()
+    beside.forward_rest()
     gather.second()
     gather.forward_first()
     gather.forward_rest()
+    beside.finish()
     gather.finish()
     deal.finish()
     for copy in pending:
         copy.wait_send()
 
 
-def front_step(attended, weight, inputs, up, down):
+def front_step(
+    input_rows, project, expand, weight, inputs, cotangent, cosine, sine, early, gain,
+    up, down, low_gate, low_up, router, low_down,
+):
     rows, columns = inputs.shape
-    dealt = jax.ShapeDtypeStruct((2 * up.shape[1], 4 * columns), bf16)
+    tokens, width = input_rows.shape
+    low = low_down.shape[0] // 4
+
+    def array(*shape, kind=bf16):
+        return jax.ShapeDtypeStruct(shape, kind)
+
     return pl.pallas_call(
         front_kernel,
         out_shape=(
-            jax.ShapeDtypeStruct((rows, columns), f32),
-            jax.ShapeDtypeStruct((4 * rows, 4 * columns), bf16),
-            jax.ShapeDtypeStruct((4 * rows, columns), bf16),
-            dealt,
-            dealt,
+            array(rows, columns, kind=f32),
+            array(tokens, width),
+            array(tokens, columns),
+            array(tokens, width),
+            array(tokens, width),
+            array(tokens, 1, kind=f32),
+            array(tokens, RANK, kind=f32),
+            array(tokens, 1, kind=f32),
+            array(tokens, RANK),
+            array(tokens, 256),
+            array(tokens, 256),
+            array(tokens, VDIM),
+            array(tokens, 1, kind=f32),
+            array(2 * up.shape[1], width),
+            array(2 * up.shape[1], width),
+            array(3 * low + 16, width),
         ),
-        in_specs=[VMEM] * 3 + [HBM] * 2,
-        out_specs=(VMEM,) * 3 + (HBM,) * 2,
+        in_specs=[VMEM] * 10 + [HBM] * 6,
+        out_specs=(VMEM,) * 13 + (HBM,) * 3,
         scratch_shapes=[
+            pltpu.VMEM((tokens, VDIM), bf16),
             pltpu.VMEM((rows, columns), bf16),
             pltpu.VMEM((3, rows, columns), bf16),
             pltpu.VMEM((3, rows, columns), bf16),
@@ -1003,16 +1086,121 @@
             *pair(3, 4),
             *pair(3),
             *gather_scratch,
-            *deal_scratch(4),
+            *gather_scratch,
+            *deal_scratch(8),
         ],
         compiler_params=params(5),
-        cost_estimate=cost(1 << 29, 150),
+        cost_estimate=cost(1 << 33, 150),
         name="front_step",
-    )(attended, weight, inputs, up, down)
-
-
-def dot(spec, left, right, kind=f32):
-    return jnp.einsum(spec, left, right, preferred_element_type=f32).astype(kind)
+    )(
+        input_rows, project, expand, weight, inputs, cotangent, cosine, sine, early, gain,
+        up, down, low_gate, low_up, router, low_down,
+    )
+
+
+def attend_back_kernel(
+    queries, keys, values, log_total, attended_grad, early, compact, content, latent_scale, gain,
+    expand, cosine, sine, project, normed, input_rows, scale, attended_rows, residual_rows, router,
+    normed_grad, narrow, query_part, ready,
+    query_grad, key_grad, value_grad, pair_grad, project_grad, first_sum, gain_sum,
+):
+    tile = 256
+    col = lax.axis_index("col")
+    tokens = queries.shape[0]
+    key_grad[...] = jnp.zeros_like(key_grad)
+    value_grad[...] = jnp.zeros_like(value_grad)
+    first_sum[...] = jnp.zeros_like(first_sum)
+    gain_sum[...] = jnp.zeros_like(gain_sum)
+    for i in range(tokens // tile):
+        at = pl.ds(i * tile, tile)
+        query = queries[at, :]
+        upstream = attended_grad[at, :]
+        scores = masked_scores(query, keys[...], early[...], i * tile)
+        probs = jnp.exp(scores - log_total[at, :])
+        value_grad[...] += over_units(probs.astype(bf16), upstream)
+        weight_grad = times_rows(upstream, values[...])
+        centre = jnp.sum(probs * weight_grad, axis=1, keepdims=True)
+        score_grad = (probs * (weight_grad - centre)).astype(bf16)
+        query_grad[at, :] = (
+            jnp.dot(score_grad, keys[...], preferred_element_type=f32) * score_scale
+        )
+        key_grad[...] += over_units(score_grad, query)
+    for i in range(tokens // tile):
+        at = pl.ds(i * tile, tile)
+        keys_back = key_grad[at, :] * score_scale
+        query_back = query_grad[at, :]
+        pair_rows = jnp.concatenate([keys_back[:, :NOPE], value_grad[at, :]], axis=1).astype(bf16)
+        pair_grad[at, :] = pair_rows
+        compact_grad = times_rows(pair_rows, expand[...])
+        inner = content[at, :]
+        scales = latent_scale[at, :]
+        weighted = compact_grad * gain[...]
+        inner_sum = jnp.sum(weighted * inner, axis=1, keepdims=True)
+        content_grad = scales * weighted - inner * (scales * scales * scales * inner_sum / RANK)
+        gain_sum[...] += jnp.sum(compact_grad * inner * scales, axis=0, keepdims=True)
+        both = query_back[:, NOPE:]
+        lane = lax.broadcasted_iota(jnp.int32, both.shape, 1)
+        both = jnp.where(lane < ROPE, both, pltpu.roll(keys_back[:, NOPE:], 64, 1))
+        both = both * cosine[at, :] - swap_halves(both) * sine[at, :]
+        rows = jnp.concatenate([content_grad, query_back[:, :NOPE], both], axis=1).astype(bf16)
+        project_grad[at, :] = rows
+        back = jnp.dot(rows, project[pl.ds(0, RANK + 256), :], preferred_element_type=f32)
+        normed_grad[at, :] = back.astype(bf16)
+        first_sum[...] += jnp.sum(
+            back * (input_rows[at, :].astype(f32) * scale[at, :]), axis=0, keepdims=True
+        )
+    each = narrow.shape[0] // 4
+    lat = each - 16
+    for k in range(4):
+        lanes_at = pl.ds(512 * k, 512)
+        part = over_units(project_grad[...], normed[:, lanes_at]).astype(bf16)
+        query_part[:, lanes_at] = part[RANK : RANK + 192]
+        latent_part = jnp.concatenate([part[:RANK], part[RANK + 192 :]], axis=0)
+        extra = jnp.concatenate(
+            [
+                gain_sum[...],
+                first_sum[:, lanes_at],
+                router[pl.ds(0, EXPERTS), lanes_at].astype(f32),
+                jnp.zeros((6, 512), f32),
+            ],
+            axis=0,
+        ).astype(bf16)
+        for r in range(4):
+            narrow[pl.ds(r * each, lat), lanes_at] = latent_part[r * lat : (r + 1) * lat]
+            narrow[pl.ds(r * each + lat, 16), lanes_at] = extra
+    head_grad = over_units(attended_rows[...], residual_rows[...]).astype(bf16)
+    for k in range(4):
+        own = lax.rem(lax.rem(col, 2) + k % 2, 2) + 2 * lax.rem(col // 2 + k // 2, 2)
+        start = pl.multiple_of(own * VDIM, VDIM)
+        ready[pl.ds(start, VDIM), :] = head_grad[k * VDIM : (k + 1) * VDIM]
+    ready[pl.ds(4 * VDIM, 256), :] = over_units(pair_grad[...], compact[...]).astype(bf16)
+
+
+def attend_back_step(*arguments):
+    tokens, width = arguments[15].shape
+    return pl.pallas_call(
+        attend_back_kernel,
+        out_shape=(
+            jax.ShapeDtypeStruct((tokens, width), bf16),
+            jax.ShapeDtypeStruct((RANK + ROPE + 64, width), bf16),
+            jax.ShapeDtypeStruct((192, width), bf16),
+            jax.ShapeDtypeStruct((768, 512), bf16),
+        ),
+        in_specs=[VMEM] * 20,
+        out_specs=(VMEM,) * 4,
+        scratch_shapes=[
+            pltpu.VMEM((tokens, 256), f32),
+            pltpu.VMEM((tokens, 256), f32),
+            pltpu.VMEM((tokens, VDIM), f32),
+            pltpu.VMEM((tokens, 256), bf16),
+            pltpu.VMEM((tokens, RANK + 256), bf16),
+            pltpu.VMEM((1, width), f32),
+            pltpu.VMEM((1, RANK), f32),
+        ],
+        compiler_params=pltpu.CompilerParams(vmem_limit_bytes=56 << 20),
+        cost_estimate=cost(1 << 34, 40),
+        name="attend_back_step",
+    )(*arguments)
 
 
 def rotary_tables(length, half_width):
@@ -1022,55 +1210,10 @@
     return (jnp.cos(angles), jnp.sin(angles))
 
 
-def rotate(values, cos_table, sin_table):
-    half_width = cos_table.shape[-1]
-    first_half = values[..., :half_width]
-    second_half = values[..., half_width:]
-    return jnp.concatenate(
-        [
-            first_half * cos_table - second_half * sin_table,
-            second_half * cos_table + first_half * sin_table,
-        ],
-        axis=-1,
-    )
-
-
 def pad_to(values, axis, size):
     widths = [(0, 0)] * values.ndim
     widths[axis] = (0, size - values.shape[axis])
     return jnp.pad(values, widths)
-
-
-def visible_mask(offset, block_rows, prefix_len):
-    query_pos = offset + jnp.arange(block_rows, dtype=jnp.int32)
-    key_pos = jnp.arange(SEQ, dtype=jnp.int32)
-    return (key_pos[None, :] <= query_pos[:, None]) | (key_pos[None, :] < prefix_len)
-
-
-def attend_forward(queries, key_rows, value_rows, prefix_len):
-    score_scale = (NOPE + ROPE) ** (-0.5)
-    scores = dot("qd,kd->qk", queries, key_rows) * score_scale
-    scores = jnp.where(visible_mask(0, SEQ, prefix_len), scores, masked_score)
-    top_score = jnp.max(scores, axis=1, keepdims=True)
-    exp_scores = jnp.exp(scores - top_score)
-    row_total = jnp.sum(exp_scores, axis=1, keepdims=True)
-    weights = (exp_scores / row_total).astype(bf16)
-    result = dot("qk,kd->qd", weights, value_rows)
-    return (result, (top_score + jnp.log(row_total))[:, 0])
-
-
-def attend_backward(queries, key_rows, value_rows, log_total, out_grad, prefix_len):
-    score_scale = (NOPE + ROPE) ** (-0.5)
-    scores = dot("qd,kd->qk", queries, key_rows) * score_scale
-    scores = jnp.where(visible_mask(0, SEQ, prefix_len), scores, masked_score)
-    weights = jnp.exp(scores - log_total[:, None])
-    value_grad = dot("qk,qd->kd", weights.astype(bf16), out_grad)
-    weight_grad = dot("qd,kd->qk", out_grad, value_rows)
-    centre = jnp.sum(weights * weight_grad, axis=1, keepdims=True)
-    score_grad = (weights * (weight_grad - centre)).astype(bf16)
-    query_grad = dot("qk,kd->qd", score_grad, key_rows) * score_scale
-    key_grad = dot("qk,qd->kd", score_grad, queries) * score_scale
-    return (query_grad, key_grad, value_grad)
 
 
 def on_device(
@@ -1100,54 +1243,57 @@
     first_gain = attention_gain.astype(f32)
     second_gain = feedforward_gain.astype(f32)
     compact_gain = latent_gain.astype(f32)
-    residual_in = inputs.astype(f32)
     rows = inputs.shape[0]
     ff = expert_gate.shape[2]
     low = shared_down.shape[0] // 4
+    cosine = jnp.tile(cos_table, (1, 4))
+    sine = jnp.tile(jnp.concatenate([-sin_table, sin_table], axis=1), (1, 2))
+    early = (jnp.arange(SEQ, dtype=jnp.int32) < prefix_len).astype(f32)[None, :]
 
     gains = jnp.stack([attention_gain, feedforward_gain])
     common = jnp.concatenate([latent_weight.T, pad_to(gains, 0, 16)], axis=0)
-    input_rows, out_grad, project_all, gates, lows = start_step(
+    input_rows, project_all, gates = start_step(
+        inputs, common, query_weight.T, expert_gate.transpose(0, 2, 1)
+    )
+    second_all = project_all[RANK + 257].astype(f32)
+    out_weight = jnp.concatenate(
+        [lax.dynamic_slice_in_dim(output_weight, (col ^ k) * VDIM, VDIM, 0) for k in range(4)],
+        axis=0,
+    )
+    (
+        residual_mid,
+        middle_rows,
+        attended_rows,
+        out_grad,
+        normed,
+        scale_one,
+        content,
+        latent_scale,
+        compact,
+        queries,
+        keys,
+        values,
+        log_total,
+        ups,
+        downs,
+        lows,
+    ) = front_step(
+        input_rows,
+        project_all,
+        expand_weight,
+        out_weight,
         inputs,
         cotangent,
-        common,
-        query_weight.T,
-        expert_gate.transpose(0, 2, 1),
+        cosine,
+        sine,
+        early,
+        compact_gain[None, :],
+        expert_up.transpose(0, 2, 1),
+        expert_down,
         shared_gate.T,
         shared_up.T,
         pad_to(router_weight.T, 0, 16),
         shared_down,
-    )
-    project_weight = project_all[: RANK + 256]
-    first_all = project_all[RANK + 256].astype(f32)
-    second_all = project_all[RANK + 257].astype(f32)
-    out_weight = jnp.concatenate(
-        [lax.dynamic_slice_in_dim(output_weight, (col ^ k) * VDIM, VDIM, 0) for k in range(4)],
-        axis=0,
-    )
-    order = col ^ jnp.arange(4, dtype=jnp.int32)
-
-    input_rows = input_rows.astype(f32)
-    scale_one = lax.rsqrt(jnp.mean(input_rows * input_rows, axis=1) + norm_eps)
-    normed = (input_rows * scale_one[:, None] * first_all[None, :]).astype(bf16)
-    projected = dot("td,qd->tq", normed, project_weight)
-    content = projected[:, :RANK]
-    latent_scale = lax.rsqrt(jnp.mean(content * content, axis=1) + norm_eps)
-    compact = (content * latent_scale[:, None] * compact_gain[None, :]).astype(bf16)
-    shared_key = rotate(projected[:, RANK + 192 :], cos_table, sin_table).astype(bf16)
-    key_value = dot("tr,rk->tk", compact, expand_weight, bf16)
-    query_rot = jnp.concatenate(
-        [
-            projected[:, RANK : RANK + NOPE],
-            rotate(projected[:, RANK + NOPE : RANK + 192], cos_table, sin_table),
-        ],
-        axis=1,
-    ).astype(bf16)
-    key_rows = jnp.concatenate([key_value[:, :NOPE], shared_key], axis=1)
-    value_rows = key_value[:, NOPE:]
-    head_result, log_total = attend_forward(query_rot, key_rows, value_rows, prefix_len)
-    residual_mid, middle_rows, attended_rows, ups, downs = front_step(
-        head_result.astype(bf16), out_weight, inputs, expert_up.transpose(0, 2, 1), expert_down
     )
 
     experts = jnp.arange(EXPERTS, dtype=jnp.int32)
@@ -1156,15 +1302,13 @@
     hidden, scale_two, act, delta, combined = expert_step(
         middle_rows, out_grad, gates, ups, downs, lows, second_all[None, :], named, mine
     )
-    expert_grad, shared_grad, router_part, combined_sum = grads_step(
-        hidden, out_grad, delta, act, combined, ff, low
+    expert_grad, shared_grad, router_part, combined_sum, hidden_grad = grads_step(
+        hidden, out_grad, delta, act, combined, gates, ups, lows
     )
     output = (residual_mid + combined_sum).astype(bf16)
     expert_sum = lax.psum_scatter(expert_grad, "dp", scatter_dimension=0, tiled=True)[0]
-    delta, expert_grad = lax.optimization_barrier((delta, expert_grad))
-    hidden_grad = back_step(delta, gates, ups, lows)
-
-    my_scale_one = lax.dynamic_slice_in_dim(scale_one, row * rows, rows, 0)[:, None]
+
+    my_scale_one = lax.dynamic_slice_in_dim(scale_one, row * rows, rows, 0)
     my_scale_two = lax.dynamic_slice_in_dim(scale_two[:, :1], row * rows, rows, 0)
     residual_grad, residual_rows, attended_grad, second_gain_part, shared_all = middle_step(
         hidden_grad,
@@ -1175,64 +1319,46 @@
         out_weight,
         shared_grad,
     )
-    head_grad = dot("th,td->hd", attended_rows, residual_rows, bf16)
-    output_weight_grad = head_grad.reshape(4, VDIM, 512)[order].reshape(4 * VDIM, 512)
-    query_rot_grad, key_grad, value_grad = attend_backward(
-        query_rot, key_rows, value_rows, log_total, attended_grad, prefix_len
-    )
-    pair_grad = jnp.concatenate([key_grad[:, :NOPE], value_grad], axis=1).astype(bf16)
-    expand_part = dot("tk,tr->kr", pair_grad, compact, bf16)
-    compact_grad = dot("tk,rk->tr", pair_grad, expand_weight)
-    weighted_compact = compact_grad * compact_gain[None, :]
-    inner_sum = jnp.sum(weighted_compact * content, axis=1)
-    content_grad = (
-        latent_scale[:, None] * weighted_compact
-        - content * (latent_scale * latent_scale * latent_scale * inner_sum / RANK)[:, None]
-    )
-    latent_gain_part = jnp.sum(compact_grad * content * latent_scale[:, None], axis=0)
-    project_grad = jnp.concatenate(
-        [
-            content_grad,
-            query_rot_grad[:, :NOPE],
-            rotate(query_rot_grad[:, NOPE:], cos_table, -sin_table),
-            rotate(key_grad[:, NOPE:], cos_table, -sin_table),
-        ],
-        axis=1,
-    ).astype(bf16)
-    normed_grad = dot("tq,qd->td", project_grad, project_weight, bf16)
-    project_part = dot("tq,td->qd", project_grad, normed, bf16)
-    latent_part = jnp.concatenate([project_part[:RANK], project_part[RANK + 192 :]], axis=0)
-    first_part = jnp.sum(
-        normed_grad.astype(f32) * (input_rows * scale_one[:, None]), axis=0, keepdims=True
-    )
-    extra = jnp.concatenate(
-        [
-            jnp.tile(latent_gain_part[None, :], (1, 4)).astype(bf16),
-            first_part.astype(bf16),
-            router_part[:EXPERTS],
-            jnp.zeros((6, D), bf16),
-        ],
-        axis=0,
-    )
-    narrow_part = jnp.concatenate(
-        [latent_part.reshape(4, -1, D), jnp.broadcast_to(extra[None], (4, 16, D))], axis=1
-    )
-    narrow_part, expert_sum = lax.optimization_barrier((narrow_part, expert_sum))
-    pairs = [
-        (dp * 4 + c, (2 * c + dp // 4) * 4 + (c ^ (dp % 4))) for dp in range(8) for c in range(4)
-    ]
-    expert_sum = lax.ppermute(expert_sum, ("dp", "col"), pairs)
+    normed_grad, narrow_part, query_part, ready = attend_back_step(
+        queries,
+        keys,
+        values,
+        log_total,
+        attended_grad,
+        early,
+        compact,
+        content,
+        latent_scale,
+        compact_gain[None, :],
+        expand_weight,
+        cosine,
+        sine,
+        project_all,
+        normed,
+        input_rows,
+        scale_one,
+        attended_rows,
+        residual_rows,
+        router_part,
+    )
     inputs_grad, sums, narrow, gains, latent_small = tail_step(
         normed_grad,
-        narrow_part.reshape(-1, D),
-        project_part[RANK : RANK + 192],
-        jnp.concatenate([output_weight_grad, expand_part], axis=0),
+        narrow_part,
+        query_part,
+        ready,
         residual_grad,
         inputs,
         my_scale_one,
         first_gain[None, :],
         second_gain_part,
     )
+    sums, narrow, shared_all, expert_sum = lax.optimization_barrier(
+        (sums, narrow, shared_all, expert_sum)
+    )
+    pairs = [
+        (dp * 4 + c, (2 * c + dp // 4) * 4 + (c ^ (dp % 4))) for dp in range(8) for c in range(4)
+    ]
+    expert_sum = lax.ppermute(expert_sum, ("dp", "col"), pairs)
     output_weight_grad = sums[:512].astype(f32)
     expand_grad = sums[512:768].T.astype(f32)
     query_weight_grad = sums[768:].T.astype(f32)
@@ -1247,7 +1373,7 @@
     expert_gate_grad = expert_sum[None, :ff].transpose(0, 2, 1)
     expert_up_grad = expert_sum[None, ff : 2 * ff].transpose(0, 2, 1)
     expert_down_grad = expert_sum[None, 2 * ff :]
-    shared_sum = shared_all.transpose(1, 0, 2, 3).reshape(4, -1, 512)[order].astype(f32)
+    shared_sum = shared_all.astype(f32)
     shared_gate_grad = shared_sum[:, :low].reshape(4 * low, 512).T
     shared_up_grad = shared_sum[:, low : 2 * low].reshape(4 * low, 512).T
     shared_down_grad = shared_sum[:, 2 * low : 3 * low].reshape(4 * low, 512)

time: 505 us -> 477 us (0.945)
  Pallas kernels: 359 us -> 406 us
  matrix products: 31.2 us -> 0 us
  local copies, waits for them, and re-layouts: 31.9 us -> 16 us
  other arithmetic: 24.6 us -> 12.8 us
  waiting for transfers between devices: 27.2 us -> 15.5 us
    dot_general x13 -> x0, matrix products: 31.2 us -> none  [dot(): jnp.einsum(spec, left, right, preferred_element_type=f32).astype(kind)]
    pallas_call x1, Pallas kernels: 71.9 us -> 89.3 us  [tail_step(): pl.pallas_call(tail_kernel, out_shape=(jax.ShapeDtypeStruct((rows, column...]
    pallas_call x4, Pallas kernels: 187 us -> 203 us  [the longest x1 88.9 us: front_step(): pl.pallas_call(front_kernel, out_shape=(array(rows, columns, kind=f32), a...]
    pallas_call x1, Pallas kernels: 75.5 us -> 87.9 us  [middle_step(): pl.pallas_call(middle_kernel, out_shape=(jax.ShapeDtypeStruct((rows, colu...]
    reduce_scatter x1, waiting for transfers between devices: 7.31 us -> 0.01 us  [on_device(): lax.psum_scatter(expert_grad, 'dp', scatter_dimension=0, tiled=True)[0]]
    unnamed x71 -> x40, local copies, waits for them, and re-layouts: 13.2 us -> 6.51 us
    gather x2 -> x0, local copies, waits for them, and re-layouts: 5.41 us -> none  [the longest x1 3.77 us: on_device(): shared_all.transpose(1, 0, 2, 3).reshape(4, -1, 512)[order].astype(f32)]
  transfers between devices with their start and end apart: 2 -> 2, of which waited for: 2 -> 1; matrix products, arithmetic and copies ran while one was open for 10% -> 4% of each run, Pallas kernels for 18% -> 43%
where the time goes in v5:
time: 477 us; the launch traced here: 468 us
  Pallas kernels  406 us (85%)
  local copies, waits for them, and re-layouts  16 us (3%)
  waiting for transfers between devices  15.5 us (3%)
  between operations  15.5 us (3%)
  other arithmetic  12.8 us (3%)
    pallas_call x1, Pallas kernels, tail_step(): pl.pallas_call(tail_kernel, out_shape=(jax.ShapeDtypeStruct((rows, column...  89.3 us
    pallas_call x1, Pallas kernels, front_step(): pl.pallas_call(front_kernel, out_shape=(array(rows, columns, kind=f32), a...  88.9 us
    pallas_call x1, Pallas kernels, middle_step(): pl.pallas_call(middle_kernel, out_shape=(jax.ShapeDtypeStruct((rows, colu...  87.9 us
    pallas_call x1, Pallas kernels, grads_step(): pl.pallas_call(functools.partial(grads_kernel, ff=ff, low=low), grid=(16,...  46.1 us
    pallas_call x1, Pallas kernels, start_step(): pl.pallas_call(start_kernel, out_shape=(jax.ShapeDtypeStruct((4 * rows, 4...  45 us
    pallas_call x1, Pallas kernels, expert_step(): pl.pallas_call(expert_kernel, grid=(tokens // tile,), out_shape=(jax.Shap...  25.3 us
    pallas_call x1, Pallas kernels, attend_back_step(): pl.pallas_call(attend_back_kernel, out_shape=(jax.ShapeDtypeStruct((token...  23.4 us
    ppermute x1, waiting for transfers between devices, on_device(): expert_sum = lax.ppermute(expert_sum, ('dp', 'col'), pairs)  15.5 us
  transfers between devices with their start and end apart: 2, of which 1 were waited for; matrix products, arithmetic and copies ran while one was open for 4% of the time, Pallas kernels for 43%

profile of v5, /device:TPU:5, one launch (start us, length us, event | category | flops | bytes accessed | tf_op | source)
XLA Modules:
  0.0 467.8 jit_solution(12159987898369155204)
XLA Ops:
  7.9 1.0 copy.46.sine
  9.3 1.0 copy.45.cosine
  11.0 0.6 fusion.7.mine
  11.8 45.0 %start_step.1 = (bf16[1024,2048]{1,0:T(8,128)(2,1)}, bf16[784,2048]{1,0:T(8,128)(2,1)}, bf16[704,2048]{1,0:T(8,128)(2,1)}) custom-call(bf16[256,512]{1,0:T(8,128)(2,1)S(1)} %copy-done, bf16[592,512]{1,0:T(8,128)(2,1)S(1)} %pad_maximum_fusion.common, bf16[768,512]{1,0:T(8,128)(2,1)S(1)} %bitcast.48, bf16[8,352,512]{2,1,0:T(8,128)(2,1)} %bitcast.51), custom_call_target="tpu_custom_call" | custom-call | bytes 157286400 | tf_op jit(solution)/shard_map/start_step/pallas_call | solution.py:229
  56.8 1.4 slice_convert_fusion.1.gain
  58.2 0.6 convert_element_type.72.named
  58.9 0.8 pad_maximum_fusion.1.weight
  59.8 88.9 %front_step.1 = (f32[256,512]{1,0:T(8,128)S(1)}, bf16[1024,2048]{1,0:T(8,128)(2,1)}, bf16[1024,512]{1,0:T(8,128)(2,1)}, bf16[1024,2048]{1,0:T(8,128)(2,1)}, bf16...) custom-call(bf16[1024,2048]{1,0:T(8,128)(2,1)} %get-tuple-element.63, ...), custom_call_target="tpu_custom_call" | custom-call | flops 8589934592 | bytes 157286400 | tf_op jit(solution)/shard_map/front_step/pallas_call | solution.py:1058
  148.7 25.3 %expert_step.1 = (bf16[1024,2048]{1,0:T(8,128)(2,1)}, f32[1024,128]{1,0:T(8,128)}, bf16[880,1024]{1,0:T(8,128)(2,1)}, bf16[1776,1024]{1,0:T(8,128)(2,1)}, bf16[1024,2048]{1,0:T(8,128)(2,1)}) custom-call(bf16[1024,2048]{1,0:T(8,128)(2,1)} %get-tuple-element.66.middle, bf16[1024,2048]{1,0:T(8,128)(2,1)} %get-tuple-element.67.out_grad, ...), custom_call_target="tpu_custom_call" | custom-call | flops 14763950080 | bytes 31457280 | tf_op jit(solution)/shard_map/expert_step/pallas_call | solution.py:427
  174.1 46.1 %grads_step.1 = (bf16[8,1056,512]{2,1,0:T(8,128)(2,1)}, bf16[4,144,512]{2,1,0:T(8,128)(2,1)S(1)}, bf16[16,2048]{1,0:T(8,128)(2,1)S(1)}, f32[256,512]{1,0:T(8,128)S(1)}, bf16[1024,2048]{1,0:T(8,128)(2,1)}) custom-call(bf16[1024,2048]{1,0:T(8,128)(2,1)} %get-tuple-element.72.hidden, bf16[1024,2048]{1,0:T(8,128)(2,1)} %get-tuple-element.67.out_grad, ...), custom_call_target="tpu_custom_call" | custom-call | flops 11811160064 | bytes 62914560 | tf_op jit(solution)/shard_map/grads_step/pallas_call | solution.py:563
  220.2 0.8 copy-done.1
  221.0 0.6 copy-done.8
  221.6 0.9 constant_dynamic-slice_fusion.1.scale
  222.6 87.9 %middle_step.1 = (f32[256,512]{1,0:T(8,128)S(1)}, bf16[1024,512]{1,0:T(8,128)(2,1)}, bf16[1024,128]{1,0:T(8,128)(2,1)S(1)}, f32[1,512]{1,0:T(1,128)S(1)}, bf16[4,576,512]{2,1,0:T(8,128)(2,1)}) custom-call(bf16[1024,2048]{1,0:T(8,128)(2,1)} %get-tuple-element.81.part, f32[256,512]{1,0:T(8,128)S(1)} %get-tuple-element.65.middle, ...), custom_call_target="tpu_custom_call" | custom-call | flops 536870912 | bytes 209715200 | tf_op jit(solution)/shard_map/middle_step/pallas_call | solution.py:711
  310.5 1.0 constant_dynamic-slice_fusion.scale
  311.5 23.4 %attend_back_step.1 = (bf16[1024,2048]{1,0:T(8,128)(2,1)}, bf16[640,2048]{1,0:T(8,128)(2,1)}, bf16[192,2048]{1,0:T(8,128)(2,1)}, bf16[768,512]{1,0:T(8,128)(2,1)}) custom-call(bf16[1024,256]{1,0:T(8,128)(2,1)} %get-tuple-element.77.queries, bf16[1024,256]{1,0:T(8,128)(2,1)} %get-tuple-element.78.keys, bf16[1024,128]{1,0:T(8,128)(2,1)} %copy-done.7, ...), custom_call_target="tpu_custom_call" | custom-call | flops 17179869184 | bytes 41943040 | tf_op jit(solution)/shard_map/attend_back_step/pallas_call | solution.py:1181
  335.0 89.3 %tail_step.1 = (bf16[256,512]{1,0:T(8,128)(2,1)S(1)}, bf16[1536,512]{1,0:T(8,128)(2,1)}, bf16[4,144,512]{2,1,0:T(8,128)(2,1)S(1)}, f32[16,512]{1,0:T(8,128)S(1)}, bf16[4,16,512]{2,1,0:T(8,128)(2,1)S(1)}) custom-call(bf16[1024,2048]{1,0:T(8,128)(2,1)} %get-tuple-element.93.part, bf16[640,2048]{1,0:T(8,128)(2,1)} %get-tuple-element.94.narrow_part, ...), custom_call_target="tpu_custom_call" | custom-call | flops 1048576 | bytes 209715200 | tf_op jit(solution)/shard_map/tail_step/pallas_call | solution.py:874
  424.3 0.6 slice.65
  425.5 0.6 slice_convert_fusion.2
  426.1 0.6 slice_bitcast_fusion.3
  426.7 0.8 add_convert_fusion
  427.4 1.9 collective-permute-start
  429.4 2.5 convert_bitcast_fusion
  431.9 3.0 copy.49
  434.9 1.0 convert_bitcast_fusion.2
  435.9 1.0 copy.50
  436.9 2.3 slice_convert_fusion
  439.2 1.2 convert_bitcast_fusion.1
  440.4 2.2 fusion.8
  442.7 15.5 %collective-permute-done = bf16[1056,512]{1,0:T(8,128)(2,1)S(1)} collective-permute-done((bf16[1056,512]{1,0:T(8,128)(2,1)}, bf16[1056,512]{1,0:T(8,128)(2,1)S(1)}, u32[]{:S(2)}, u32[]{:S(2)}) %collective-permute-start) | collective-permute-done | bytes 1081376 | tf_op jit(solution)/shard_map/ppermute | solution.py:1361
  458.5 1.4 slice_bitcast_fusion
  459.9 0.7 copy.53
  (58 shorter events, 2.1 us)
Async XLA Ops:
  7.2 1.8 copy-start.10
  7.2 420.3 %reduce-scatter.2.cloned.1.call-start = ((), (), s32[]{:S(2)}) async-start(), calls=%async_computation.1 | async-start | bytes 9732096 | tf_op jit(solution)/shard_map/reduce_scatter | solution.py:1309
  7.3 2.0 copy-start.15
  7.3 2.0 copy-start.16
  7.9 3.1 copy-start.17
  7.9 3.7 copy-start.11
  8.9 2.8 copy-start
  11.0 48.8 %copy-start.3 = (f32[1,1024]{1,0:T(1,128)}, f32[1,1024]{1,0:T(1,128)S(1)}, u32[]{:S(2)}) copy-start(f32[1,1024]{1,0:T(1,128)S(1)} %compare_convert_fusion.early) | copy-start | bytes 12292
  11.0 48.7 %copy-start.4 = (f32[512]{0:T(512)}, f32[512]{0:T(512)S(1)}, u32[]{:S(2)}) copy-start(f32[512]{0:T(512)S(1)} %broadcast_in_dim.36) | copy-start | bytes 6148
  11.7 46.5 %copy-start.13 = (s32[1024,6]{0,1:T(8,128)S(1)}, s32[1024,6]{0,1:T(8,128)}, u32[]{:S(2)}) copy-start(s32[1024,6]{0,1:T(8,128)} %param.33) | copy-start | bytes 73732
  11.7 47.1 %copy-start.14 = (bf16[512,8]{0,1:T(8,128)(2,1)S(1)}, bf16[512,8]{0,1:T(8,128)(2,1)}, u32[]{:S(2)}) copy-start(bf16[512,8]{0,1:T(8,128)(2,1)} %param.26) | copy-start | bytes 24580
  11.8 47.1 %copy-start.12 = (bf16[512,512]{1,0:T(8,128)(2,1)S(1)}, bf16[512,512]{1,0:T(8,128)(2,1)}, u32[]{:S(2)}) copy-start(bf16[512,512]{1,0:T(8,128)(2,1)} %param.24) | copy-start | bytes 1572868
  56.8 3.0 copy-start.2
  56.8 3.0 copy-start.5
  148.7 25.4 %copy-start.7 = (bf16[1024,128]{1,0:T(8,128)(2,1)}, bf16[1024,128]{1,0:T(8,128)(2,1)S(1)}, u32[]{:S(2)}) copy-start(bf16[1024,128]{1,0:T(8,128)(2,1)S(1)} %get-tuple-element.79.values) | copy-start | bytes 786436
  220.2 0.8 copy-start.1
  221.0 0.6 copy-start.8
  310.5 1.0 copy-start.6
  427.4 30.7 %collective-permute-start = (bf16[1056,512]{1,0:T(8,128)(2,1)}, bf16[1056,512]{1,0:T(8,128)(2,1)S(1)}, u32[]{:S(2)}, u32[]{:S(2)}) collective-permute-start(bf16[1056,512]{1,0:T(8,128)(2,1)} %bitcast.65), channel_id=1, source_target_pairs={{0,0},{1,33},{2,66},{3,99},{16,1},{17,32},{18,67},{19,98},{32,2},{... | collective-permute-start | bytes 3244040 | tf_op jit(solution)/shard_map/ppermute | solution.py:1361
  436.9 3.5 copy-start.9
Sparse Core Ops, SparseCore 0:
  221.2 169.1 reduce-scatter.1
